TPU v7x, 32 devices: a whole 2x2x4 slice. The times are simulated.
32 devices in a mesh: rows: 8 (over z, y), cols: 4 (over x, core).
Axes of the slice: x: 2, y: 2, z: 4, core: 2. Of those that a mesh axis runs over, the one named last changes fastest.
Arguments:
- features: bfloat16 [8192, 256], P(('rows', 'cols')), may hold values from -6 to 6
- weight: bfloat16 [256, 256], replicated, may hold values from -0.375 to 0.375
- bias: float32 [256], replicated, may hold values from -3 to 3
- tile_values: bfloat16 [8, 4, 8, 3, 128, 128], P('rows', 'cols'), may hold values from -0.21875 to 0.21875
- tile_source: int32 [8, 4, 8, 3], P('rows', 'cols'), may hold values from 0 to 7
- tile_dest: int32 [8, 4, 8, 3], P('rows', 'cols'), may hold values from 0 to 1
- send_counts: int32 [8, 4, 8], P('rows', 'cols'), may hold values from 0 to 3, as said below
- cotangent: bfloat16 [8192, 256], P(('rows', 'cols')), may hold values from -6 to 6
Outputs:
- output: bfloat16 [8192, 256], P(('rows', 'cols'))
- input_grad: bfloat16 [8192, 256], P(('rows', 'cols'))
- weight_grad: float32 [256, 256], replicated
- bias_grad: float32 [256], replicated
Inputs may be any that keep to these rules, and one draw needn't show every extreme that they name: `send_counts`: in each column group one owner, drawn from the seed, receives 3 live slots from every sender.
All inputs are finite; a program needn't handle non-finite values.
Results may differ from a plain program's by a relative error of at most 0.014.
Values may be sent and summed in bfloat16 or wider, within the bound.
No kernel may reach another device: no remote copies, remote signals or barrier semaphores. Data moves between devices by JAX's collectives and lax.ppermute only.
A program may use at most 128 MiB of HBM per device.

v0:
```python
import math

import jax
import jax.numpy as jnp
from jax import lax
from jax.sharding import PartitionSpec as P


def local(features, weight, bias, tile_values, tile_source, tile_dest, send_counts, cotangent):
    tile_size = tile_values.shape[-1]
    width = weight.shape[1]
    owners = tile_values.shape[2]
    slot_cap = tile_values.shape[3]
    own_tiles = features.shape[0] // tile_size
    tile_vals = tile_values[0, 0]
    source_ids = tile_source[0, 0]
    target_ids = tile_dest[0, 0]
    counts_here = send_counts[0, 0]
    slot_iota = lax.broadcasted_iota(jnp.int32, (owners, slot_cap), 1)
    live_slots = slot_iota < counts_here[:, None]
    dest_iota = jnp.arange(own_tiles, dtype=jnp.int32)
    local_hidden = jnp.dot(features, weight, preferred_element_type=jnp.float32).astype(
        jnp.bfloat16
    )
    block_hidden = lax.all_gather(local_hidden, "cols", axis=0, tiled=True)
    span_tiles = block_hidden.shape[0] // tile_size
    span_iota = jnp.arange(span_tiles, dtype=jnp.int32)
    block_tiles = block_hidden.reshape(span_tiles, tile_size, width)
    pick_source = (source_ids[:, :, None] == span_iota[None, None, :]).astype(jnp.bfloat16)
    chosen = jnp.einsum(
        "osj,jaf->osaf", pick_source, block_tiles, preferred_element_type=jnp.float32
    ).astype(jnp.bfloat16)
    partial_tiles = jnp.einsum(
        "osab,osaf->osbf", tile_vals, chosen, preferred_element_type=jnp.float32
    )
    routing = (
        (target_ids[:, :, None] == dest_iota[None, None, :]) & live_slots[:, :, None]
    ).astype(jnp.float32)
    contrib = jnp.einsum("ost,osbf->otbf", routing, partial_tiles).astype(jnp.bfloat16)
    received = lax.all_to_all(contrib, "rows", split_axis=0, concat_axis=0, tiled=True)
    summed = jnp.sum(received, axis=0, dtype=jnp.float32)
    pre = summed.reshape(own_tiles * tile_size, width) + bias[None, :]
    output = jax.nn.gelu(pre).astype(jnp.bfloat16)
    _, backward_fn = jax.vjp(jax.nn.gelu, pre)
    grad_pre = backward_fn(cotangent.astype(jnp.float32))[0].astype(jnp.bfloat16)
    piece = lax.all_gather(grad_pre, "rows", axis=0, tiled=True)
    owner_count = piece.shape[0] // (own_tiles * tile_size)
    piece_tiles = piece.reshape(owner_count, own_tiles, tile_size, width)
    pick_target = (target_ids[:, :, None] == dest_iota[None, None, :]).astype(jnp.bfloat16)
    grad_sel = jnp.einsum(
        "ost,otbf->osbf", pick_target, piece_tiles, preferred_element_type=jnp.float32
    ).astype(jnp.bfloat16)
    term = jnp.einsum("osab,osbf->osaf", tile_vals, grad_sel, preferred_element_type=jnp.float32)
    spread = ((source_ids[:, :, None] == span_iota[None, None, :]) & live_slots[:, :, None]).astype(
        jnp.float32
    )
    block_grad = jnp.einsum("osj,osaf->jaf", spread, term)
    grad_hidden = lax.psum_scatter(
        block_grad.reshape(span_tiles * tile_size, width), "cols", scatter_dimension=0, tiled=True
    )
    grad_rounded = grad_hidden.astype(jnp.bfloat16)
    input_grad = jnp.einsum(
        "nf,gf->ng", grad_rounded, weight, preferred_element_type=jnp.float32
    ).astype(jnp.bfloat16)
    weight_local = jnp.einsum(
        "nf,ng->fg", features, grad_rounded, preferred_element_type=jnp.float32
    )
    bias_local = jnp.sum(grad_pre, axis=0, dtype=jnp.float32)
    weight_total, bias_total = lax.psum((weight_local, bias_local), ("rows", "cols"))
    node_total = features.shape[0] * lax.axis_size("rows") * lax.axis_size("cols")
    scale_factor = 1.0 / math.sqrt(node_total)
    return (output, input_grad, weight_total * scale_factor, bias_total * scale_factor)


def solution(mesh):
    in_specs = (
        P(("rows", "cols"), None),
        P(),
        P(),
        P("rows", "cols", None, None, None, None),
        P("rows", "cols", None, None),
        P("rows", "cols", None, None),
        P("rows", "cols", None),
        P(("rows", "cols"), None),
    )
    out_specs = (P(("rows", "cols"), None), P(("rows", "cols"), None), P(), P())
    return jax.shard_map(local, mesh=mesh, in_specs=in_specs, out_specs=out_specs, check_vma=False)
```

profile of v0, /device:TPU:0, one launch (start us, length us, event | category | flops | bytes accessed | tf_op | source)
XLA Modules:
  0.0 282.6 jit_solution(18335156939184593300)
XLA Ops:
  7.2 0.0 copy-start
  7.2 0.0 all-gather.2.cloned.1.call-start
  7.2 0.7 iota_compare_fusion.4
  8.0 0.1 copy.30
  8.1 0.7 copy.60
  8.7 0.8 copy.45
  9.5 1.2 convolution_convert_fusion.4
  10.6 8.6 %all_gather.6 = bf16[1024,256]{1,0:T(8,128)(2,1)S(1)} all-gather(bf16[256,256]{1,0:T(8,128)(2,1)S(1)} %convolution_convert_fusion.4), channel_id=1, replica_groups=mesh['rows'=8,'cols'=4] {'cols'}, dimensions={0}, use_global_device_ids=true | all-gather | bytes 655360 | tf_op jit(solution)/shard_map/all_gather | solution.py:25
  19.3 0.6 convolution_convert_fusion.1
  19.9 0.0 copy-done
  19.9 0.7 convolution_bitcast_fusion.1
  20.6 2.5 copy.34
  23.1 2.8 convolution_convert_fusion.2
  26.0 0.0 copy-start.3
  26.0 0.0 copy-start.4
  26.0 32.0 %all_to_all.5 = bf16[8,2,128,256]{3,1,2,0:T(2,128)(2,1)S(1)} all-to-all(bf16[8,2,128,256]{3,1,2,0:T(2,128)(2,1)S(1)} %convolution_convert_fusion.2), channel_id=1, replica_groups=mesh['rows'=8,'cols'=4] {'rows'}, dimensions={0} | all-to-all | bytes 2097152 | tf_op jit(solution)/shard_map/all_to_all | solution.py:40
  58.0 0.9 convert_reduce_fusion
  59.0 0.0 copy-done.3
  59.0 0.0 copy-done.4
  59.0 0.9 convert_reduce_fusion.1
  59.9 0.0 all-gather.2.cloned.1.call-update
  59.9 0.0 reduce-scatter.2.cloned.1.call-start
  60.0 38.9 %all-gather.2.cloned.1.call-done = bf16[2048,256]{1,0:T(8,128)(2,1)} async-done(((bf16[256,256]{1,0:T(8,128)(2,1)}), bf16[2048,256]{1,0:T(8,128)(2,1)}) %all-gather.2.cloned.1.call-update) | async-done | bytes 1048592 | tf_op jit(solution)/shard_map/all_gather | solution.py:46
  98.9 3.2 %convolution_convert_fusion = bf16[8,3,128,256]{3,1,2,0:T(4,128)(2,1)S(1)} fusion(bf16[8,2,128,256]{3,2,1,0:T(8,128)(2,1)} %bitcast.68, s32[8,3]{1,0:T(8,128)S(1)} %bitcast.67), kind=kOutput, calls=%fused_computation.3 | convolution fusion | flops 3932208 | bytes 2621536 | tf_op jit(solution)/shard_map/ost,otbf->osbf/dot_general | solution.py:50
  102.1 1.8 convolution_bitcast_fusion
  103.8 2.1 copy.38
  106.0 0.4 convolution_bitcast_fusion.2
  106.4 0.0 copy-start.1
  106.4 0.0 copy-start.2
  106.4 1.3 copy.39
  107.7 0.0 reduce-scatter.2.cloned.1.call-update
  107.8 0.0 all-reduce.2.cloned.1.call-start
  107.8 38.3 %psum.15 = f32[256]{0:T(256)S(1)} all-reduce(f32[256]{0:T(256)S(1)} %get-tuple-element.20), channel_id=1, replica_groups=mesh['rows'=8,'cols'=4] {'rows','cols'}, use_global_device_ids=true, to_apply=%region_4.0 | all-reduce | flops 256 | bytes 2048 | tf_op jit(solution)/shard_map/psum | solution.py:69
  146.1 0.6 broadcast_multiply_fusion.1
  146.7 0.0 reduce-scatter.2.cloned.1.call-done
  146.7 0.0 copy-done.1
  146.7 1.9 convolution_bitcast_fusion.3
  148.5 0.0 all-reduce.2.cloned.1.call-update
  148.6 0.0 copy-done.2
  148.6 1.8 convolution_convert_fusion.3
  150.4 123.8 %all-reduce.2.cloned.1.call-done = f32[256,256]{0,1:T(8,128)} async-done(((f32[256,256]{0,1:T(8,128)}), f32[256,256]{0,1:T(8,128)}) %all-reduce.2.cloned.1.call-update) | async-done | bytes 262160 | tf_op jit(solution)/shard_map/psum | solution.py:69
  274.2 1.0 broadcast_multiply_fusion
  275.2 0.8 copy.40
  (1 shorter events, 0.0 us)
Async XLA Ops:
  7.2 12.7 %copy-start = (bf16[1,1,8,3,128,128]{5,4,3,2,1,0:T(8,128)(2,1)S(1)}, bf16[1,1,8,3,128,128]{5,4,3,2,1,0:T(8,128)(2,1)}, u32[]{:S(2)}) copy-start(bf16[1,1,8,3,128,128]{5,4,3,2,1,0:T(8,128)(2,1)} %param.11) | copy-start | bytes 2359300
  7.2 91.7 %all-gather.2.cloned.1.call-start = ((), (), s32[]{:S(2)}) async-start(), calls=%async_computation.2 | async-start | bytes 1179648 | tf_op jit(solution)/shard_map/all_gather | solution.py:46
  26.0 33.0 %copy-start.3 = (bf16[256,256]{1,0:T(8,128)(2,1)S(1)}, bf16[256,256]{1,0:T(8,128)(2,1)}, u32[]{:S(2)}) copy-start(bf16[256,256]{1,0:T(8,128)(2,1)} %param.15) | copy-start | bytes 393220
  26.0 33.0 %copy-start.4 = (f32[256]{0:T(256)S(1)}, f32[256]{0:T(256)}, u32[]{:S(2)}) copy-start(f32[256]{0:T(256)} %param.10) | copy-start | bytes 3076
  59.9 86.7 %reduce-scatter.2.cloned.1.call-start = ((), (), s32[]{:S(2)}) async-start(), calls=%async_computation.3 | async-start | bytes 1310720 | tf_op jit(solution)/shard_map/reduce_scatter | solution.py:58
  106.4 40.2 %copy-start.1 = (bf16[256,256]{1,0:T(8,128)(2,1)S(1)}, bf16[256,256]{1,0:T(8,128)(2,1)}, u32[]{:S(2)}) copy-start(bf16[256,256]{1,0:T(8,128)(2,1)} %param.8) | copy-start | bytes 393220
  106.4 42.1 %copy-start.2 = (bf16[256,256]{1,0:T(8,128)(2,1)S(1)}, bf16[256,256]{1,0:T(8,128)(2,1)}, u32[]{:S(2)}) copy-start(bf16[256,256]{1,0:T(8,128)(2,1)} %param.9) | copy-start | bytes 393220
  107.8 166.4 %all-reduce.2.cloned.1.call-start = ((), (), s32[]{:S(2)}) async-start(), calls=%async_computation.4 | async-start | bytes 524288 | tf_op jit(solution)/shard_map/psum | solution.py:69
Sparse Core Ops, SparseCore 0:
  60.0 38.7 all-gather.1
  107.9 23.6 reduce-scatter.1
  148.7 125.4 all-reduce.1
where the time goes:
time: 283 us
  waiting for transfers between devices  163 us (58%)
  blocking collectives  78.9 us (28%)
  matrix products  14.3 us (5%)
  between operations  13.9 us (5%)
  local copies, waits for them, and re-layouts  8.43 us (3%)
  other arithmetic  4.12 us (1%)
    psum x1, waiting for transfers between devices, local(): lax.psum((weight_local, bias_local), ('rows', 'cols'))  124 us
    all_gather x1, waiting for transfers between devices, local(): piece = lax.all_gather(grad_pre, 'rows', axis=0, tiled=True)  38.9 us
    psum x1, blocking collectives, local(): lax.psum((weight_local, bias_local), ('rows', 'cols'))  38.3 us
    all_to_all x1, blocking collectives, local(): lax.all_to_all(contrib, 'rows', split_axis=0, concat_axis=0, tiled=True)  32 us
    all_gather x1, blocking collectives, local(): block_hidden = lax.all_gather(local_hidden, 'cols', axis=0, tiled=True)  8.62 us
  transfers between devices with their start and end apart: 3, of which 2 were waited for; matrix products, arithmetic and copies ran while one was open for 1% of the time, Pallas kernels for 0%

commit v1 on v0

v1 whole, which is shorter than its diff:
```python
import functools
import math

import jax
import jax.numpy as jnp
from jax import lax
from jax.experimental import pallas as pl
from jax.experimental.pallas import tpu as pltpu
from jax.sharding import PartitionSpec as P

F32 = jnp.float32
BF16 = jnp.bfloat16
PAD = 16


def call(body, out_shape, scratch=(), n_smem=0, n_vmem=0, flops=0):
    specs = [pl.BlockSpec(memory_space=pltpu.SMEM)] * n_smem
    specs += [pl.BlockSpec(memory_space=pltpu.VMEM)] * n_vmem
    many = isinstance(out_shape, (list, tuple))
    vmem = pl.BlockSpec(memory_space=pltpu.VMEM)
    return pl.pallas_call(
        body,
        out_shape=out_shape,
        in_specs=specs,
        out_specs=[vmem] * len(out_shape) if many else vmem,
        scratch_shapes=list(scratch),
        cost_estimate=pl.CostEstimate(flops=flops, bytes_accessed=2_000_000, transcendentals=0),
        compiler_params=pltpu.CompilerParams(vmem_limit_bytes=48 * 1024 * 1024),
    )


def tree_sum(items):
    items = [x.astype(F32) for x in items]
    while len(items) > 1:
        items = [items[i] + items[i + 1] for i in range(0, len(items), 2)]
    return items[0]


def send(x, axis, offset):
    size = lax.axis_size(axis)
    return lax.ppermute(x, axis, [(i, i ^ offset) for i in range(size)])


def push_kernel(rows, slots, tiles, span, code_ref, place_ref, *refs):
    feat_refs, vals_ref, out_ref, turned = refs[:-3], refs[-3], refs[-2], refs[-1]
    size = vals_ref.shape[-1]
    row, col = place_ref[0], place_ref[1]
    for k, ref in enumerate(feat_refs):
        for t in range(tiles):
            turned[(col ^ k) * tiles + t] = ref[t * size : (t + 1) * size, :].T
    for k in range(rows):
        owner = row ^ k
        total = None
        for s in range(slots):
            word = code_ref[owner * slots + s]
            vals = vals_ref[owner, s]
            zero = jnp.zeros_like(vals)
            picked = jnp.concatenate(
                [jnp.where(word % 256 == t, vals, zero) for t in range(tiles)], axis=1
            )
            part = jnp.dot(turned[word // 256], picked, preferred_element_type=F32)
            total = part if total is None else total + part
        out_ref[k] = total.astype(BF16)


def middle_kernel(cols, n_parts, place_ref, *refs):
    parts = refs[:n_parts]
    weight_ref, bias_ref, cot_ref, out_ref, grad_ref, terms_ref, wg = refs[n_parts:]
    agg_t = tree_sum([p[...] for p in parts])
    high = agg_t.astype(BF16)
    low = (agg_t - high.astype(F32)).astype(BF16)
    dims = (((0,), (0,)), ((), ()))
    weight = weight_ref[...]
    pre = lax.dot_general(high, weight, dims, preferred_element_type=F32)
    pre += lax.dot_general(low, weight, dims, preferred_element_type=F32)
    pre += bias_ref[...]
    c = math.sqrt(2.0 / math.pi)
    square = pre * pre
    t = jnp.tanh(c * pre * (1.0 + 0.044715 * square))
    half = 0.5 * (1.0 + t)
    out_ref[...] = (pre * half).astype(BF16)
    slope = half + 0.5 * pre * (1.0 - t * t) * (c * (1.0 + 3 * 0.044715 * square))
    grad = (cot_ref[...].astype(F32) * slope).astype(BF16)
    grad_ref[...] = lax.dot_general(
        grad, weight, (((1,), (1,)), ((), ())), preferred_element_type=F32
    ).astype(BF16)
    wg[...] = jnp.dot(high, grad, preferred_element_type=F32)
    wg[...] += jnp.dot(low, grad, preferred_element_type=F32)
    bias_row = jnp.sum(grad.astype(F32), axis=0, keepdims=True).astype(BF16)
    bias_rows = jnp.broadcast_to(bias_row, (PAD, bias_row.shape[1]))
    depth = wg.shape[0] // cols
    for k in range(cols):
        start = pl.multiple_of((place_ref[1] ^ k) * depth, depth)
        terms_ref[k, :depth, :] = wg[pl.ds(start, depth), :].astype(BF16)
        terms_ref[k, depth:, :] = bias_rows


def pull_kernel(rows, cols, slots, tiles, code_ref, place_ref, *refs):
    grad_refs, vals_ref, out_ref, total = refs[:rows], refs[rows], refs[rows + 1], refs[rows + 2]
    size = vals_ref.shape[-1]
    row, col = place_ref[0], place_ref[1]
    total[...] = jnp.zeros_like(total)
    for k in range(rows):
        owner = row ^ k
        for s in range(slots):
            word = code_ref[owner * slots + s]
            dest = word % 256
            live = dest < tiles
            start = pl.multiple_of(jnp.where(live, dest, 0) * size, size)
            block = grad_refs[k][pl.ds(start, size), :]
            term = jnp.dot(vals_ref[owner, s], block, preferred_element_type=F32)
            source = word // 256
            total[source] += jnp.where(live, term, 0.0)
    for k in range(cols):
        for t in range(tiles):
            out_ref[k, t * size : (t + 1) * size, :] = total[(col ^ k) * tiles + t].astype(BF16)


def last_kernel(cols, scale, place_ref, *refs):
    blocks, pieces = refs[:cols], refs[cols : 2 * cols]
    bias_ref, in_ref, wg_ref, bg_ref = refs[2 * cols :]
    in_ref[...] = tree_sum([b[...] for b in blocks]).astype(BF16)
    depth = wg_ref.shape[0] // cols
    for k in range(cols):
        start = pl.multiple_of((place_ref[1] ^ k) * depth, depth)
        wg_ref[pl.ds(start, depth), :] = pieces[k][...].astype(F32) * scale
    bg_ref[...] = bias_ref[...] * scale


def local(features, weight, bias, tile_values, tile_source, tile_dest, send_counts, cotangent):
    rows, cols = lax.axis_size("rows"), lax.axis_size("cols")
    size = tile_values.shape[-1]
    slots = tile_values.shape[3]
    nodes, width_in = features.shape
    width = weight.shape[1]
    tiles = nodes // size
    span = tiles * cols
    vals = tile_values[0, 0]
    place = jnp.stack([lax.axis_index("rows"), lax.axis_index("cols")]).astype(jnp.int32)

    live = lax.broadcasted_iota(jnp.int32, (rows, slots), 1) < send_counts[0, 0][:, None]
    code = (tile_source[0, 0] * 256 + jnp.where(live, tile_dest[0, 0], 255)).reshape(-1)

    far = [send(features, "cols", k) for k in range(cols - 1, 0, -1)][::-1]
    flops = 2 * rows * slots * size * size * width
    contrib = call(
        functools.partial(push_kernel, rows, slots, tiles, span),
        jax.ShapeDtypeStruct((rows, width_in, nodes), BF16),
        [pltpu.VMEM((span, width_in, size), BF16)],
        2,
        cols + 1,
        flops,
    )(code, place, features, *far, vals)

    pair = {k: send(contrib[k + 1], "rows", 1) for k in range(rows - 2, -1, -2)}
    parts = [contrib[0], pair[0]]
    direct = {}
    for k in range(rows - 2, 0, -2):
        both = (contrib[k].astype(F32) + pair[k].astype(F32)).astype(BF16)
        direct[k] = send(both, "rows", k)
    own = (contrib[0].astype(F32) + pair[0].astype(F32)).astype(F32)
    parts = [own] + [direct[k] for k in range(2, rows, 2)]

    depth = width_in // cols
    output, grad, terms = call(
        functools.partial(middle_kernel, cols, len(parts)),
        [
            jax.ShapeDtypeStruct((nodes, width), BF16),
            jax.ShapeDtypeStruct((nodes, width_in), BF16),
            jax.ShapeDtypeStruct((cols, depth + PAD, width), BF16),
        ],
        [pltpu.VMEM((width_in, width), F32)],
        1,
        len(parts) + 3,
        10 * width * width * nodes,
    )(place, *parts, weight, bias[None, :], cotangent)

    got = {0: grad}
    for k in range(2, rows, 2):
        got[k] = send(grad, "rows", k)
    got[1] = send(grad, "rows", 1)
    for k in range(2, rows, 2):
        got[k + 1] = send(got[k], "rows", 1)

    part = tree_sum([terms[0]] + [send(terms[k], "cols", k) for k in range(1, cols)]).astype(BF16)
    part = tree_sum([part] + [send(part, "rows", k) for k in range(2, rows, 2)]).astype(BF16)
    part = part.astype(F32) + send(part, "rows", 1).astype(F32)
    piece = part[:depth].astype(BF16)

    blocks = call(
        functools.partial(pull_kernel, rows, cols, slots, tiles),
        jax.ShapeDtypeStruct((cols, nodes, width_in), BF16),
        [pltpu.VMEM((span, size, width_in), F32)],
        2,
        rows + 1,
        flops,
    )(code, place, *[got[k] for k in range(rows)], vals)
    arrived = [blocks[0]] + [send(blocks[k], "cols", k) for k in range(1, cols)]
    pieces = [piece] + [send(piece, "cols", k) for k in range(1, cols)]
    scale = 1.0 / math.sqrt(nodes * rows * cols)
    input_grad, weight_grad, bias_grad = call(
        functools.partial(last_kernel, cols, scale),
        [
            jax.ShapeDtypeStruct((nodes, width_in), BF16),
            jax.ShapeDtypeStruct((width_in, width), F32),
            jax.ShapeDtypeStruct((1, width), F32),
        ],
        (),
        1,
        2 * cols + 1,
    )(place, *arrived, *pieces, part[depth : depth + 1])
    return output, input_grad, weight_grad, bias_grad[0]


def solution(mesh):
    in_specs = (
        P(("rows", "cols"), None),
        P(),
        P(),
        P("rows", "cols", None, None, None, None),
        P("rows", "cols", None, None),
        P("rows", "cols", None, None),
        P("rows", "cols", None),
        P(("rows", "cols"), None),
    )
    out_specs = (P(("rows", "cols"), None), P(("rows", "cols"), None), P(), P())
    return jax.shard_map(local, mesh=mesh, in_specs=in_specs, out_specs=out_specs, check_vma=False)
```

time: 283 us -> 91.4 us (0.32)
  waiting for transfers between devices: 163 us -> 46.6 us
  blocking collectives: 78.9 us -> 0 us
  starting transfers between devices: 0.12 us -> 33.2 us
  matrix products: 14.3 us -> 0 us
  between operations: 13.9 us -> 0.77 us
  Pallas kernels: 0 us -> 6.03 us
  local copies, waits for them, and re-layouts: 8.43 us -> 4.34 us
  other arithmetic: 4.12 us -> 0.36 us
    psum x1 -> x0, waiting for transfers between devices: 124 us -> none  [local(): lax.psum((weight_local, bias_local), ('rows', 'cols'))]
    ppermute x0 -> x30, waiting for transfers between devices: none -> 46.6 us  [send(): return lax.ppermute(x, axis, [(i, i ^ offset) for i in range(size)])]
    all_gather x1 -> x0, waiting for transfers between devices: 38.9 us -> none  [local(): piece = lax.all_gather(grad_pre, 'rows', axis=0, tiled=True)]
    psum x1 -> x0, blocking collectives: 38.3 us -> none  [local(): lax.psum((weight_local, bias_local), ('rows', 'cols'))]
    ppermute x0 -> x30, starting transfers between devices: none -> 33.2 us  [send(): return lax.ppermute(x, axis, [(i, i ^ offset) for i in range(size)])]
    all_to_all x1 -> x0, blocking collectives: 32 us -> none  [local(): lax.all_to_all(contrib, 'rows', split_axis=0, concat_axis=0, tiled=True)]
    dot_general x9 -> x0, matrix products: 14.3 us -> none  [the longest x1 3.15 us: local(): jnp.einsum('ost,otbf->osbf', pick_target, piece_tiles, preferred_element_...]
    all_gather x1 -> x0, blocking collectives: 8.62 us -> none  [local(): block_hidden = lax.all_gather(local_hidden, 'cols', axis=0, tiled=True)]
  transfers between devices with their start and end apart: 3 -> 30, of which waited for: 2 -> 17; matrix products, arithmetic and copies ran while one was open for 1% -> 1% of each run, Pallas kernels for 0% -> 1%
where the time goes in v1:
time: 91.4 us; the launch traced here: 91.2 us
  waiting for transfers between devices  46.6 us (51%)
  starting transfers between devices  33.2 us (36%)
  Pallas kernels  6.03 us (7%)
  local copies, waits for them, and re-layouts  4.34 us (5%)
    ppermute x30, waiting for transfers between devices, send(): return lax.ppermute(x, axis, [(i, i ^ offset) for i in range(size)])  46.6 us
    ppermute x30, starting transfers between devices, send(): return lax.ppermute(x, axis, [(i, i ^ offset) for i in range(size)])  33.2 us
    unnamed x19, local copies, waits for them, and re-layouts  3.91 us
  transfers between devices with their start and end apart: 30, of which 17 were waited for; matrix products, arithmetic and copies ran while one was open for 1% of the time, Pallas kernels for 1%

profile of v1, /device:TPU:0, one launch (start us, length us, event | category | flops | bytes accessed | tf_op | source)
XLA Modules:
  0.0 91.2 jit_solution(7595109416697056019)
XLA Ops:
  0.6 3.0 %collective-permute-start.1 = (bf16[256,256]{1,0:T(8,128)(2,1)}, bf16[256,256]{1,0:T(8,128)(2,1)S(1)}, u32[]{:S(2)}, u32[]{:S(2)}) collective-permute-start(bf16[256,256]{1,0:T(8,128)(2,1)} %refs_0_.1), channel_id=1, source_target_pairs={{0,2},{1,3},{2,0},{3,1},{4,6},{5,7},{6,4},{7,5},{8,10},{9,11},{10,... | collective-permute-start | bytes 393224 | tf_op jit(solution)/shard_map/ppermute | solution.py:41
  3.6 0.2 collective-permute-start.2
  3.9 0.1 iota_compare_fusion
  3.9 0.1 lt.17
  4.0 0.5 copy-done.6
  4.5 0.1 copy.14
  4.6 0.1 mul.8
  4.7 0.6 copy-done.7
  5.3 0.1 copy.15
  5.4 0.1 squeeze.48
  5.5 0.1 pad_add_fusion.place_ref
  5.6 2.3 %collective-permute-done.1.refs_2_ = bf16[256,256]{1,0:T(8,128)(2,1)S(1)} collective-permute-done((bf16[256,256]{1,0:T(8,128)(2,1)}, bf16[256,256]{1,0:T(8,128)(2,1)S(1)}, u32[]{:S(2)}, u32[]{:S(2)}) %collective-permute-start.1) | collective-permute-done | bytes 131104 | tf_op jit(solution)/shard_map/ppermute | solution.py:41
  7.9 0.0 collective-permute-done.refs_1_
  7.9 1.8 %collective-permute-done.2.refs_3_ = bf16[256,256]{1,0:T(8,128)(2,1)S(1)} collective-permute-done((bf16[256,256]{1,0:T(8,128)(2,1)}, bf16[256,256]{1,0:T(8,128)(2,1)S(1)}, u32[]{:S(2)}, u32[]{:S(2)}) %collective-permute-start.2) | collective-permute-done | bytes 131104 | tf_op jit(solution)/shard_map/ppermute | solution.py:41
  9.7 1.1 %copy-done = bf16[1,1,8,3,128,128]{5,4,3,2,1,0:T(8,128)(2,1)S(1)} copy-done((bf16[1,1,8,3,128,128]{5,4,3,2,1,0:T(8,128)(2,1)S(1)}, bf16[1,1,8,3,128,128]{5,4,3,2,1,0:T(8,128)(2,1)}, u32[]{:S(2)}) %copy-start) | copy-done | bytes 786456
  10.8 0.9 copy-done.2
  11.8 1.7 %shard_map.111 = bf16[8,256,256]{2,1,0:T(8,128)(2,1)S(1)} custom-call(s32[24]{0:T(128)S(1)} %select_add_fusion.code_ref, s32[2]{0:T(128)S(1)} %pad_add_fusion.place_ref, bf16[256,256]{1,0:T(8,128)(2,1)S(1)} %copy-done.2, bf16[256,256]{1,0:T(8,128)(2,1)S(1)} %collective-permute-done.refs_1_, bf16[256,256]{1,0:T(8,128)(2,1)S(1)} %collective-permute-done.1.refs_2_, ...), custom_call_target="tpu_custom_call" | custom-call | flops 201326592 | bytes 2000000 | tf_op jit(solution)/shard_map/pallas_call | solution.py:146
  13.5 1.5 %collective-permute-start.8 = (bf16[256,256]{1,0:T(8,128)(2,1)S(1)}, bf16[256,256]{1,0:T(8,128)(2,1)S(1)}, u32[]{:S(2)}, u32[]{:S(2)}) collective-permute-start(bf16[256,256]{1,0:T(8,128)(2,1)S(1)} %get-tuple-element.20), channel_id=1, source_target_pairs={{0,4},{4,0},{8,12},{12,8},{16,20},{20,16},{24,28},{28,24},{1,5},{5... | collective-permute-start | bytes 393224 | tf_op jit(solution)/shard_map/ppermute | solution.py:41
  15.0 0.6 collective-permute-start.6
  15.6 1.5 %collective-permute-start.4 = (bf16[256,256]{1,0:T(8,128)(2,1)S(1)}, bf16[256,256]{1,0:T(8,128)(2,1)S(1)}, u32[]{:S(2)}, u32[]{:S(2)}) collective-permute-start(bf16[256,256]{1,0:T(8,128)(2,1)S(1)} %get-tuple-element.22), channel_id=1, source_target_pairs={{0,4},{4,0},{8,12},{12,8},{16,20},{20,16},{24,28},{28,24},{1,5},{5... | collective-permute-start | bytes 393224 | tf_op jit(solution)/shard_map/ppermute | solution.py:41
  17.1 0.6 collective-permute-start.3
  17.6 2.3 %collective-permute-done.8 = bf16[256,256]{1,0:T(8,128)(2,1)S(1)} collective-permute-done((bf16[256,256]{1,0:T(8,128)(2,1)S(1)}, bf16[256,256]{1,0:T(8,128)(2,1)S(1)}, u32[]{:S(2)}, u32[]{:S(2)}) %collective-permute-start.8) | collective-permute-done | bytes 131104 | tf_op jit(solution)/shard_map/ppermute | solution.py:41
  19.9 2.8 %collective-permute-done.6 = bf16[256,256]{1,0:T(8,128)(2,1)S(1)} collective-permute-done((bf16[256,256]{1,0:T(8,128)(2,1)S(1)}, bf16[256,256]{1,0:T(8,128)(2,1)S(1)}, u32[]{:S(2)}, u32[]{:S(2)}) %collective-permute-start.6) | collective-permute-done | bytes 131104 | tf_op jit(solution)/shard_map/ppermute | solution.py:41
  22.7 2.8 %collective-permute-done.4 = bf16[256,256]{1,0:T(8,128)(2,1)S(1)} collective-permute-done((bf16[256,256]{1,0:T(8,128)(2,1)S(1)}, bf16[256,256]{1,0:T(8,128)(2,1)S(1)}, u32[]{:S(2)}, u32[]{:S(2)}) %collective-permute-start.4) | collective-permute-done | bytes 131104 | tf_op jit(solution)/shard_map/ppermute | solution.py:41
  25.5 2.2 %collective-permute-done.3 = bf16[256,256]{1,0:T(8,128)(2,1)S(1)} collective-permute-done((bf16[256,256]{1,0:T(8,128)(2,1)S(1)}, bf16[256,256]{1,0:T(8,128)(2,1)S(1)}, u32[]{:S(2)}, u32[]{:S(2)}) %collective-permute-start.3) | collective-permute-done | bytes 131104 | tf_op jit(solution)/shard_map/ppermute | solution.py:41
  27.7 0.1 fusion
  27.8 3.9 %collective-permute-start.9 = (bf16[256,256]{1,0:T(8,128)(2,1)S(1)}, bf16[256,256]{1,0:T(8,128)(2,1)S(1)}, u32[]{:S(2)}, u32[]{:S(2)}) collective-permute-start(bf16[256,256]{1,0:T(8,128)(2,1)S(1)} %get-tuple-element.16), channel_id=1, source_target_pairs={{0,24},{4,28},{8,16},{12,20},{16,8},{20,12},{24,0},{28,4},{1,25},{... | collective-permute-start | bytes 393224 | tf_op jit(solution)/shard_map/ppermute | solution.py:41
  31.7 0.6 collective-permute-start.5
  32.4 3.8 %collective-permute-done.9.refs_3_ = bf16[256,256]{1,0:T(8,128)(2,1)S(1)} collective-permute-done((bf16[256,256]{1,0:T(8,128)(2,1)S(1)}, bf16[256,256]{1,0:T(8,128)(2,1)S(1)}, u32[]{:S(2)}, u32[]{:S(2)}) %collective-permute-start.9) | collective-permute-done | bytes 131104 | tf_op jit(solution)/shard_map/ppermute | solution.py:41
  36.1 6.6 %collective-permute-done.7.refs_2_ = bf16[256,256]{1,0:T(8,128)(2,1)S(1)} collective-permute-done((bf16[256,256]{1,0:T(8,128)(2,1)S(1)}, bf16[256,256]{1,0:T(8,128)(2,1)S(1)}, u32[]{:S(2)}, u32[]{:S(2)}) %collective-permute-start.7) | collective-permute-done | bytes 131104 | tf_op jit(solution)/shard_map/ppermute | solution.py:41
  42.8 0.0 collective-permute-done.5.refs_1_
  42.8 0.7 copy-done.5
  43.5 1.8 %shard_map.112 = (bf16[256,256]{1,0:T(8,128)(2,1)}, bf16[256,256]{1,0:T(8,128)(2,1)S(1)}, bf16[4,80,256]{2,1,0:T(8,128)(2,1)S(1)}) custom-call(s32[2]{0:T(128)S(1)} %pad_add_fusion.place_ref, f32[256,256]{1,0:T(8,128)S(1)} %get-tuple-element.19.refs_0_, bf16[256,256]{1,0:T(8,128)(2,1)S(1)} %collective-permute-done.5.refs_1_, ...), custom_call_target="tpu_custom_call" | custom-call | flops 167772160 | bytes 2000000 | tf_op jit(solution)/shard_map/pallas_call | solution.py:165
  45.3 0.1 collective-permute-start.20
  45.3 1.9 %collective-permute-start.22 = (bf16[80,256]{1,0:T(8,128)(2,1)S(1)}, bf16[80,256]{1,0:T(8,128)(2,1)S(1)}, u32[]{:S(2)}, u32[]{:S(2)}) collective-permute-start(bf16[80,256]{1,0:T(8,128)(2,1)S(1)} %get-tuple-element.29), channel_id=1, source_target_pairs={{0,3},{1,2},{2,1},{3,0},{4,7},{5,6},{6,5},{7,4},{8,11},{9,10},{10,... | collective-permute-start | bytes 122888 | tf_op jit(solution)/shard_map/ppermute | solution.py:41
  47.2 0.2 collective-permute-start.21
  47.5 2.5 %collective-permute-start.15 = (bf16[256,256]{1,0:T(8,128)(2,1)S(1)}, bf16[256,256]{1,0:T(8,128)(2,1)S(1)}, u32[]{:S(2)}, u32[]{:S(2)}) collective-permute-start(bf16[256,256]{1,0:T(8,128)(2,1)S(1)} %get-tuple-element.11.refs_0_), channel_id=1, source_target_pairs={{0,24},{4,28},{8,16},{12,20},{16,8},{20,12},{24,0},{28,4},{1,25},{... | collective-permute-start | bytes 393224 | tf_op jit(solution)/shard_map/ppermute | solution.py:41
  50.0 0.0 collective-permute-start.13
  50.0 0.0 collective-permute-done.20
  50.0 1.9 %collective-permute-start.11 = (bf16[256,256]{1,0:T(8,128)(2,1)S(1)}, bf16[256,256]{1,0:T(8,128)(2,1)S(1)}, u32[]{:S(2)}, u32[]{:S(2)}) collective-permute-start(bf16[256,256]{1,0:T(8,128)(2,1)S(1)} %get-tuple-element.11.refs_0_), channel_id=1, source_target_pairs={{0,8},{4,12},{8,0},{12,4},{16,24},{20,28},{24,16},{28,20},{1,9},{5... | collective-permute-start | bytes 393224 | tf_op jit(solution)/shard_map/ppermute | solution.py:41
  51.9 2.5 %collective-permute-start.25 = (bf16[80,256]{1,0:T(8,128)(2,1)S(1)}, bf16[80,256]{1,0:T(8,128)(2,1)S(1)}, u32[]{:S(2)}, u32[]{:S(2)}) collective-permute-start(bf16[80,256]{1,0:T(8,128)(2,1)S(1)} %fusion.4), channel_id=1, source_target_pairs={{0,24},{4,28},{8,16},{12,20},{16,8},{20,12},{24,0},{28,4},{1,25},{... | collective-permute-start | bytes 122888 | tf_op jit(solution)/shard_map/ppermute | solution.py:41
  54.5 7.2 %collective-permute-done.25 = bf16[80,256]{1,0:T(8,128)(2,1)S(1)} collective-permute-done((bf16[80,256]{1,0:T(8,128)(2,1)S(1)}, bf16[80,256]{1,0:T(8,128)(2,1)S(1)}, u32[]{:S(2)}, u32[]{:S(2)}) %collective-permute-start.25) | collective-permute-done | bytes 40992 | tf_op jit(solution)/shard_map/ppermute | solution.py:41
  61.7 2.2 %collective-permute-start.23 = (bf16[80,256]{1,0:T(8,128)(2,1)S(1)}, bf16[80,256]{1,0:T(8,128)(2,1)S(1)}, u32[]{:S(2)}, u32[]{:S(2)}) collective-permute-start(bf16[80,256]{1,0:T(8,128)(2,1)S(1)} %fusion.4), channel_id=1, source_target_pairs={{0,8},{4,12},{8,0},{12,4},{16,24},{20,28},{24,16},{28,20},{1,9},{5... | collective-permute-start | bytes 122888 | tf_op jit(solution)/shard_map/ppermute | solution.py:41
  63.8 0.2 collective-permute-done.24
  64.0 1.5 %collective-permute-start.10 = (bf16[256,256]{1,0:T(8,128)(2,1)S(1)}, bf16[256,256]{1,0:T(8,128)(2,1)S(1)}, u32[]{:S(2)}, u32[]{:S(2)}) collective-permute-start(bf16[256,256]{1,0:T(8,128)(2,1)S(1)} %get-tuple-element.11.refs_0_), channel_id=1, source_target_pairs={{0,4},{4,0},{8,12},{12,8},{16,20},{20,16},{24,28},{28,24},{1,5},{5... | collective-permute-start | bytes 393224 | tf_op jit(solution)/shard_map/ppermute | solution.py:41
  65.5 0.5 collective-permute-start.16
  66.0 1.5 %collective-permute-start.14 = (bf16[256,256]{1,0:T(8,128)(2,1)S(1)}, bf16[256,256]{1,0:T(8,128)(2,1)S(1)}, u32[]{:S(2)}, u32[]{:S(2)}) collective-permute-start(bf16[256,256]{1,0:T(8,128)(2,1)S(1)} %collective-permute-done.13.refs_4_), channel_id=1, source_target_pairs={{0,4},{4,0},{8,12},{12,8},{16,20},{20,16},{24,28},{28,24},{1,5},{5... | collective-permute-start | bytes 393224 | tf_op jit(solution)/shard_map/ppermute | solution.py:41
  67.6 0.5 collective-permute-start.12
  68.1 1.6 %collective-permute-start.26 = (bf16[80,256]{1,0:T(8,128)(2,1)S(1)}, bf16[80,256]{1,0:T(8,128)(2,1)S(1)}, u32[]{:S(2)}, u32[]{:S(2)}) collective-permute-start(bf16[80,256]{1,0:T(8,128)(2,1)S(1)} %add_convert_fusion), channel_id=1, source_target_pairs={{0,4},{4,0},{8,12},{12,8},{16,20},{20,16},{24,28},{28,24},{1,5},{5... | collective-permute-start | bytes 122888 | tf_op jit(solution)/shard_map/ppermute | solution.py:41
  69.7 0.7 collective-permute-done.10.refs_1_
  70.4 2.8 %collective-permute-done.16.refs_7_ = bf16[256,256]{1,0:T(8,128)(2,1)S(1)} collective-permute-done((bf16[256,256]{1,0:T(8,128)(2,1)S(1)}, bf16[256,256]{1,0:T(8,128)(2,1)S(1)}, u32[]{:S(2)}, u32[]{:S(2)}) %collective-permute-start.16) | collective-permute-done | bytes 131104 | tf_op jit(solution)/shard_map/ppermute | solution.py:41
  73.2 2.8 %collective-permute-done.14.refs_5_ = bf16[256,256]{1,0:T(8,128)(2,1)S(1)} collective-permute-done((bf16[256,256]{1,0:T(8,128)(2,1)S(1)}, bf16[256,256]{1,0:T(8,128)(2,1)S(1)}, u32[]{:S(2)}, u32[]{:S(2)}) %collective-permute-start.14) | collective-permute-done | bytes 131104 | tf_op jit(solution)/shard_map/ppermute | solution.py:41
  76.0 2.3 %collective-permute-done.12.refs_3_ = bf16[256,256]{1,0:T(8,128)(2,1)S(1)} collective-permute-done((bf16[256,256]{1,0:T(8,128)(2,1)S(1)}, bf16[256,256]{1,0:T(8,128)(2,1)S(1)}, u32[]{:S(2)}, u32[]{:S(2)}) %collective-permute-start.12) | collective-permute-done | bytes 131104 | tf_op jit(solution)/shard_map/ppermute | solution.py:41
  78.3 1.2 %shard_map.113 = bf16[4,256,256]{2,1,0:T(8,128)(2,1)S(1)} custom-call(s32[24]{0:T(128)S(1)} %select_add_fusion.code_ref, s32[2]{0:T(128)S(1)} %pad_add_fusion.place_ref, bf16[256,256]{1,0:T(8,128)(2,1)S(1)} %get-tuple-element.11.refs_0_, bf16[256,256]{1,0:T(8,128)(2,1)S(1)} %collective-permute-done.10.refs_1_, ...), custom_call_target="tpu_custom_call" | custom-call | flops 201326592 | bytes 2000000 | tf_op jit(solution)/shard_map/pallas_call | solution.py:190
  79.5 0.1 collective-permute-start.19
  79.6 1.8 %collective-permute-start.18 = (bf16[256,256]{1,0:T(8,128)(2,1)S(1)}, bf16[256,256]{1,0:T(8,128)(2,1)S(1)}, u32[]{:S(2)}, u32[]{:S(2)}) collective-permute-start(bf16[256,256]{1,0:T(8,128)(2,1)S(1)} %get-tuple-element.25), channel_id=1, source_target_pairs={{0,2},{1,3},{2,0},{3,1},{4,6},{5,7},{6,4},{7,5},{8,10},{9,11},{10,... | collective-permute-start | bytes 393224 | tf_op jit(solution)/shard_map/ppermute | solution.py:41
  81.4 0.1 collective-permute-start.17
  81.5 1.3 %collective-permute-start.29 = (bf16[64,256]{1,0:T(8,128)(2,1)S(1)}, bf16[64,256]{1,0:T(8,128)(2,1)S(1)}, u32[]{:S(2)}, u32[]{:S(2)}) collective-permute-start(bf16[64,256]{1,0:T(8,128)(2,1)S(1)} %slice.112.refs_4_), channel_id=1, source_target_pairs={{0,3},{1,2},{2,1},{3,0},{4,7},{5,6},{6,5},{7,4},{8,11},{9,10},{10,... | collective-permute-start | bytes 98312 | tf_op jit(solution)/shard_map/ppermute | solution.py:41
  82.8 0.8 collective-permute-start.28
  83.6 5.0 %collective-permute-done.29.refs_7_ = bf16[64,256]{1,0:T(8,128)(2,1)S(1)} collective-permute-done((bf16[64,256]{1,0:T(8,128)(2,1)S(1)}, bf16[64,256]{1,0:T(8,128)(2,1)S(1)}, u32[]{:S(2)}, u32[]{:S(2)}) %collective-permute-start.29) | collective-permute-done | bytes 32800 | tf_op jit(solution)/shard_map/ppermute | solution.py:41
  88.7 0.3 collective-permute-start.27
  89.0 0.6 collective-permute-done.28.refs_6_
  89.6 0.3 collective-permute-done.27.refs_5_
  89.9 1.3 %shard_map.114 = (bf16[256,256]{1,0:T(8,128)(2,1)}, f32[256,256]{1,0:T(8,128)}, f32[1,256]{1,0:T(1,128)}) custom-call(s32[2]{0:T(128)S(1)} %pad_add_fusion.place_ref, bf16[256,256]{1,0:T(8,128)(2,1)S(1)} %get-tuple-element.27.refs_0_, bf16[256,256]{1,0:T(8,128)(2,1)S(1)} %collective-permute-done.17.refs_1_, ...), custom_call_target="tpu_custom_call" | custom-call | bytes 2000000 | tf_op jit(solution)/shard_map/pallas_call | solution.py:201
  (36 shorter events, 0.2 us)
Async XLA Ops:
  0.6 3.2 %copy-start.8 = (s32[1,1,8]{2,1,0:T(1,128)S(1)}, s32[1,1,8]{2,1,0:T(1,128)}, u32[]{:S(2)}) copy-start(s32[1,1,8]{2,1,0:T(1,128)} %param.14) | copy-start | bytes 100
  0.6 7.2 %collective-permute-start.1 = (bf16[256,256]{1,0:T(8,128)(2,1)}, bf16[256,256]{1,0:T(8,128)(2,1)S(1)}, u32[]{:S(2)}, u32[]{:S(2)}) collective-permute-start(bf16[256,256]{1,0:T(8,128)(2,1)} %refs_0_.1), channel_id=1, source_target_pairs={{0,2},{1,3},{2,0},{3,1},{4,6},{5,7},{6,4},{7,5},{8,10},{9,11},{10,... | collective-permute-start | bytes 393224 | tf_op jit(solution)/shard_map/ppermute | solution.py:41
  3.6 4.2 %collective-permute-start = (bf16[256,256]{1,0:T(8,128)(2,1)}, bf16[256,256]{1,0:T(8,128)(2,1)S(1)}, u32[]{:S(2)}, u32[]{:S(2)}) collective-permute-start(bf16[256,256]{1,0:T(8,128)(2,1)} %refs_0_.1), channel_id=1, source_target_pairs={{0,1},{1,0},{2,3},{3,2},{4,5},{5,4},{6,7},{7,6},{8,9},{9,8},{10,11... | collective-permute-start | bytes 393224 | tf_op jit(solution)/shard_map/ppermute | solution.py:41
  3.6 6.1 %collective-permute-start.2 = (bf16[256,256]{1,0:T(8,128)(2,1)}, bf16[256,256]{1,0:T(8,128)(2,1)S(1)}, u32[]{:S(2)}, u32[]{:S(2)}) collective-permute-start(bf16[256,256]{1,0:T(8,128)(2,1)} %refs_0_.1), channel_id=1, source_target_pairs={{0,3},{1,2},{2,1},{3,0},{4,7},{5,6},{6,5},{7,4},{8,11},{9,10},{10,... | collective-permute-start | bytes 393224 | tf_op jit(solution)/shard_map/ppermute | solution.py:41
  3.9 0.7 copy-start.6
  4.6 0.7 copy-start.7
  9.7 1.1 %copy-start = (bf16[1,1,8,3,128,128]{5,4,3,2,1,0:T(8,128)(2,1)S(1)}, bf16[1,1,8,3,128,128]{5,4,3,2,1,0:T(8,128)(2,1)}, u32[]{:S(2)}) copy-start(bf16[1,1,8,3,128,128]{5,4,3,2,1,0:T(8,128)(2,1)} %param.11) | copy-start | bytes 2359300
  10.8 0.9 copy-start.2
  13.5 6.4 %collective-permute-start.8 = (bf16[256,256]{1,0:T(8,128)(2,1)S(1)}, bf16[256,256]{1,0:T(8,128)(2,1)S(1)}, u32[]{:S(2)}, u32[]{:S(2)}) collective-permute-start(bf16[256,256]{1,0:T(8,128)(2,1)S(1)} %get-tuple-element.20), channel_id=1, source_target_pairs={{0,4},{4,0},{8,12},{12,8},{16,20},{20,16},{24,28},{28,24},{1,5},{5... | collective-permute-start | bytes 393224 | tf_op jit(solution)/shard_map/ppermute | solution.py:41
  15.0 7.7 %collective-permute-start.6 = (bf16[256,256]{1,0:T(8,128)(2,1)S(1)}, bf16[256,256]{1,0:T(8,128)(2,1)S(1)}, u32[]{:S(2)}, u32[]{:S(2)}) collective-permute-start(bf16[256,256]{1,0:T(8,128)(2,1)S(1)} %get-tuple-element.21), channel_id=1, source_target_pairs={{0,4},{4,0},{8,12},{12,8},{16,20},{20,16},{24,28},{28,24},{1,5},{5... | collective-permute-start | bytes 393224 | tf_op jit(solution)/shard_map/ppermute | solution.py:41
  15.6 9.9 %collective-permute-start.4 = (bf16[256,256]{1,0:T(8,128)(2,1)S(1)}, bf16[256,256]{1,0:T(8,128)(2,1)S(1)}, u32[]{:S(2)}, u32[]{:S(2)}) collective-permute-start(bf16[256,256]{1,0:T(8,128)(2,1)S(1)} %get-tuple-element.22), channel_id=1, source_target_pairs={{0,4},{4,0},{8,12},{12,8},{16,20},{20,16},{24,28},{28,24},{1,5},{5... | collective-permute-start | bytes 393224 | tf_op jit(solution)/shard_map/ppermute | solution.py:41
  17.1 25.7 %copy-start.3 = (bf16[256,256]{1,0:T(8,128)(2,1)S(1)}, bf16[256,256]{1,0:T(8,128)(2,1)}, u32[]{:S(2)}) copy-start(bf16[256,256]{1,0:T(8,128)(2,1)} %refs_4_.1) | copy-start | bytes 393220
  17.1 25.7 %copy-start.4 = (bf16[256,256]{1,0:T(8,128)(2,1)S(1)}, bf16[256,256]{1,0:T(8,128)(2,1)}, u32[]{:S(2)}) copy-start(bf16[256,256]{1,0:T(8,128)(2,1)} %refs_6_.1) | copy-start | bytes 393220
  17.1 10.6 %collective-permute-start.3 = (bf16[256,256]{1,0:T(8,128)(2,1)S(1)}, bf16[256,256]{1,0:T(8,128)(2,1)S(1)}, u32[]{:S(2)}, u32[]{:S(2)}) collective-permute-start(bf16[256,256]{1,0:T(8,128)(2,1)S(1)} %get-tuple-element.23), channel_id=1, source_target_pairs={{0,4},{4,0},{8,12},{12,8},{16,20},{20,16},{24,28},{28,24},{1,5},{5... | collective-permute-start | bytes 393224 | tf_op jit(solution)/shard_map/ppermute | solution.py:41
  27.8 8.3 %collective-permute-start.9 = (bf16[256,256]{1,0:T(8,128)(2,1)S(1)}, bf16[256,256]{1,0:T(8,128)(2,1)S(1)}, u32[]{:S(2)}, u32[]{:S(2)}) collective-permute-start(bf16[256,256]{1,0:T(8,128)(2,1)S(1)} %get-tuple-element.16), channel_id=1, source_target_pairs={{0,24},{4,28},{8,16},{12,20},{16,8},{20,12},{24,0},{28,4},{1,25},{... | collective-permute-start | bytes 393224 | tf_op jit(solution)/shard_map/ppermute | solution.py:41
  31.7 11.1 %collective-permute-start.7 = (bf16[256,256]{1,0:T(8,128)(2,1)S(1)}, bf16[256,256]{1,0:T(8,128)(2,1)S(1)}, u32[]{:S(2)}, u32[]{:S(2)}) collective-permute-start(bf16[256,256]{1,0:T(8,128)(2,1)S(1)} %get-tuple-element.17), channel_id=1, source_target_pairs={{0,16},{4,20},{8,24},{12,28},{16,0},{20,4},{24,8},{28,12},{1,17},{... | collective-permute-start | bytes 393224 | tf_op jit(solution)/shard_map/ppermute | solution.py:41
  31.7 11.1 %collective-permute-start.5 = (bf16[256,256]{1,0:T(8,128)(2,1)S(1)}, bf16[256,256]{1,0:T(8,128)(2,1)S(1)}, u32[]{:S(2)}, u32[]{:S(2)}) collective-permute-start(bf16[256,256]{1,0:T(8,128)(2,1)S(1)} %get-tuple-element.18), channel_id=1, source_target_pairs={{0,8},{4,12},{8,0},{12,4},{16,24},{20,28},{24,16},{28,20},{1,9},{5... | collective-permute-start | bytes 393224 | tf_op jit(solution)/shard_map/ppermute | solution.py:41
  42.8 0.7 copy-start.5
  43.5 34.8 %copy-start.1 = (bf16[1,1,8,3,128,128]{5,4,3,2,1,0:T(8,128)(2,1)S(1)}, bf16[1,1,8,3,128,128]{5,4,3,2,1,0:T(8,128)(2,1)}, u32[]{:S(2)}) copy-start(bf16[1,1,8,3,128,128]{5,4,3,2,1,0:T(8,128)(2,1)} %param.11) | copy-start | bytes 2359300
  45.3 4.7 %collective-permute-start.20 = (bf16[80,256]{1,0:T(8,128)(2,1)S(1)}, bf16[80,256]{1,0:T(8,128)(2,1)S(1)}, u32[]{:S(2)}, u32[]{:S(2)}) collective-permute-start(bf16[80,256]{1,0:T(8,128)(2,1)S(1)} %get-tuple-element.28), channel_id=1, source_target_pairs={{0,1},{1,0},{2,3},{3,2},{4,5},{5,4},{6,7},{7,6},{8,9},{9,8},{10,11... | collective-permute-start | bytes 122888 | tf_op jit(solution)/shard_map/ppermute | solution.py:41
  45.3 6.5 %collective-permute-start.22 = (bf16[80,256]{1,0:T(8,128)(2,1)S(1)}, bf16[80,256]{1,0:T(8,128)(2,1)S(1)}, u32[]{:S(2)}, u32[]{:S(2)}) collective-permute-start(bf16[80,256]{1,0:T(8,128)(2,1)S(1)} %get-tuple-element.29), channel_id=1, source_target_pairs={{0,3},{1,2},{2,1},{3,0},{4,7},{5,6},{6,5},{7,4},{8,11},{9,10},{10,... | collective-permute-start | bytes 122888 | tf_op jit(solution)/shard_map/ppermute | solution.py:41
  47.2 4.6 %collective-permute-start.21 = (bf16[80,256]{1,0:T(8,128)(2,1)S(1)}, bf16[80,256]{1,0:T(8,128)(2,1)S(1)}, u32[]{:S(2)}, u32[]{:S(2)}) collective-permute-start(bf16[80,256]{1,0:T(8,128)(2,1)S(1)} %get-tuple-element.30), channel_id=1, source_target_pairs={{0,2},{1,3},{2,0},{3,1},{4,6},{5,7},{6,4},{7,5},{8,10},{9,11},{10,... | collective-permute-start | bytes 122888 | tf_op jit(solution)/shard_map/ppermute | solution.py:41
  47.5 18.0 %collective-permute-start.15 = (bf16[256,256]{1,0:T(8,128)(2,1)S(1)}, bf16[256,256]{1,0:T(8,128)(2,1)S(1)}, u32[]{:S(2)}, u32[]{:S(2)}) collective-permute-start(bf16[256,256]{1,0:T(8,128)(2,1)S(1)} %get-tuple-element.11.refs_0_), channel_id=1, source_target_pairs={{0,24},{4,28},{8,16},{12,20},{16,8},{20,12},{24,0},{28,4},{1,25},{... | collective-permute-start | bytes 393224 | tf_op jit(solution)/shard_map/ppermute | solution.py:41
  50.0 16.1 %collective-permute-start.13 = (bf16[256,256]{1,0:T(8,128)(2,1)S(1)}, bf16[256,256]{1,0:T(8,128)(2,1)S(1)}, u32[]{:S(2)}, u32[]{:S(2)}) collective-permute-start(bf16[256,256]{1,0:T(8,128)(2,1)S(1)} %get-tuple-element.11.refs_0_), channel_id=1, source_target_pairs={{0,16},{4,20},{8,24},{12,28},{16,0},{20,4},{24,8},{28,12},{1,17},{... | collective-permute-start | bytes 393224 | tf_op jit(solution)/shard_map/ppermute | solution.py:41
  50.0 17.6 %collective-permute-start.11 = (bf16[256,256]{1,0:T(8,128)(2,1)S(1)}, bf16[256,256]{1,0:T(8,128)(2,1)S(1)}, u32[]{:S(2)}, u32[]{:S(2)}) collective-permute-start(bf16[256,256]{1,0:T(8,128)(2,1)S(1)} %get-tuple-element.11.refs_0_), channel_id=1, source_target_pairs={{0,8},{4,12},{8,0},{12,4},{16,24},{20,28},{24,16},{28,20},{1,9},{5... | collective-permute-start | bytes 393224 | tf_op jit(solution)/shard_map/ppermute | solution.py:41
  51.9 9.7 %collective-permute-start.25 = (bf16[80,256]{1,0:T(8,128)(2,1)S(1)}, bf16[80,256]{1,0:T(8,128)(2,1)S(1)}, u32[]{:S(2)}, u32[]{:S(2)}) collective-permute-start(bf16[80,256]{1,0:T(8,128)(2,1)S(1)} %fusion.4), channel_id=1, source_target_pairs={{0,24},{4,28},{8,16},{12,20},{16,8},{20,12},{24,0},{28,4},{1,25},{... | collective-permute-start | bytes 122888 | tf_op jit(solution)/shard_map/ppermute | solution.py:41
  54.5 9.6 %collective-permute-start.24 = (bf16[80,256]{1,0:T(8,128)(2,1)S(1)}, bf16[80,256]{1,0:T(8,128)(2,1)S(1)}, u32[]{:S(2)}, u32[]{:S(2)}) collective-permute-start(bf16[80,256]{1,0:T(8,128)(2,1)S(1)} %fusion.4), channel_id=1, source_target_pairs={{0,16},{4,20},{8,24},{12,28},{16,0},{20,4},{24,8},{28,12},{1,17},{... | collective-permute-start | bytes 122888 | tf_op jit(solution)/shard_map/ppermute | solution.py:41
  61.7 6.4 %collective-permute-start.23 = (bf16[80,256]{1,0:T(8,128)(2,1)S(1)}, bf16[80,256]{1,0:T(8,128)(2,1)S(1)}, u32[]{:S(2)}, u32[]{:S(2)}) collective-permute-start(bf16[80,256]{1,0:T(8,128)(2,1)S(1)} %fusion.4), channel_id=1, source_target_pairs={{0,8},{4,12},{8,0},{12,4},{16,24},{20,28},{24,16},{28,20},{1,9},{5... | collective-permute-start | bytes 122888 | tf_op jit(solution)/shard_map/ppermute | solution.py:41
  64.0 6.4 %collective-permute-start.10 = (bf16[256,256]{1,0:T(8,128)(2,1)S(1)}, bf16[256,256]{1,0:T(8,128)(2,1)S(1)}, u32[]{:S(2)}, u32[]{:S(2)}) collective-permute-start(bf16[256,256]{1,0:T(8,128)(2,1)S(1)} %get-tuple-element.11.refs_0_), channel_id=1, source_target_pairs={{0,4},{4,0},{8,12},{12,8},{16,20},{20,16},{24,28},{28,24},{1,5},{5... | collective-permute-start | bytes 393224 | tf_op jit(solution)/shard_map/ppermute | solution.py:41
  65.5 7.7 %collective-permute-start.16 = (bf16[256,256]{1,0:T(8,128)(2,1)S(1)}, bf16[256,256]{1,0:T(8,128)(2,1)S(1)}, u32[]{:S(2)}, u32[]{:S(2)}) collective-permute-start(bf16[256,256]{1,0:T(8,128)(2,1)S(1)} %collective-permute-done.15.refs_6_), channel_id=1, source_target_pairs={{0,4},{4,0},{8,12},{12,8},{16,20},{20,16},{24,28},{28,24},{1,5},{5... | collective-permute-start | bytes 393224 | tf_op jit(solution)/shard_map/ppermute | solution.py:41
  66.0 10.0 %collective-permute-start.14 = (bf16[256,256]{1,0:T(8,128)(2,1)S(1)}, bf16[256,256]{1,0:T(8,128)(2,1)S(1)}, u32[]{:S(2)}, u32[]{:S(2)}) collective-permute-start(bf16[256,256]{1,0:T(8,128)(2,1)S(1)} %collective-permute-done.13.refs_4_), channel_id=1, source_target_pairs={{0,4},{4,0},{8,12},{12,8},{16,20},{20,16},{24,28},{28,24},{1,5},{5... | collective-permute-start | bytes 393224 | tf_op jit(solution)/shard_map/ppermute | solution.py:41
  67.6 10.7 %collective-permute-start.12 = (bf16[256,256]{1,0:T(8,128)(2,1)S(1)}, bf16[256,256]{1,0:T(8,128)(2,1)S(1)}, u32[]{:S(2)}, u32[]{:S(2)}) collective-permute-start(bf16[256,256]{1,0:T(8,128)(2,1)S(1)} %collective-permute-done.11.refs_2_), channel_id=1, source_target_pairs={{0,4},{4,0},{8,12},{12,8},{16,20},{20,16},{24,28},{28,24},{1,5},{5... | collective-permute-start | bytes 393224 | tf_op jit(solution)/shard_map/ppermute | solution.py:41
  68.1 13.4 %collective-permute-start.26 = (bf16[80,256]{1,0:T(8,128)(2,1)S(1)}, bf16[80,256]{1,0:T(8,128)(2,1)S(1)}, u32[]{:S(2)}, u32[]{:S(2)}) collective-permute-start(bf16[80,256]{1,0:T(8,128)(2,1)S(1)} %add_convert_fusion), channel_id=1, source_target_pairs={{0,4},{4,0},{8,12},{12,8},{16,20},{20,16},{24,28},{28,24},{1,5},{5... | collective-permute-start | bytes 122888 | tf_op jit(solution)/shard_map/ppermute | solution.py:41
  79.5 10.3 %collective-permute-start.19 = (bf16[256,256]{1,0:T(8,128)(2,1)S(1)}, bf16[256,256]{1,0:T(8,128)(2,1)S(1)}, u32[]{:S(2)}, u32[]{:S(2)}) collective-permute-start(bf16[256,256]{1,0:T(8,128)(2,1)S(1)} %get-tuple-element.24), channel_id=1, source_target_pairs={{0,3},{1,2},{2,1},{3,0},{4,7},{5,6},{6,5},{7,4},{8,11},{9,10},{10,... | collective-permute-start | bytes 393224 | tf_op jit(solution)/shard_map/ppermute | solution.py:41
  79.6 10.3 %collective-permute-start.18 = (bf16[256,256]{1,0:T(8,128)(2,1)S(1)}, bf16[256,256]{1,0:T(8,128)(2,1)S(1)}, u32[]{:S(2)}, u32[]{:S(2)}) collective-permute-start(bf16[256,256]{1,0:T(8,128)(2,1)S(1)} %get-tuple-element.25), channel_id=1, source_target_pairs={{0,2},{1,3},{2,0},{3,1},{4,6},{5,7},{6,4},{7,5},{8,10},{9,11},{10,... | collective-permute-start | bytes 393224 | tf_op jit(solution)/shard_map/ppermute | solution.py:41
  81.4 8.5 %collective-permute-start.17 = (bf16[256,256]{1,0:T(8,128)(2,1)S(1)}, bf16[256,256]{1,0:T(8,128)(2,1)S(1)}, u32[]{:S(2)}, u32[]{:S(2)}) collective-permute-start(bf16[256,256]{1,0:T(8,128)(2,1)S(1)} %get-tuple-element.26), channel_id=1, source_target_pairs={{0,1},{1,0},{2,3},{3,2},{4,5},{5,4},{6,7},{7,6},{8,9},{9,8},{10,11... | collective-permute-start | bytes 393224 | tf_op jit(solution)/shard_map/ppermute | solution.py:41
  81.5 7.2 %collective-permute-start.29 = (bf16[64,256]{1,0:T(8,128)(2,1)S(1)}, bf16[64,256]{1,0:T(8,128)(2,1)S(1)}, u32[]{:S(2)}, u32[]{:S(2)}) collective-permute-start(bf16[64,256]{1,0:T(8,128)(2,1)S(1)} %slice.112.refs_4_), channel_id=1, source_target_pairs={{0,3},{1,2},{2,1},{3,0},{4,7},{5,6},{6,5},{7,4},{8,11},{9,10},{10,... | collective-permute-start | bytes 98312 | tf_op jit(solution)/shard_map/ppermute | solution.py:41
  82.8 6.8 %collective-permute-start.28 = (bf16[64,256]{1,0:T(8,128)(2,1)S(1)}, bf16[64,256]{1,0:T(8,128)(2,1)S(1)}, u32[]{:S(2)}, u32[]{:S(2)}) collective-permute-start(bf16[64,256]{1,0:T(8,128)(2,1)S(1)} %slice.112.refs_4_), channel_id=1, source_target_pairs={{0,2},{1,3},{2,0},{3,1},{4,6},{5,7},{6,4},{7,5},{8,10},{9,11},{10,... | collective-permute-start | bytes 98312 | tf_op jit(solution)/shard_map/ppermute | solution.py:41
  88.7 1.2 %collective-permute-start.27 = (bf16[64,256]{1,0:T(8,128)(2,1)S(1)}, bf16[64,256]{1,0:T(8,128)(2,1)S(1)}, u32[]{:S(2)}, u32[]{:S(2)}) collective-permute-start(bf16[64,256]{1,0:T(8,128)(2,1)S(1)} %slice.112.refs_4_), channel_id=1, source_target_pairs={{0,1},{1,0},{2,3},{3,2},{4,5},{5,4},{6,7},{7,6},{8,9},{9,8},{10,11... | collective-permute-start | bytes 98312 | tf_op jit(solution)/shard_map/ppermute | solution.py:41

commit v2 on v1

v2 whole, which is shorter than its diff:
```python
import functools
import math

import jax
import jax.numpy as jnp
from jax import lax
from jax.experimental import pallas as pl
from jax.experimental.pallas import tpu as pltpu
from jax.sharding import PartitionSpec as P

F32 = jnp.float32
BF16 = jnp.bfloat16
PAD = 16


def call(body, out_shape, scratch=(), n_smem=0, n_vmem=0, flops=0, n_any=0):
    specs = [pl.BlockSpec(memory_space=pltpu.SMEM)] * n_smem
    specs += [pl.BlockSpec(memory_space=pltpu.VMEM)] * n_vmem
    specs += [pl.BlockSpec(memory_space=pl.ANY)] * n_any
    many = isinstance(out_shape, (list, tuple))
    vmem = pl.BlockSpec(memory_space=pltpu.VMEM)
    return pl.pallas_call(
        body,
        out_shape=out_shape,
        in_specs=specs,
        out_specs=[vmem] * len(out_shape) if many else vmem,
        scratch_shapes=list(scratch),
        cost_estimate=pl.CostEstimate(flops=flops, bytes_accessed=2_000_000, transcendentals=0),
        compiler_params=pltpu.CompilerParams(vmem_limit_bytes=48 * 1024 * 1024),
    )


def tree_sum(items):
    items = [x.astype(F32) for x in items]
    while len(items) > 1:
        items = [sum(items[i + 1 : i + 2], items[i]) for i in range(0, len(items), 2)]
    return items[0]


def send(x, axis, offset):
    size = lax.axis_size(axis)
    return lax.ppermute(x, axis, [(i, i ^ offset) for i in range(size)])


def prepare_kernel(
    tiles, source_hbm, dest_hbm, count_hbm, feat_hbm, vals_hbm, picked_ref, own_ref, code_ref,
    source_ref, dest_ref, count_ref, feat, vals, sems,
):
    rows, slots, size, _ = vals.shape
    small = [(source_hbm, source_ref), (dest_hbm, dest_ref), (count_hbm, count_ref), (feat_hbm, feat)]
    copies = [pltpu.make_async_copy(x, y, sems.at[i]) for i, (x, y) in enumerate(small)]
    copies += [
        pltpu.make_async_copy(vals_hbm.at[o], vals.at[o], sems.at[len(small) + o]) for o in range(rows)
    ]
    for copy in copies:
        copy.start()
    for copy in copies[: len(small)]:
        copy.wait()
    for o in range(rows):
        for s in range(slots):
            code_ref[o * slots + s] = source_ref[0, s, 0, o]
    for k in range(tiles):
        own_ref[k] = feat[k * size : (k + 1) * size, :].T
    for o in range(rows):
        copies[len(small) + o].wait()
        for s in range(slots):
            live = s < count_ref[0, 0, o]
            dest = jnp.where(live, dest_ref[0, s, 0, o], tiles)
            block = vals[o, s]
            zero = jnp.zeros_like(block)
            for t in range(tiles):
                picked_ref[o, s, :, t * size : (t + 1) * size] = jnp.where(dest == t, block, zero)


def push_one(k, place_ref, code_ref, turned, picked_ref):
    owner = place_ref[0] ^ k
    total = None
    for s in range(picked_ref.shape[1]):
        part = jnp.dot(
            turned[code_ref[owner * picked_ref.shape[1] + s]], picked_ref[owner, s], preferred_element_type=F32
        )
        total = part if total is None else total + part
    return total.astype(BF16)


def push_first_kernel(ks, tiles, place_ref, code_ref, *refs):
    n = len(refs) - len(ks) - 1
    own_ref, far, picked_ref = refs[0], refs[1 : n - 1], refs[n - 1]
    outs, turned = refs[n:-1], refs[-1]
    size = picked_ref.shape[2]
    col = place_ref[1]
    for t in range(tiles):
        turned[col * tiles + t] = own_ref[t]
    for k, ref in enumerate(far, 1):
        for t in range(tiles):
            turned[(col ^ k) * tiles + t] = ref[t * size : (t + 1) * size, :].T
    for k, out_ref in zip(ks, outs):
        out_ref[...] = push_one(k, place_ref, code_ref, turned, picked_ref)


def push_second_kernel(ks, place_ref, code_ref, turned, picked_ref, *outs):
    for k, out_ref in zip(ks, outs):
        out_ref[...] = push_one(k, place_ref, code_ref, turned, picked_ref)


def add_kernel(*refs):
    refs[-1][...] = tree_sum([r[...] for r in refs[:-1]]).astype(refs[-1].dtype)


def middle_kernel(n_parts, place_ref, *refs):
    parts = refs[:n_parts]
    weight_ref, bias_ref, cot_ref, back_ref, pre_ref = refs[n_parts : n_parts + 5]
    terms, wg = refs[n_parts + 5 : -1], refs[-1]
    agg = tree_sum([p[...] for p in parts])
    high = agg.astype(BF16)
    low = (agg - high.astype(F32)).astype(BF16)
    dims = (((0,), (0,)), ((), ()))
    weight = weight_ref[...]
    pre = lax.dot_general(high, weight, dims, preferred_element_type=F32)
    pre += lax.dot_general(low, weight, dims, preferred_element_type=F32)
    pre += bias_ref[...]
    pre_ref[...] = pre
    c = math.sqrt(2.0 / math.pi)
    square = pre * pre
    t = jnp.tanh(c * pre * (1.0 + 0.044715 * square))
    slope = 0.5 * (1.0 + t) + 0.5 * pre * (1.0 - t * t) * (c * (1.0 + 3 * 0.044715 * square))
    grad = (cot_ref[...].astype(F32) * slope).astype(BF16)
    back_ref[...] = lax.dot_general(
        grad, weight, (((1,), (1,)), ((), ())), preferred_element_type=F32
    ).astype(BF16)
    wg[...] = jnp.dot(high, grad, preferred_element_type=F32)
    bias_row = jnp.sum(grad.astype(F32), axis=0, keepdims=True).astype(BF16)
    bias_rows = jnp.broadcast_to(bias_row, (PAD, bias_row.shape[1]))
    depth = wg.shape[0] // len(terms)
    for k, part in enumerate(terms):
        start = pl.multiple_of((place_ref[1] ^ k) * depth, depth)
        part[:depth, :] = wg[pl.ds(start, depth), :].astype(BF16)
        part[depth:, :] = bias_rows


def output_kernel(pre_ref, out_ref):
    pre = pre_ref[...]
    c = math.sqrt(2.0 / math.pi)
    t = jnp.tanh(c * pre * (1.0 + 0.044715 * pre * pre))
    out_ref[...] = (pre * (0.5 * (1.0 + t))).astype(BF16)


def pack_kernel(n_after, block_ref, *refs):
    part_ref, packed_ref = refs[-2:]
    part = tree_sum([r[...] for r in refs[: -2 - n_after]]).astype(BF16)
    part_ref[...] = part
    nodes = block_ref.shape[0]
    packed_ref[:nodes, :] = block_ref[...]
    packed_ref[nodes:, :] = part


def unpack_kernel(part_ref, packed_ref, out_ref):
    below = packed_ref.shape[0] - part_ref.shape[0]
    out_ref[...] = (part_ref[...].astype(F32) + packed_ref[below:, :].astype(F32)).astype(BF16)


def pull_kernel(rows, cols, tiles, place_ref, code_ref, *refs):
    grad_refs, picked_ref, outs, total = refs[:rows], refs[rows], refs[rows + 2 : -1], refs[-1]
    slots, size = picked_ref.shape[1], picked_ref.shape[2]
    row, col = place_ref[0], place_ref[1]
    total[...] = jnp.zeros_like(total)
    for k in range(rows):
        owner = row ^ k
        block = grad_refs[k][: tiles * size, :]
        for s in range(slots):
            total[code_ref[owner * picked_ref.shape[1] + s]] += jnp.dot(
                picked_ref[owner, s], block, preferred_element_type=F32
            )
    for k in range(cols):
        for t in range(tiles):
            outs[k][t * size : (t + 1) * size, :] = total[(col ^ k) * tiles + t].astype(BF16)


def last_kernel(cols, n_blocks, scale, place_ref, *refs):
    blocks, pieces = refs[:n_blocks], refs[n_blocks : n_blocks + cols]
    bias_ref, in_ref, wg_ref, bg_ref = refs[n_blocks + cols :]
    total = blocks[0][...].astype(F32)
    for b in blocks[1:]:
        total += b[...].astype(F32)
    in_ref[...] = total.astype(BF16)
    depth = wg_ref.shape[0] // cols
    for k in range(cols):
        start = pl.multiple_of((place_ref[1] ^ k) * depth, depth)
        wg_ref[pl.ds(start, depth), :] = pieces[k][...].astype(F32) * scale
    bg_ref[...] = bias_ref[...].astype(F32) * scale


def local(features, weight, bias, tile_values, tile_source, tile_dest, send_counts, cotangent):
    rows, cols = lax.axis_size("rows"), lax.axis_size("cols")
    size = tile_values.shape[-1]
    slots = tile_values.shape[3]
    nodes, width_in = features.shape
    width = weight.shape[1]
    tiles = nodes // size
    span = tiles * cols
    vals = tile_values[0, 0]
    place = jnp.stack([lax.axis_index("rows"), lax.axis_index("cols")]).astype(jnp.int32)
    source = tile_source.transpose(0, 3, 1, 2)
    dest = tile_dest.transpose(0, 3, 1, 2)
    shape = jax.ShapeDtypeStruct
    block = shape((width_in, nodes), BF16)
    flops = rows * slots * size * size * tiles * width

    far = {k: send(features, "cols", k) for k in range(cols - 1, 0, -1)}
    hbm, smem = pl.BlockSpec(memory_space=pltpu.HBM), pl.BlockSpec(memory_space=pltpu.SMEM)
    vmem = pl.BlockSpec(memory_space=pltpu.VMEM)
    picked, own, code = pl.pallas_call(
        functools.partial(prepare_kernel, tiles),
        out_shape=[
            shape((rows, slots, size, tiles * size), BF16),
            shape((tiles, width_in, size), BF16),
            shape((rows * slots,), jnp.int32),
        ],
        in_specs=[hbm] * 5,
        out_specs=[vmem, vmem, smem],
        scratch_shapes=[
            pltpu.SMEM(source.shape, jnp.int32),
            pltpu.SMEM(dest.shape, jnp.int32),
            pltpu.SMEM(send_counts.shape, jnp.int32),
            pltpu.VMEM(features.shape, BF16),
            pltpu.VMEM(vals.shape, BF16),
            pltpu.SemaphoreType.DMA((4 + rows,)),
        ],
        cost_estimate=pl.CostEstimate(flops=flops, bytes_accessed=2_000_000, transcendentals=0),
        compiler_params=pltpu.CompilerParams(vmem_limit_bytes=48 * 1024 * 1024),
    )(source, dest, send_counts, features, vals)

    odd = list(range(rows - 1, 0, -2))
    even = list(range(rows - 2, -1, -2))
    *sent, turned = call(
        functools.partial(push_first_kernel, odd, tiles),
        [block] * len(odd) + [shape((span, width_in, size), BF16)],
        n_smem=2,
        n_vmem=cols + 1,
        flops=flops,
    )(place, code, own, *[far[k] for k in range(1, cols)], picked)
    kept = call(
        functools.partial(push_second_kernel, even),
        [block] * len(even),
        n_smem=2,
        n_vmem=2,
        flops=flops,
    )(place, code, turned, picked)

    summed = {k: [kept_k, send(sent_k, "rows", 1)] for k, kept_k, sent_k in zip(even, kept, sent)}
    bit = 2
    while bit < rows:
        for k in range(rows - bit, 0, -2 * bit):
            n = len(summed[k])
            both = call(add_kernel, block, n_vmem=n)(*summed.pop(k))
            summed[k ^ bit].append(send(both, "rows", bit))
        bit *= 2
    parts = summed[0]

    depth = width_in // cols
    part_shape = shape((depth + PAD, width), BF16)
    back, pre, *terms = call(
        functools.partial(middle_kernel, len(parts)),
        [shape((nodes, width_in), BF16), shape((nodes, width), F32)] + [part_shape] * cols,
        [pltpu.VMEM((width_in, width), F32)],
        1,
        len(parts) + 3,
        8 * width * width * nodes,
    )(place, *parts, weight, bias[None, :], cotangent)

    got = {0: back}
    bit = rows // 2
    while bit > 1:
        for k in sorted(got):
            got[k ^ bit] = send(got[k], "rows", bit)
        bit //= 2
    for k in range(0, rows - 2, 2):
        got[k + 1] = send(got[k], "rows", 1)

    output = call(output_kernel, shape((nodes, width), BF16), n_vmem=1)(pre)

    after = [got[k] for k in range(1, rows - 2, 2)]
    part, packed = call(
        functools.partial(pack_kernel, len(after)),
        [part_shape, shape((nodes + depth + PAD, width), BF16)],
        n_vmem=cols + 1,
        n_any=len(after),
    )(got[rows - 2], terms[0], *[send(terms[k], "cols", k) for k in range(cols - 1, 0, -1)][::-1], *after)
    got[rows - 1] = send(packed, "rows", 1)
    part = call(unpack_kernel, part_shape, n_vmem=2)(part, got[rows - 1])
    others = [send(part, "rows", k) for k in range(2, rows, 2)]

    blocks = call(
        functools.partial(pull_kernel, rows, cols, tiles),
        [shape((nodes, width_in), BF16)] * cols,
        [pltpu.VMEM((span, size, width_in), F32)],
        2,
        rows + 1,
        flops,
        n_any=1,
    )(place, code, *[got[k] for k in range(rows)], picked, part)
    arrived = [blocks[0]]
    for k in range(cols - 2, 0, -2):
        near = send(blocks[k + 1], "cols", 1)
        both = call(add_kernel, shape((nodes, width_in), BF16), n_vmem=2)(blocks[k], near)
        arrived.append(send(both, "cols", k))
    arrived.append(send(blocks[1], "cols", 1))
    part = call(add_kernel, part_shape, n_vmem=rows // 2)(part, *others)
    piece = part[:depth]
    pieces = [piece] + [send(piece, "cols", k) for k in range(cols - 1, 0, -1)][::-1]
    scale = 1.0 / math.sqrt(nodes * rows * cols)
    input_grad, weight_grad, bias_grad = call(
        functools.partial(last_kernel, cols, len(arrived), scale),
        [
            shape((nodes, width_in), BF16),
            shape((width_in, width), F32),
            shape((1, width), F32),
        ],
        n_smem=1,
        n_vmem=len(arrived) + cols + 1,
    )(place, *arrived, *pieces, part[depth : depth + 1])
    return output, input_grad, weight_grad, bias_grad[0]


def solution(mesh):
    in_specs = (
        P(("rows", "cols"), None),
        P(),
        P(),
        P("rows", "cols", None, None, None, None),
        P("rows", "cols", None, None),
        P("rows", "cols", None, None),
        P("rows", "cols", None),
        P(("rows", "cols"), None),
    )
    out_specs = (P(("rows", "cols"), None), P(("rows", "cols"), None), P(), P())
    return jax.shard_map(local, mesh=mesh, in_specs=in_specs, out_specs=out_specs, check_vma=False)
```

time: 91.4 us -> 74.9 us (0.82)
  waiting for transfers between devices: 46.6 us -> 29.4 us
  Pallas kernels: 6.03 us -> 9.41 us
  starting transfers between devices: 33.2 us -> 30.9 us
    ppermute x30 -> x29, waiting for transfers between devices: 46.6 us -> 29.4 us  [send(): return lax.ppermute(x, axis, [(i, i ^ offset) for i in range(size)])]
    pallas_call x4 -> x14, Pallas kernels: 6.03 us -> 9.41 us  [the longest x1 2.26 us: local(): pl.pallas_call(functools.partial(prepare_kernel, tiles), out_shape=[shape...]
    ppermute x30 -> x29, starting transfers between devices: 33.2 us -> 30.9 us  [send(): return lax.ppermute(x, axis, [(i, i ^ offset) for i in range(size)])]
    unnamed x19 -> x16, local copies, waits for them, and re-layouts: 3.91 us -> 4.06 us
  transfers between devices with their start and end apart: 30 -> 29, of which waited for: 17 -> 17; matrix products, arithmetic and copies ran while one was open for 1% -> 0% of each run, Pallas kernels for 1% -> 6%
where the time goes in v2:
time: 74.9 us; the launch traced here: 74.7 us
  starting transfers between devices  30.9 us (41%)
  waiting for transfers between devices  29.4 us (39%)
  Pallas kernels  9.41 us (13%)
  local copies, waits for them, and re-layouts  4.07 us (5%)
  between operations  0.77 us (1%)
    ppermute x29, starting transfers between devices, send(): return lax.ppermute(x, axis, [(i, i ^ offset) for i in range(size)])  30.9 us
    ppermute x29, waiting for transfers between devices, send(): return lax.ppermute(x, axis, [(i, i ^ offset) for i in range(size)])  29.4 us
    unnamed x16, local copies, waits for them, and re-layouts  4.06 us
    pallas_call x1, Pallas kernels, local(): pl.pallas_call(functools.partial(prepare_kernel, tiles), out_shape=[shape...  2.26 us
  transfers between devices with their start and end apart: 29, of which 17 were waited for; matrix products, arithmetic and copies ran while one was open for 0% of the time, Pallas kernels for 6%

profile of v2, /device:TPU:0, one launch (start us, length us, event | category | flops | bytes accessed | tf_op | source)
XLA Modules:
  0.0 74.7 jit_solution(2678376228684784255)
XLA Ops:
  0.6 0.5 collective-permute-start
  1.1 2.6 %collective-permute-start.2 = (bf16[256,256]{1,0:T(8,128)(2,1)}, bf16[256,256]{1,0:T(8,128)(2,1)S(1)}, u32[]{:S(2)}, u32[]{:S(2)}) collective-permute-start(bf16[256,256]{1,0:T(8,128)(2,1)} %feat_hbm.1), channel_id=1, source_target_pairs={{0,3},{1,2},{2,1},{3,0},{4,7},{5,6},{6,5},{7,4},{8,11},{9,10},{10,... | collective-permute-start | bytes 393224 | tf_op jit(solution)/shard_map/ppermute | solution.py:42
  3.8 0.0 collective-permute-start.1
  3.8 1.1 %copy-done = bf16[1,1,8,3,128,128]{5,4,3,2,1,0:T(8,128)(2,1)S(1)} copy-done((bf16[1,1,8,3,128,128]{5,4,3,2,1,0:T(8,128)(2,1)S(1)}, bf16[1,1,8,3,128,128]{5,4,3,2,1,0:T(8,128)(2,1)}, u32[]{:S(2)}) %copy-start) | copy-done | bytes 786456
  4.9 0.9 %copy-done.1 = bf16[256,256]{1,0:T(8,128)(2,1)S(1)} copy-done((bf16[256,256]{1,0:T(8,128)(2,1)S(1)}, bf16[256,256]{1,0:T(8,128)(2,1)}, u32[]{:S(2)}) %copy-start.1) | copy-done | bytes 131096
  5.8 0.7 copy-done.4
  6.5 0.7 copy-done.5
  7.2 0.7 copy-done.7
  7.9 2.3 %shard_map.111 = (bf16[8,3,128,256]{3,2,1,0:T(8,128)(2,1)S(1)}, bf16[2,256,128]{2,1,0:T(8,128)(2,1)S(1)}, s32[24]{0:T(128)S(1)}) custom-call(s32[1,3,1,8]{3,2,1,0:T(1,128)S(1)} %bitcast.8, s32[1,3,1,8]{3,2,1,0:T(1,128)S(1)} %bitcast.9, s32[1,1,8]{2,1,0:T(1,128)S(1)} %copy-done.7, bf16[256,256]{1,0:T(8,128)(2,1)S(1)} %copy-done.1, ...), custom_call_target="tpu_custom_call" | custom-call | flops 201326592 | bytes 2000000 | tf_op jit(solution)/shard_map/pallas_call | solution.py:212
  10.1 0.1 pad_add_fusion.place_ref
  10.2 0.0 collective-permute-done.refs_1_
  10.2 0.0 collective-permute-done.2.refs_3_
  10.2 0.6 collective-permute-done.1.refs_2_
  10.8 1.2 %shard_map.112 = (bf16[256,256]{1,0:T(8,128)(2,1)S(1)}, bf16[256,256]{1,0:T(8,128)(2,1)S(1)}, bf16[256,256]{1,0:T(8,128)(2,1)S(1)}, bf16[256,256]{1,0:T(8,128)(2,1)S(1)}, bf16[8,256,128]{2,1,0:T(8,128)(2,1)S(1)}) custom-call(s32[2]{0:T(128)S(1)} %pad_add_fusion.place_ref, s32[24]{0:T(128)S(1)} %get-tuple-element.31.code_ref, ...), custom_call_target="tpu_custom_call" | custom-call | flops 201326592 | bytes 2000000 | tf_op jit(solution)/shard_map/pallas_call | solution.py:235
  12.1 1.8 %collective-permute-start.7 = (bf16[256,256]{1,0:T(8,128)(2,1)S(1)}, bf16[256,256]{1,0:T(8,128)(2,1)S(1)}, u32[]{:S(2)}, u32[]{:S(2)}) collective-permute-start(bf16[256,256]{1,0:T(8,128)(2,1)S(1)} %get-tuple-element.42), channel_id=1, source_target_pairs={{0,4},{4,0},{8,12},{12,8},{16,20},{20,16},{24,28},{28,24},{1,5},{5... | collective-permute-start | bytes 393224 | tf_op jit(solution)/shard_map/ppermute | solution.py:42
  13.9 0.3 collective-permute-start.4
  14.2 1.1 %shard_map.113 = (bf16[256,256]{1,0:T(8,128)(2,1)S(1)}, bf16[256,256]{1,0:T(8,128)(2,1)S(1)}, bf16[256,256]{1,0:T(8,128)(2,1)S(1)}, bf16[256,256]{1,0:T(8,128)(2,1)S(1)}) custom-call(s32[2]{0:T(128)S(1)} %pad_add_fusion.place_ref, s32[24]{0:T(128)S(1)} %get-tuple-element.31.code_ref, bf16[8,256,128]{2,1,0:T(8,128)(2,1)S(1)} %get-tuple-element.34.turned, ...), custom_call_target="tpu_custom_call" | custom-call | flops 201326592 | bytes 2000000 | tf_op jit(solution)/shard_map/pallas_call | solution.py:242
  15.3 1.8 %collective-permute-start.6 = (bf16[256,256]{1,0:T(8,128)(2,1)S(1)}, bf16[256,256]{1,0:T(8,128)(2,1)S(1)}, u32[]{:S(2)}, u32[]{:S(2)}) collective-permute-start(bf16[256,256]{1,0:T(8,128)(2,1)S(1)} %get-tuple-element.40), channel_id=1, source_target_pairs={{0,4},{4,0},{8,12},{12,8},{16,20},{20,16},{24,28},{28,24},{1,5},{5... | collective-permute-start | bytes 393224 | tf_op jit(solution)/shard_map/ppermute | solution.py:42
  17.1 1.4 %collective-permute-done.7.refs_1_ = bf16[256,256]{1,0:T(8,128)(2,1)S(1)} collective-permute-done((bf16[256,256]{1,0:T(8,128)(2,1)S(1)}, bf16[256,256]{1,0:T(8,128)(2,1)S(1)}, u32[]{:S(2)}, u32[]{:S(2)}) %collective-permute-start.7) | collective-permute-done | bytes 131104 | tf_op jit(solution)/shard_map/ppermute | solution.py:42
  18.6 1.9 %collective-permute-start.8 = (bf16[256,256]{1,0:T(8,128)(2,1)S(1)}, bf16[256,256]{1,0:T(8,128)(2,1)S(1)}, u32[]{:S(2)}, u32[]{:S(2)}) collective-permute-start(bf16[256,256]{1,0:T(8,128)(2,1)S(1)} %shard_map.115), channel_id=1, source_target_pairs={{0,8},{4,12},{8,0},{12,4},{16,24},{20,28},{24,16},{28,20},{1,9},{5... | collective-permute-start | bytes 393224 | tf_op jit(solution)/shard_map/ppermute | solution.py:42
  20.5 1.5 %collective-permute-start.3 = (bf16[256,256]{1,0:T(8,128)(2,1)S(1)}, bf16[256,256]{1,0:T(8,128)(2,1)S(1)}, u32[]{:S(2)}, u32[]{:S(2)}) collective-permute-start(bf16[256,256]{1,0:T(8,128)(2,1)S(1)} %get-tuple-element.36), channel_id=1, source_target_pairs={{0,4},{4,0},{8,12},{12,8},{16,20},{20,16},{24,28},{28,24},{1,5},{5... | collective-permute-start | bytes 393224 | tf_op jit(solution)/shard_map/ppermute | solution.py:42
  22.0 0.0 collective-permute-done.4.refs_1_
  22.0 1.3 %collective-permute-start.5 = (bf16[256,256]{1,0:T(8,128)(2,1)S(1)}, bf16[256,256]{1,0:T(8,128)(2,1)S(1)}, u32[]{:S(2)}, u32[]{:S(2)}) collective-permute-start(bf16[256,256]{1,0:T(8,128)(2,1)S(1)} %shard_map.114), channel_id=1, source_target_pairs={{0,8},{4,12},{8,0},{12,4},{16,24},{20,28},{24,16},{28,20},{1,9},{5... | collective-permute-start | bytes 393224 | tf_op jit(solution)/shard_map/ppermute | solution.py:42
  23.3 0.9 %collective-permute-done.6.refs_1_ = bf16[256,256]{1,0:T(8,128)(2,1)S(1)} collective-permute-done((bf16[256,256]{1,0:T(8,128)(2,1)S(1)}, bf16[256,256]{1,0:T(8,128)(2,1)S(1)}, u32[]{:S(2)}, u32[]{:S(2)}) %collective-permute-start.6) | collective-permute-done | bytes 131104 | tf_op jit(solution)/shard_map/ppermute | solution.py:42
  24.1 0.5 collective-permute-done.8.refs_2_
  24.7 0.1 shard_map.116
  24.7 2.3 %collective-permute-start.9 = (bf16[256,256]{1,0:T(8,128)(2,1)S(1)}, bf16[256,256]{1,0:T(8,128)(2,1)S(1)}, u32[]{:S(2)}, u32[]{:S(2)}) collective-permute-start(bf16[256,256]{1,0:T(8,128)(2,1)S(1)} %shard_map.116), channel_id=1, source_target_pairs={{0,16},{4,20},{8,24},{12,28},{16,0},{20,4},{24,8},{28,12},{1,17},{... | collective-permute-start | bytes 393224 | tf_op jit(solution)/shard_map/ppermute | solution.py:42
  27.0 0.0 collective-permute-done.3.refs_1_
  27.0 0.7 collective-permute-done.5.refs_2_
  27.8 4.3 %collective-permute-done.9.refs_3_ = bf16[256,256]{1,0:T(8,128)(2,1)S(1)} collective-permute-done((bf16[256,256]{1,0:T(8,128)(2,1)S(1)}, bf16[256,256]{1,0:T(8,128)(2,1)S(1)}, u32[]{:S(2)}, u32[]{:S(2)}) %collective-permute-start.9) | collective-permute-done | bytes 131104 | tf_op jit(solution)/shard_map/ppermute | solution.py:42
  32.1 1.2 %shard_map.117 = (bf16[256,256]{1,0:T(8,128)(2,1)S(1)}, f32[256,256]{1,0:T(8,128)S(1)}, bf16[80,256]{1,0:T(8,128)(2,1)S(1)}, bf16[80,256]{1,0:T(8,128)(2,1)S(1)}...) custom-call(s32[2]{0:T(128)S(1)} %pad_add_fusion.place_ref, bf16[256,256]{1,0:T(8,128)(2,1)S(1)} %get-tuple-element.35.refs_0_, ...), custom_call_target="tpu_custom_call" | custom-call | flops 134217728 | bytes 2000000 | tf_op jit(solution)/shard_map/pallas_call | solution.py:262
  33.3 1.0 %collective-permute-start.13 = (bf16[256,256]{1,0:T(8,128)(2,1)S(1)}, bf16[256,256]{1,0:T(8,128)(2,1)S(1)}, u32[]{:S(2)}, u32[]{:S(2)}) collective-permute-start(bf16[256,256]{1,0:T(8,128)(2,1)S(1)} %get-tuple-element.44.refs_0_), channel_id=1, source_target_pairs={{0,16},{4,20},{8,24},{12,28},{16,0},{20,4},{24,8},{28,12},{1,17},{... | collective-permute-start | bytes 393224 | tf_op jit(solution)/shard_map/ppermute | solution.py:42
  34.3 2.8 %collective-permute-start.11 = (bf16[256,256]{1,0:T(8,128)(2,1)S(1)}, bf16[256,256]{1,0:T(8,128)(2,1)S(1)}, u32[]{:S(2)}, u32[]{:S(2)}) collective-permute-start(bf16[256,256]{1,0:T(8,128)(2,1)S(1)} %get-tuple-element.44.refs_0_), channel_id=1, source_target_pairs={{0,8},{4,12},{8,0},{12,4},{16,24},{20,28},{24,16},{28,20},{1,9},{5... | collective-permute-start | bytes 393224 | tf_op jit(solution)/shard_map/ppermute | solution.py:42
  37.1 1.5 %collective-permute-start.10 = (bf16[256,256]{1,0:T(8,128)(2,1)S(1)}, bf16[256,256]{1,0:T(8,128)(2,1)S(1)}, u32[]{:S(2)}, u32[]{:S(2)}) collective-permute-start(bf16[256,256]{1,0:T(8,128)(2,1)S(1)} %get-tuple-element.44.refs_0_), channel_id=1, source_target_pairs={{0,4},{4,0},{8,12},{12,8},{16,20},{20,16},{24,28},{28,24},{1,5},{5... | collective-permute-start | bytes 393224 | tf_op jit(solution)/shard_map/ppermute | solution.py:42
  38.6 2.2 %collective-permute-done.13.refs_4_ = bf16[256,256]{1,0:T(8,128)(2,1)S(1)} collective-permute-done((bf16[256,256]{1,0:T(8,128)(2,1)S(1)}, bf16[256,256]{1,0:T(8,128)(2,1)S(1)}, u32[]{:S(2)}, u32[]{:S(2)}) %collective-permute-start.13) | collective-permute-done | bytes 131104 | tf_op jit(solution)/shard_map/ppermute | solution.py:42
  40.8 0.0 collective-permute-start.15
  40.8 1.2 %collective-permute-start.14 = (bf16[256,256]{1,0:T(8,128)(2,1)S(1)}, bf16[256,256]{1,0:T(8,128)(2,1)S(1)}, u32[]{:S(2)}, u32[]{:S(2)}) collective-permute-start(bf16[256,256]{1,0:T(8,128)(2,1)S(1)} %collective-permute-done.13.refs_4_), channel_id=1, source_target_pairs={{0,4},{4,0},{8,12},{12,8},{16,20},{20,16},{24,28},{28,24},{1,5},{5... | collective-permute-start | bytes 393224 | tf_op jit(solution)/shard_map/ppermute | solution.py:42
  41.9 0.3 collective-permute-done.11.refs_2_
  42.3 0.9 %collective-permute-start.12 = (bf16[256,256]{1,0:T(8,128)(2,1)S(1)}, bf16[256,256]{1,0:T(8,128)(2,1)S(1)}, u32[]{:S(2)}, u32[]{:S(2)}) collective-permute-start(bf16[256,256]{1,0:T(8,128)(2,1)S(1)} %collective-permute-done.11.refs_2_), channel_id=1, source_target_pairs={{0,4},{4,0},{8,12},{12,8},{16,20},{20,16},{24,28},{28,24},{1,5},{5... | collective-permute-start | bytes 393224 | tf_op jit(solution)/shard_map/ppermute | solution.py:42
  43.2 1.2 %collective-permute-done.16.refs_1_ = bf16[80,256]{1,0:T(8,128)(2,1)S(1)} collective-permute-done((bf16[80,256]{1,0:T(8,128)(2,1)S(1)}, bf16[80,256]{1,0:T(8,128)(2,1)S(1)}, u32[]{:S(2)}, u32[]{:S(2)}) %collective-permute-start.16) | collective-permute-done | bytes 40992 | tf_op jit(solution)/shard_map/ppermute | solution.py:42
  44.4 1.5 %collective-permute-start.17 = (bf16[80,256]{1,0:T(8,128)(2,1)S(1)}, bf16[80,256]{1,0:T(8,128)(2,1)S(1)}, u32[]{:S(2)}, u32[]{:S(2)}) collective-permute-start(bf16[80,256]{1,0:T(8,128)(2,1)S(1)} %get-tuple-element.47), channel_id=1, source_target_pairs={{0,2},{1,3},{2,0},{3,1},{4,6},{5,7},{6,4},{7,5},{8,10},{9,11},{10,... | collective-permute-start | bytes 122888 | tf_op jit(solution)/shard_map/ppermute | solution.py:42
  45.9 2.5 %collective-permute-done.17.refs_2_ = bf16[80,256]{1,0:T(8,128)(2,1)S(1)} collective-permute-done((bf16[80,256]{1,0:T(8,128)(2,1)S(1)}, bf16[80,256]{1,0:T(8,128)(2,1)S(1)}, u32[]{:S(2)}, u32[]{:S(2)}) %collective-permute-start.17) | collective-permute-done | bytes 40992 | tf_op jit(solution)/shard_map/ppermute | solution.py:42
  48.4 0.1 collective-permute-start.18
  48.5 3.7 %collective-permute-done.18.refs_3_ = bf16[80,256]{1,0:T(8,128)(2,1)S(1)} collective-permute-done((bf16[80,256]{1,0:T(8,128)(2,1)S(1)}, bf16[80,256]{1,0:T(8,128)(2,1)S(1)}, u32[]{:S(2)}, u32[]{:S(2)}) %collective-permute-start.18) | collective-permute-done | bytes 40992 | tf_op jit(solution)/shard_map/ppermute | solution.py:42
  52.3 0.0 collective-permute-done.10.refs_4_.refs_1_
  52.3 0.9 %collective-permute-start.19 = (bf16[336,256]{1,0:T(8,128)(2,1)S(1)}, bf16[336,256]{1,0:T(8,128)(2,1)S(1)}, u32[]{:S(2)}, u32[]{:S(2)}) collective-permute-start(bf16[336,256]{1,0:T(8,128)(2,1)S(1)} %get-tuple-element.49), channel_id=1, source_target_pairs={{0,4},{4,0},{8,12},{12,8},{16,20},{20,16},{24,28},{28,24},{1,5},{5... | collective-permute-start | bytes 516104 | tf_op jit(solution)/shard_map/ppermute | solution.py:42
  53.2 5.6 %collective-permute-done.19.packed_ref.refs_7_ = bf16[336,256]{1,0:T(8,128)(2,1)S(1)} collective-permute-done((bf16[336,256]{1,0:T(8,128)(2,1)S(1)}, bf16[336,256]{1,0:T(8,128)(2,1)S(1)}, u32[]{:S(2)}, u32[]{:S(2)}) %collective-permute-start.19) | collective-permute-done | bytes 172064 | tf_op jit(solution)/shard_map/ppermute | solution.py:42
  58.8 1.3 %shard_map.121 = (bf16[256,256]{1,0:T(8,128)(2,1)S(1)}, bf16[256,256]{1,0:T(8,128)(2,1)S(1)}, bf16[256,256]{1,0:T(8,128)(2,1)S(1)}, bf16[256,256]{1,0:T(8,128)(2,1)S(1)}) custom-call(s32[2]{0:T(128)S(1)} %pad_add_fusion.place_ref, s32[24]{0:T(128)S(1)} %get-tuple-element.31.code_ref, bf16[256,256]{1,0:T(8,128)(2,1)S(1)} %get-tuple-element.44.refs_0_, ...), custom_call_target="tpu_custom_call" | custom-call | flops 201326592 | bytes 2000000 | tf_op jit(solution)/shard_map/pallas_call | solution.py:293
  60.1 0.1 collective-permute-start.20
  60.2 0.5 collective-permute-start.22
  60.7 0.8 %collective-permute-done.20.refs_1_ = bf16[256,256]{1,0:T(8,128)(2,1)S(1)} collective-permute-done((bf16[256,256]{1,0:T(8,128)(2,1)S(1)}, bf16[256,256]{1,0:T(8,128)(2,1)S(1)}, u32[]{:S(2)}, u32[]{:S(2)}) %collective-permute-start.20) | collective-permute-done | bytes 131104 | tf_op jit(solution)/shard_map/ppermute | solution.py:42
  61.6 0.2 collective-permute-start.21
  61.7 1.8 %collective-permute-start.25 = (bf16[80,256]{1,0:T(8,128)(2,1)S(1)}, bf16[80,256]{1,0:T(8,128)(2,1)S(1)}, u32[]{:S(2)}, u32[]{:S(2)}) collective-permute-start(bf16[80,256]{1,0:T(8,128)(2,1)S(1)} %shard_map.120.refs_9_.refs_0_), channel_id=1, source_target_pairs={{0,24},{4,28},{8,16},{12,20},{16,8},{20,12},{24,0},{28,4},{1,25},{... | collective-permute-start | bytes 122888 | tf_op jit(solution)/shard_map/ppermute | solution.py:42
  63.5 1.1 %collective-permute-start.24 = (bf16[80,256]{1,0:T(8,128)(2,1)S(1)}, bf16[80,256]{1,0:T(8,128)(2,1)S(1)}, u32[]{:S(2)}, u32[]{:S(2)}) collective-permute-start(bf16[80,256]{1,0:T(8,128)(2,1)S(1)} %shard_map.120.refs_9_.refs_0_), channel_id=1, source_target_pairs={{0,16},{4,20},{8,24},{12,28},{16,0},{20,4},{24,8},{28,12},{1,17},{... | collective-permute-start | bytes 122888 | tf_op jit(solution)/shard_map/ppermute | solution.py:42
  64.6 1.5 %collective-permute-start.23 = (bf16[80,256]{1,0:T(8,128)(2,1)S(1)}, bf16[80,256]{1,0:T(8,128)(2,1)S(1)}, u32[]{:S(2)}, u32[]{:S(2)}) collective-permute-start(bf16[80,256]{1,0:T(8,128)(2,1)S(1)} %shard_map.120.refs_9_.refs_0_), channel_id=1, source_target_pairs={{0,8},{4,12},{8,0},{12,4},{16,24},{20,28},{24,16},{28,20},{1,9},{5... | collective-permute-start | bytes 122888 | tf_op jit(solution)/shard_map/ppermute | solution.py:42
  66.1 1.7 %collective-permute-done.25.refs_3_ = bf16[80,256]{1,0:T(8,128)(2,1)S(1)} collective-permute-done((bf16[80,256]{1,0:T(8,128)(2,1)S(1)}, bf16[80,256]{1,0:T(8,128)(2,1)S(1)}, u32[]{:S(2)}, u32[]{:S(2)}) %collective-permute-start.25) | collective-permute-done | bytes 40992 | tf_op jit(solution)/shard_map/ppermute | solution.py:42
  67.8 1.4 %collective-permute-done.24.refs_2_ = bf16[80,256]{1,0:T(8,128)(2,1)S(1)} collective-permute-done((bf16[80,256]{1,0:T(8,128)(2,1)S(1)}, bf16[80,256]{1,0:T(8,128)(2,1)S(1)}, u32[]{:S(2)}, u32[]{:S(2)}) %collective-permute-start.24) | collective-permute-done | bytes 40992 | tf_op jit(solution)/shard_map/ppermute | solution.py:42
  69.3 0.2 collective-permute-start.28
  69.4 1.5 %collective-permute-start.27 = (bf16[64,256]{1,0:T(8,128)(2,1)S(1)}, bf16[64,256]{1,0:T(8,128)(2,1)S(1)}, u32[]{:S(2)}, u32[]{:S(2)}) collective-permute-start(bf16[64,256]{1,0:T(8,128)(2,1)S(1)} %slice.8.refs_3_), channel_id=1, source_target_pairs={{0,2},{1,3},{2,0},{3,1},{4,6},{5,7},{6,4},{7,5},{8,10},{9,11},{10,... | collective-permute-start | bytes 98312 | tf_op jit(solution)/shard_map/ppermute | solution.py:42
  70.9 0.3 collective-permute-start.26
  71.2 0.7 shard_map.118
  72.0 1.1 %collective-permute-done.28.refs_6_ = bf16[64,256]{1,0:T(8,128)(2,1)S(1)} collective-permute-done((bf16[64,256]{1,0:T(8,128)(2,1)S(1)}, bf16[64,256]{1,0:T(8,128)(2,1)S(1)}, u32[]{:S(2)}, u32[]{:S(2)}) %collective-permute-start.28) | collective-permute-done | bytes 32800 | tf_op jit(solution)/shard_map/ppermute | solution.py:42
  73.0 0.4 collective-permute-done.27.refs_5_
  73.4 1.3 %shard_map.124 = (bf16[256,256]{1,0:T(8,128)(2,1)}, f32[256,256]{1,0:T(8,128)}, f32[1,256]{1,0:T(1,128)}) custom-call(s32[2]{0:T(128)S(1)} %pad_add_fusion.place_ref, bf16[256,256]{1,0:T(8,128)(2,1)S(1)} %get-tuple-element.51.refs_0_, bf16[256,256]{1,0:T(8,128)(2,1)S(1)} %collective-permute-done.21.refs_1_, ...), custom_call_target="tpu_custom_call" | custom-call | bytes 2000000 | tf_op jit(solution)/shard_map/pallas_call | solution.py:312
  (27 shorter events, 0.2 us)
Async XLA Ops:
  0.6 9.6 %collective-permute-start = (bf16[256,256]{1,0:T(8,128)(2,1)}, bf16[256,256]{1,0:T(8,128)(2,1)S(1)}, u32[]{:S(2)}, u32[]{:S(2)}) collective-permute-start(bf16[256,256]{1,0:T(8,128)(2,1)} %feat_hbm.1), channel_id=1, source_target_pairs={{0,1},{1,0},{2,3},{3,2},{4,5},{5,4},{6,7},{7,6},{8,9},{9,8},{10,11... | collective-permute-start | bytes 393224 | tf_op jit(solution)/shard_map/ppermute | solution.py:42
  1.1 9.1 %collective-permute-start.2 = (bf16[256,256]{1,0:T(8,128)(2,1)}, bf16[256,256]{1,0:T(8,128)(2,1)S(1)}, u32[]{:S(2)}, u32[]{:S(2)}) collective-permute-start(bf16[256,256]{1,0:T(8,128)(2,1)} %feat_hbm.1), channel_id=1, source_target_pairs={{0,3},{1,2},{2,1},{3,0},{4,7},{5,6},{6,5},{7,4},{8,11},{9,10},{10,... | collective-permute-start | bytes 393224 | tf_op jit(solution)/shard_map/ppermute | solution.py:42
  3.8 7.1 %collective-permute-start.1 = (bf16[256,256]{1,0:T(8,128)(2,1)}, bf16[256,256]{1,0:T(8,128)(2,1)S(1)}, u32[]{:S(2)}, u32[]{:S(2)}) collective-permute-start(bf16[256,256]{1,0:T(8,128)(2,1)} %feat_hbm.1), channel_id=1, source_target_pairs={{0,2},{1,3},{2,0},{3,1},{4,6},{5,7},{6,4},{7,5},{8,10},{9,11},{10,... | collective-permute-start | bytes 393224 | tf_op jit(solution)/shard_map/ppermute | solution.py:42
  3.8 1.1 %copy-start = (bf16[1,1,8,3,128,128]{5,4,3,2,1,0:T(8,128)(2,1)S(1)}, bf16[1,1,8,3,128,128]{5,4,3,2,1,0:T(8,128)(2,1)}, u32[]{:S(2)}) copy-start(bf16[1,1,8,3,128,128]{5,4,3,2,1,0:T(8,128)(2,1)} %param.11) | copy-start | bytes 2359300
  4.9 0.9 %copy-start.1 = (bf16[256,256]{1,0:T(8,128)(2,1)S(1)}, bf16[256,256]{1,0:T(8,128)(2,1)}, u32[]{:S(2)}) copy-start(bf16[256,256]{1,0:T(8,128)(2,1)} %feat_hbm.1) | copy-start | bytes 393220
  5.8 0.7 copy-start.4
  6.5 0.7 copy-start.5
  7.2 0.7 copy-start.7
  12.1 6.5 %collective-permute-start.7 = (bf16[256,256]{1,0:T(8,128)(2,1)S(1)}, bf16[256,256]{1,0:T(8,128)(2,1)S(1)}, u32[]{:S(2)}, u32[]{:S(2)}) collective-permute-start(bf16[256,256]{1,0:T(8,128)(2,1)S(1)} %get-tuple-element.42), channel_id=1, source_target_pairs={{0,4},{4,0},{8,12},{12,8},{16,20},{20,16},{24,28},{28,24},{1,5},{5... | collective-permute-start | bytes 393224 | tf_op jit(solution)/shard_map/ppermute | solution.py:42
  13.9 8.1 %collective-permute-start.4 = (bf16[256,256]{1,0:T(8,128)(2,1)S(1)}, bf16[256,256]{1,0:T(8,128)(2,1)S(1)}, u32[]{:S(2)}, u32[]{:S(2)}) collective-permute-start(bf16[256,256]{1,0:T(8,128)(2,1)S(1)} %get-tuple-element.38), channel_id=1, source_target_pairs={{0,4},{4,0},{8,12},{12,8},{16,20},{20,16},{24,28},{28,24},{1,5},{5... | collective-permute-start | bytes 393224 | tf_op jit(solution)/shard_map/ppermute | solution.py:42
  14.2 17.9 %copy-start.2 = (bf16[256,256]{1,0:T(8,128)(2,1)S(1)}, bf16[256,256]{1,0:T(8,128)(2,1)}, u32[]{:S(2)}) copy-start(bf16[256,256]{1,0:T(8,128)(2,1)} %refs_4_.1) | copy-start | bytes 393220
  14.2 17.9 %copy-start.3 = (bf16[256,256]{1,0:T(8,128)(2,1)S(1)}, bf16[256,256]{1,0:T(8,128)(2,1)}, u32[]{:S(2)}) copy-start(bf16[256,256]{1,0:T(8,128)(2,1)} %refs_6_.1) | copy-start | bytes 393220
  14.2 17.9 %copy-start.6 = (f32[256]{0:T(256)S(1)}, f32[256]{0:T(256)}, u32[]{:S(2)}) copy-start(f32[256]{0:T(256)} %param.10) | copy-start | bytes 3076
  15.3 8.9 %collective-permute-start.6 = (bf16[256,256]{1,0:T(8,128)(2,1)S(1)}, bf16[256,256]{1,0:T(8,128)(2,1)S(1)}, u32[]{:S(2)}, u32[]{:S(2)}) collective-permute-start(bf16[256,256]{1,0:T(8,128)(2,1)S(1)} %get-tuple-element.40), channel_id=1, source_target_pairs={{0,4},{4,0},{8,12},{12,8},{16,20},{20,16},{24,28},{28,24},{1,5},{5... | collective-permute-start | bytes 393224 | tf_op jit(solution)/shard_map/ppermute | solution.py:42
  18.6 6.1 %collective-permute-start.8 = (bf16[256,256]{1,0:T(8,128)(2,1)S(1)}, bf16[256,256]{1,0:T(8,128)(2,1)S(1)}, u32[]{:S(2)}, u32[]{:S(2)}) collective-permute-start(bf16[256,256]{1,0:T(8,128)(2,1)S(1)} %shard_map.115), channel_id=1, source_target_pairs={{0,8},{4,12},{8,0},{12,4},{16,24},{20,28},{24,16},{28,20},{1,9},{5... | collective-permute-start | bytes 393224 | tf_op jit(solution)/shard_map/ppermute | solution.py:42
  20.5 6.6 %collective-permute-start.3 = (bf16[256,256]{1,0:T(8,128)(2,1)S(1)}, bf16[256,256]{1,0:T(8,128)(2,1)S(1)}, u32[]{:S(2)}, u32[]{:S(2)}) collective-permute-start(bf16[256,256]{1,0:T(8,128)(2,1)S(1)} %get-tuple-element.36), channel_id=1, source_target_pairs={{0,4},{4,0},{8,12},{12,8},{16,20},{20,16},{24,28},{28,24},{1,5},{5... | collective-permute-start | bytes 393224 | tf_op jit(solution)/shard_map/ppermute | solution.py:42
  22.0 5.7 %collective-permute-start.5 = (bf16[256,256]{1,0:T(8,128)(2,1)S(1)}, bf16[256,256]{1,0:T(8,128)(2,1)S(1)}, u32[]{:S(2)}, u32[]{:S(2)}) collective-permute-start(bf16[256,256]{1,0:T(8,128)(2,1)S(1)} %shard_map.114), channel_id=1, source_target_pairs={{0,8},{4,12},{8,0},{12,4},{16,24},{20,28},{24,16},{28,20},{1,9},{5... | collective-permute-start | bytes 393224 | tf_op jit(solution)/shard_map/ppermute | solution.py:42
  24.7 7.3 %collective-permute-start.9 = (bf16[256,256]{1,0:T(8,128)(2,1)S(1)}, bf16[256,256]{1,0:T(8,128)(2,1)S(1)}, u32[]{:S(2)}, u32[]{:S(2)}) collective-permute-start(bf16[256,256]{1,0:T(8,128)(2,1)S(1)} %shard_map.116), channel_id=1, source_target_pairs={{0,16},{4,20},{8,24},{12,28},{16,0},{20,4},{24,8},{28,12},{1,17},{... | collective-permute-start | bytes 393224 | tf_op jit(solution)/shard_map/ppermute | solution.py:42
  33.3 7.4 %collective-permute-start.13 = (bf16[256,256]{1,0:T(8,128)(2,1)S(1)}, bf16[256,256]{1,0:T(8,128)(2,1)S(1)}, u32[]{:S(2)}, u32[]{:S(2)}) collective-permute-start(bf16[256,256]{1,0:T(8,128)(2,1)S(1)} %get-tuple-element.44.refs_0_), channel_id=1, source_target_pairs={{0,16},{4,20},{8,24},{12,28},{16,0},{20,4},{24,8},{28,12},{1,17},{... | collective-permute-start | bytes 393224 | tf_op jit(solution)/shard_map/ppermute | solution.py:42
  34.3 8.0 %collective-permute-start.11 = (bf16[256,256]{1,0:T(8,128)(2,1)S(1)}, bf16[256,256]{1,0:T(8,128)(2,1)S(1)}, u32[]{:S(2)}, u32[]{:S(2)}) collective-permute-start(bf16[256,256]{1,0:T(8,128)(2,1)S(1)} %get-tuple-element.44.refs_0_), channel_id=1, source_target_pairs={{0,8},{4,12},{8,0},{12,4},{16,24},{20,28},{24,16},{28,20},{1,9},{5... | collective-permute-start | bytes 393224 | tf_op jit(solution)/shard_map/ppermute | solution.py:42
  37.1 15.2 %collective-permute-start.10 = (bf16[256,256]{1,0:T(8,128)(2,1)S(1)}, bf16[256,256]{1,0:T(8,128)(2,1)S(1)}, u32[]{:S(2)}, u32[]{:S(2)}) collective-permute-start(bf16[256,256]{1,0:T(8,128)(2,1)S(1)} %get-tuple-element.44.refs_0_), channel_id=1, source_target_pairs={{0,4},{4,0},{8,12},{12,8},{16,20},{20,16},{24,28},{28,24},{1,5},{5... | collective-permute-start | bytes 393224 | tf_op jit(solution)/shard_map/ppermute | solution.py:42
  40.8 11.5 %collective-permute-start.15 = (bf16[256,256]{1,0:T(8,128)(2,1)S(1)}, bf16[256,256]{1,0:T(8,128)(2,1)S(1)}, u32[]{:S(2)}, u32[]{:S(2)}) collective-permute-start(bf16[256,256]{1,0:T(8,128)(2,1)S(1)} %collective-permute-done.13.refs_4_), channel_id=1, source_target_pairs={{0,8},{4,12},{8,0},{12,4},{16,24},{20,28},{24,16},{28,20},{1,9},{5... | collective-permute-start | bytes 393224 | tf_op jit(solution)/shard_map/ppermute | solution.py:42
  40.8 11.5 %collective-permute-start.14 = (bf16[256,256]{1,0:T(8,128)(2,1)S(1)}, bf16[256,256]{1,0:T(8,128)(2,1)S(1)}, u32[]{:S(2)}, u32[]{:S(2)}) collective-permute-start(bf16[256,256]{1,0:T(8,128)(2,1)S(1)} %collective-permute-done.13.refs_4_), channel_id=1, source_target_pairs={{0,4},{4,0},{8,12},{12,8},{16,20},{20,16},{24,28},{28,24},{1,5},{5... | collective-permute-start | bytes 393224 | tf_op jit(solution)/shard_map/ppermute | solution.py:42
  42.3 10.0 %collective-permute-start.12 = (bf16[256,256]{1,0:T(8,128)(2,1)S(1)}, bf16[256,256]{1,0:T(8,128)(2,1)S(1)}, u32[]{:S(2)}, u32[]{:S(2)}) collective-permute-start(bf16[256,256]{1,0:T(8,128)(2,1)S(1)} %collective-permute-done.11.refs_2_), channel_id=1, source_target_pairs={{0,4},{4,0},{8,12},{12,8},{16,20},{20,16},{24,28},{28,24},{1,5},{5... | collective-permute-start | bytes 393224 | tf_op jit(solution)/shard_map/ppermute | solution.py:42
  43.2 1.2 %collective-permute-start.16 = (bf16[80,256]{1,0:T(8,128)(2,1)S(1)}, bf16[80,256]{1,0:T(8,128)(2,1)S(1)}, u32[]{:S(2)}, u32[]{:S(2)}) collective-permute-start(bf16[80,256]{1,0:T(8,128)(2,1)S(1)} %get-tuple-element.46), channel_id=1, source_target_pairs={{0,1},{1,0},{2,3},{3,2},{4,5},{5,4},{6,7},{7,6},{8,9},{9,8},{10,11... | collective-permute-start | bytes 122888 | tf_op jit(solution)/shard_map/ppermute | solution.py:42
  44.4 4.0 %collective-permute-start.17 = (bf16[80,256]{1,0:T(8,128)(2,1)S(1)}, bf16[80,256]{1,0:T(8,128)(2,1)S(1)}, u32[]{:S(2)}, u32[]{:S(2)}) collective-permute-start(bf16[80,256]{1,0:T(8,128)(2,1)S(1)} %get-tuple-element.47), channel_id=1, source_target_pairs={{0,2},{1,3},{2,0},{3,1},{4,6},{5,7},{6,4},{7,5},{8,10},{9,11},{10,... | collective-permute-start | bytes 122888 | tf_op jit(solution)/shard_map/ppermute | solution.py:42
  48.4 3.8 %collective-permute-start.18 = (bf16[80,256]{1,0:T(8,128)(2,1)S(1)}, bf16[80,256]{1,0:T(8,128)(2,1)S(1)}, u32[]{:S(2)}, u32[]{:S(2)}) collective-permute-start(bf16[80,256]{1,0:T(8,128)(2,1)S(1)} %get-tuple-element.48), channel_id=1, source_target_pairs={{0,3},{1,2},{2,1},{3,0},{4,7},{5,6},{6,5},{7,4},{8,11},{9,10},{10,... | collective-permute-start | bytes 122888 | tf_op jit(solution)/shard_map/ppermute | solution.py:42
  52.3 6.5 %collective-permute-start.19 = (bf16[336,256]{1,0:T(8,128)(2,1)S(1)}, bf16[336,256]{1,0:T(8,128)(2,1)S(1)}, u32[]{:S(2)}, u32[]{:S(2)}) collective-permute-start(bf16[336,256]{1,0:T(8,128)(2,1)S(1)} %get-tuple-element.49), channel_id=1, source_target_pairs={{0,4},{4,0},{8,12},{12,8},{16,20},{20,16},{24,28},{28,24},{1,5},{5... | collective-permute-start | bytes 516104 | tf_op jit(solution)/shard_map/ppermute | solution.py:42
  60.1 1.4 %collective-permute-start.20 = (bf16[256,256]{1,0:T(8,128)(2,1)S(1)}, bf16[256,256]{1,0:T(8,128)(2,1)S(1)}, u32[]{:S(2)}, u32[]{:S(2)}) collective-permute-start(bf16[256,256]{1,0:T(8,128)(2,1)S(1)} %get-tuple-element.53), channel_id=1, source_target_pairs={{0,1},{1,0},{2,3},{3,2},{4,5},{5,4},{6,7},{7,6},{8,9},{9,8},{10,11... | collective-permute-start | bytes 393224 | tf_op jit(solution)/shard_map/ppermute | solution.py:42
  60.2 13.2 %collective-permute-start.22 = (bf16[256,256]{1,0:T(8,128)(2,1)S(1)}, bf16[256,256]{1,0:T(8,128)(2,1)S(1)}, u32[]{:S(2)}, u32[]{:S(2)}) collective-permute-start(bf16[256,256]{1,0:T(8,128)(2,1)S(1)} %get-tuple-element.54), channel_id=1, source_target_pairs={{0,1},{1,0},{2,3},{3,2},{4,5},{5,4},{6,7},{7,6},{8,9},{9,8},{10,11... | collective-permute-start | bytes 393224 | tf_op jit(solution)/shard_map/ppermute | solution.py:42
  61.6 11.8 %collective-permute-start.21 = (bf16[256,256]{1,0:T(8,128)(2,1)S(1)}, bf16[256,256]{1,0:T(8,128)(2,1)S(1)}, u32[]{:S(2)}, u32[]{:S(2)}) collective-permute-start(bf16[256,256]{1,0:T(8,128)(2,1)S(1)} %shard_map.122), channel_id=1, source_target_pairs={{0,2},{1,3},{2,0},{3,1},{4,6},{5,7},{6,4},{7,5},{8,10},{9,11},{10,... | collective-permute-start | bytes 393224 | tf_op jit(solution)/shard_map/ppermute | solution.py:42
  61.7 6.1 %collective-permute-start.25 = (bf16[80,256]{1,0:T(8,128)(2,1)S(1)}, bf16[80,256]{1,0:T(8,128)(2,1)S(1)}, u32[]{:S(2)}, u32[]{:S(2)}) collective-permute-start(bf16[80,256]{1,0:T(8,128)(2,1)S(1)} %shard_map.120.refs_9_.refs_0_), channel_id=1, source_target_pairs={{0,24},{4,28},{8,16},{12,20},{16,8},{20,12},{24,0},{28,4},{1,25},{... | collective-permute-start | bytes 122888 | tf_op jit(solution)/shard_map/ppermute | solution.py:42
  63.5 5.7 %collective-permute-start.24 = (bf16[80,256]{1,0:T(8,128)(2,1)S(1)}, bf16[80,256]{1,0:T(8,128)(2,1)S(1)}, u32[]{:S(2)}, u32[]{:S(2)}) collective-permute-start(bf16[80,256]{1,0:T(8,128)(2,1)S(1)} %shard_map.120.refs_9_.refs_0_), channel_id=1, source_target_pairs={{0,16},{4,20},{8,24},{12,28},{16,0},{20,4},{24,8},{28,12},{1,17},{... | collective-permute-start | bytes 122888 | tf_op jit(solution)/shard_map/ppermute | solution.py:42
  64.6 4.6 %collective-permute-start.23 = (bf16[80,256]{1,0:T(8,128)(2,1)S(1)}, bf16[80,256]{1,0:T(8,128)(2,1)S(1)}, u32[]{:S(2)}, u32[]{:S(2)}) collective-permute-start(bf16[80,256]{1,0:T(8,128)(2,1)S(1)} %shard_map.120.refs_9_.refs_0_), channel_id=1, source_target_pairs={{0,8},{4,12},{8,0},{12,4},{16,24},{20,28},{24,16},{28,20},{1,9},{5... | collective-permute-start | bytes 122888 | tf_op jit(solution)/shard_map/ppermute | solution.py:42
  69.3 3.7 %collective-permute-start.28 = (bf16[64,256]{1,0:T(8,128)(2,1)S(1)}, bf16[64,256]{1,0:T(8,128)(2,1)S(1)}, u32[]{:S(2)}, u32[]{:S(2)}) collective-permute-start(bf16[64,256]{1,0:T(8,128)(2,1)S(1)} %slice.8.refs_3_), channel_id=1, source_target_pairs={{0,3},{1,2},{2,1},{3,0},{4,7},{5,6},{6,5},{7,4},{8,11},{9,10},{10,... | collective-permute-start | bytes 98312 | tf_op jit(solution)/shard_map/ppermute | solution.py:42
  69.4 3.9 %collective-permute-start.27 = (bf16[64,256]{1,0:T(8,128)(2,1)S(1)}, bf16[64,256]{1,0:T(8,128)(2,1)S(1)}, u32[]{:S(2)}, u32[]{:S(2)}) collective-permute-start(bf16[64,256]{1,0:T(8,128)(2,1)S(1)} %slice.8.refs_3_), channel_id=1, source_target_pairs={{0,2},{1,3},{2,0},{3,1},{4,6},{5,7},{6,4},{7,5},{8,10},{9,11},{10,... | collective-permute-start | bytes 98312 | tf_op jit(solution)/shard_map/ppermute | solution.py:42
  70.9 2.5 %collective-permute-start.26 = (bf16[64,256]{1,0:T(8,128)(2,1)S(1)}, bf16[64,256]{1,0:T(8,128)(2,1)S(1)}, u32[]{:S(2)}, u32[]{:S(2)}) collective-permute-start(bf16[64,256]{1,0:T(8,128)(2,1)S(1)} %slice.8.refs_3_), channel_id=1, source_target_pairs={{0,1},{1,0},{2,3},{3,2},{4,5},{5,4},{6,7},{7,6},{8,9},{9,8},{10,11... | collective-permute-start | bytes 98312 | tf_op jit(solution)/shard_map/ppermute | solution.py:42

commit v3 on v2

--- a/solution.py
+++ b/solution.py
@@ -43,30 +43,19 @@
 
 
 def prepare_kernel(
-    tiles, source_hbm, dest_hbm, count_hbm, feat_hbm, vals_hbm, picked_ref, own_ref, code_ref,
-    source_ref, dest_ref, count_ref, feat, vals, sems,
+    tiles, source_ref, dest_ref, count_ref, feat_ref, vals_ref, picked_ref, own_ref, code_ref
 ):
-    rows, slots, size, _ = vals.shape
-    small = [(source_hbm, source_ref), (dest_hbm, dest_ref), (count_hbm, count_ref), (feat_hbm, feat)]
-    copies = [pltpu.make_async_copy(x, y, sems.at[i]) for i, (x, y) in enumerate(small)]
-    copies += [
-        pltpu.make_async_copy(vals_hbm.at[o], vals.at[o], sems.at[len(small) + o]) for o in range(rows)
-    ]
-    for copy in copies:
-        copy.start()
-    for copy in copies[: len(small)]:
-        copy.wait()
+    rows, slots, size, _ = vals_ref.shape
     for o in range(rows):
         for s in range(slots):
             code_ref[o * slots + s] = source_ref[0, s, 0, o]
     for k in range(tiles):
-        own_ref[k] = feat[k * size : (k + 1) * size, :].T
+        own_ref[k] = feat_ref[k * size : (k + 1) * size, :].T
     for o in range(rows):
-        copies[len(small) + o].wait()
         for s in range(slots):
             live = s < count_ref[0, 0, o]
             dest = jnp.where(live, dest_ref[0, s, 0, o], tiles)
-            block = vals[o, s]
+            block = vals_ref[o, s]
             zero = jnp.zeros_like(block)
             for t in range(tiles):
                 picked_ref[o, s, :, t * size : (t + 1) * size] = jnp.where(dest == t, block, zero)
@@ -74,13 +63,10 @@
 
 def push_one(k, place_ref, code_ref, turned, picked_ref):
     owner = place_ref[0] ^ k
-    total = None
-    for s in range(picked_ref.shape[1]):
-        part = jnp.dot(
-            turned[code_ref[owner * picked_ref.shape[1] + s]], picked_ref[owner, s], preferred_element_type=F32
-        )
-        total = part if total is None else total + part
-    return total.astype(BF16)
+    _, slots, size, wide = picked_ref.shape
+    sources = jnp.concatenate([turned[code_ref[owner * slots + s]] for s in range(slots)], axis=1)
+    chosen = picked_ref[owner].reshape(slots * size, wide)
+    return jnp.dot(sources, chosen, preferred_element_type=F32).astype(BF16)
 
 
 def push_first_kernel(ks, tiles, place_ref, code_ref, *refs):
@@ -109,8 +95,7 @@
 
 def middle_kernel(n_parts, place_ref, *refs):
     parts = refs[:n_parts]
-    weight_ref, bias_ref, cot_ref, back_ref, pre_ref = refs[n_parts : n_parts + 5]
-    terms, wg = refs[n_parts + 5 : -1], refs[-1]
+    weight_ref, bias_ref, cot_ref, back_ref, pre_ref, keep_ref, away_ref, wg = refs[n_parts:]
     agg = tree_sum([p[...] for p in parts])
     high = agg.astype(BF16)
     low = (agg - high.astype(F32)).astype(BF16)
@@ -131,11 +116,11 @@
     wg[...] = jnp.dot(high, grad, preferred_element_type=F32)
     bias_row = jnp.sum(grad.astype(F32), axis=0, keepdims=True).astype(BF16)
     bias_rows = jnp.broadcast_to(bias_row, (PAD, bias_row.shape[1]))
-    depth = wg.shape[0] // len(terms)
-    for k, part in enumerate(terms):
-        start = pl.multiple_of((place_ref[1] ^ k) * depth, depth)
-        part[:depth, :] = wg[pl.ds(start, depth), :].astype(BF16)
-        part[depth:, :] = bias_rows
+    depth = wg.shape[0] // 2
+    mine = place_ref[1] % 2
+    for which, ref in ((mine, keep_ref), (1 - mine, away_ref)):
+        ref[:depth, :] = wg[pl.ds(pl.multiple_of(which * depth, depth), depth), :].astype(BF16)
+        ref[depth:, :] = bias_rows
 
 
 def output_kernel(pre_ref, out_ref):
@@ -145,18 +130,26 @@
     out_ref[...] = (pre * (0.5 * (1.0 + t))).astype(BF16)
 
 
-def pack_kernel(n_after, block_ref, *refs):
-    part_ref, packed_ref = refs[-2:]
-    part = tree_sum([r[...] for r in refs[: -2 - n_after]]).astype(BF16)
-    part_ref[...] = part
-    nodes = block_ref.shape[0]
-    packed_ref[:nodes, :] = block_ref[...]
-    packed_ref[nodes:, :] = part
-
-
-def unpack_kernel(part_ref, packed_ref, out_ref):
-    below = packed_ref.shape[0] - part_ref.shape[0]
-    out_ref[...] = (part_ref[...].astype(F32) + packed_ref[below:, :].astype(F32)).astype(BF16)
+def pack_kernel(block_ref, part_ref, *refs):
+    out_ref = refs[-1]
+    nodes = part_ref.shape[0]
+    out_ref[:-nodes, :] = block_ref[...]
+    out_ref[-nodes:, :] = part_ref[...]
+
+
+def repack_kernel(packed_ref, part_ref, *refs):
+    sum_ref, out_ref = refs[-2:]
+    depth = part_ref.shape[0]
+    nodes = packed_ref.shape[0] - depth
+    total = (part_ref[...].astype(F32) + packed_ref[nodes:, :].astype(F32)).astype(BF16)
+    sum_ref[...] = total
+    out_ref[:nodes, :] = packed_ref[:nodes, :]
+    out_ref[nodes:, :] = total
+
+
+def unpack_kernel(packed_ref, part_ref, sum_ref):
+    nodes = packed_ref.shape[0] - part_ref.shape[0]
+    sum_ref[...] = (part_ref[...].astype(F32) + packed_ref[nodes:, :].astype(F32)).astype(BF16)
 
 
 def pull_kernel(rows, cols, tiles, place_ref, code_ref, *refs):
@@ -167,27 +160,26 @@
     for k in range(rows):
         owner = row ^ k
         block = grad_refs[k][: tiles * size, :]
+        terms = jnp.dot(
+            picked_ref[owner].reshape(slots * size, block.shape[0]), block, preferred_element_type=F32
+        )
         for s in range(slots):
-            total[code_ref[owner * picked_ref.shape[1] + s]] += jnp.dot(
-                picked_ref[owner, s], block, preferred_element_type=F32
-            )
+            total[code_ref[owner * slots + s]] += terms[s * size : (s + 1) * size]
     for k in range(cols):
         for t in range(tiles):
             outs[k][t * size : (t + 1) * size, :] = total[(col ^ k) * tiles + t].astype(BF16)
 
 
-def last_kernel(cols, n_blocks, scale, place_ref, *refs):
-    blocks, pieces = refs[:n_blocks], refs[n_blocks : n_blocks + cols]
-    bias_ref, in_ref, wg_ref, bg_ref = refs[n_blocks + cols :]
-    total = blocks[0][...].astype(F32)
-    for b in blocks[1:]:
-        total += b[...].astype(F32)
-    in_ref[...] = total.astype(BF16)
-    depth = wg_ref.shape[0] // cols
-    for k in range(cols):
-        start = pl.multiple_of((place_ref[1] ^ k) * depth, depth)
-        wg_ref[pl.ds(start, depth), :] = pieces[k][...].astype(F32) * scale
-    bg_ref[...] = bias_ref[...].astype(F32) * scale
+def last_kernel(n_blocks, scale, place_ref, *refs):
+    blocks = refs[:n_blocks]
+    part_ref, other_ref, in_ref, wg_ref, bg_ref = refs[n_blocks:]
+    in_ref[...] = tree_sum([b[...] for b in blocks]).astype(BF16)
+    depth = other_ref.shape[0]
+    mine = place_ref[1] % 2
+    for which, ref in ((mine, part_ref), (1 - mine, other_ref)):
+        start = pl.multiple_of(which * depth, depth)
+        wg_ref[pl.ds(start, depth), :] = ref[:depth, :].astype(F32) * scale
+    bg_ref[...] = part_ref[depth : depth + 1, :].astype(F32) * scale
 
 
 def local(features, weight, bias, tile_values, tile_source, tile_dest, send_counts, cotangent):
@@ -207,8 +199,7 @@
     flops = rows * slots * size * size * tiles * width
 
     far = {k: send(features, "cols", k) for k in range(cols - 1, 0, -1)}
-    hbm, smem = pl.BlockSpec(memory_space=pltpu.HBM), pl.BlockSpec(memory_space=pltpu.SMEM)
-    vmem = pl.BlockSpec(memory_space=pltpu.VMEM)
+    smem, vmem = pl.BlockSpec(memory_space=pltpu.SMEM), pl.BlockSpec(memory_space=pltpu.VMEM)
     picked, own, code = pl.pallas_call(
         functools.partial(prepare_kernel, tiles),
         out_shape=[
@@ -216,16 +207,8 @@
             shape((tiles, width_in, size), BF16),
             shape((rows * slots,), jnp.int32),
         ],
-        in_specs=[hbm] * 5,
+        in_specs=[smem] * 3 + [vmem] * 2,
         out_specs=[vmem, vmem, smem],
-        scratch_shapes=[
-            pltpu.SMEM(source.shape, jnp.int32),
-            pltpu.SMEM(dest.shape, jnp.int32),
-            pltpu.SMEM(send_counts.shape, jnp.int32),
-            pltpu.VMEM(features.shape, BF16),
-            pltpu.VMEM(vals.shape, BF16),
-            pltpu.SemaphoreType.DMA((4 + rows,)),
-        ],
         cost_estimate=pl.CostEstimate(flops=flops, bytes_accessed=2_000_000, transcendentals=0),
         compiler_params=pltpu.CompilerParams(vmem_limit_bytes=48 * 1024 * 1024),
     )(source, dest, send_counts, features, vals)
@@ -257,38 +240,50 @@
         bit *= 2
     parts = summed[0]
 
-    depth = width_in // cols
+    depth = width_in // 2
     part_shape = shape((depth + PAD, width), BF16)
-    back, pre, *terms = call(
+    back, pre, part, away = call(
         functools.partial(middle_kernel, len(parts)),
-        [shape((nodes, width_in), BF16), shape((nodes, width), F32)] + [part_shape] * cols,
+        [shape((nodes, width_in), BF16), shape((nodes, width), F32), part_shape, part_shape],
         [pltpu.VMEM((width_in, width), F32)],
         1,
         len(parts) + 3,
         8 * width * width * nodes,
     )(place, *parts, weight, bias[None, :], cotangent)
-
-    got = {0: back}
+    output = call(output_kernel, shape((nodes, width), BF16), n_vmem=1)(pre)
+
+    part = call(add_kernel, part_shape, n_vmem=2)(part, send(away, "cols", 1))
+    bit = 2
+    while bit < cols:
+        part = call(add_kernel, part_shape, n_vmem=2)(part, send(part, "cols", bit))
+        bit *= 2
+
+    got = {0: back, 1: send(back, "rows", 1)}
+    packed_shape = shape((nodes + depth + PAD, width), BF16)
     bit = rows // 2
     while bit > 1:
-        for k in sorted(got):
-            got[k ^ bit] = send(got[k], "rows", bit)
+        for k in sorted(k for k in got if k % 2 == 0):
+            if k ^ bit == rows - 2:
+                packed = call(pack_kernel, packed_shape, n_vmem=2, n_any=1)(got[k], part, got[1])
+                got[k ^ bit] = send(packed, "rows", bit)
+            else:
+                got[k ^ bit] = send(got[k], "rows", bit)
         bit //= 2
-    for k in range(0, rows - 2, 2):
+    for k in range(2, rows - 2, 2):
         got[k + 1] = send(got[k], "rows", 1)
-
-    output = call(output_kernel, shape((nodes, width), BF16), n_vmem=1)(pre)
-
-    after = [got[k] for k in range(1, rows - 2, 2)]
+    others = [got[k] for k in range(1, rows - 2, 2)]
     part, packed = call(
-        functools.partial(pack_kernel, len(after)),
-        [part_shape, shape((nodes + depth + PAD, width), BF16)],
-        n_vmem=cols + 1,
-        n_any=len(after),
-    )(got[rows - 2], terms[0], *[send(terms[k], "cols", k) for k in range(cols - 1, 0, -1)][::-1], *after)
+        repack_kernel, [part_shape, packed_shape], n_vmem=2, n_any=len(others)
+    )(got[rows - 2], part, *others)
     got[rows - 1] = send(packed, "rows", 1)
-    part = call(unpack_kernel, part_shape, n_vmem=2)(part, got[rows - 1])
-    others = [send(part, "rows", k) for k in range(2, rows, 2)]
+    part = call(unpack_kernel, part_shape, n_vmem=2)(got[rows - 1], part)
+    after = part
+    bit = 4
+    while bit < rows:
+        part = call(add_kernel, part_shape, n_vmem=2)(part, send(part, "rows", bit))
+        bit *= 2
+    half = part[:depth]
+    other = send(half, "cols", 1)
 
     blocks = call(
         functools.partial(pull_kernel, rows, cols, tiles),
@@ -298,27 +293,24 @@
         rows + 1,
         flops,
         n_any=1,
-    )(place, code, *[got[k] for k in range(rows)], picked, part)
+    )(place, code, *[got[k] for k in range(rows)], picked, after)
     arrived = [blocks[0]]
     for k in range(cols - 2, 0, -2):
         near = send(blocks[k + 1], "cols", 1)
         both = call(add_kernel, shape((nodes, width_in), BF16), n_vmem=2)(blocks[k], near)
         arrived.append(send(both, "cols", k))
     arrived.append(send(blocks[1], "cols", 1))
-    part = call(add_kernel, part_shape, n_vmem=rows // 2)(part, *others)
-    piece = part[:depth]
-    pieces = [piece] + [send(piece, "cols", k) for k in range(cols - 1, 0, -1)][::-1]
     scale = 1.0 / math.sqrt(nodes * rows * cols)
     input_grad, weight_grad, bias_grad = call(
-        functools.partial(last_kernel, cols, len(arrived), scale),
+        functools.partial(last_kernel, len(arrived), scale),
         [
             shape((nodes, width_in), BF16),
             shape((width_in, width), F32),
             shape((1, width), F32),
         ],
         n_smem=1,
-        n_vmem=len(arrived) + cols + 1,
-    )(place, *arrived, *pieces, part[depth : depth + 1])
+        n_vmem=len(arrived) + 2,
+    )(place, *arrived, part, other)
     return output, input_grad, weight_grad, bias_grad[0]
 
 

time: 74.9 us -> 68.4 us (0.913)
  starting transfers between devices: 30.9 us -> 27.8 us
  waiting for transfers between devices: 29.4 us -> 27.1 us
  Pallas kernels: 9.41 us -> 8.43 us
    ppermute x29 -> x24, starting transfers between devices: 30.9 us -> 27.8 us  [send(): return lax.ppermute(x, axis, [(i, i ^ offset) for i in range(size)])]
    ppermute x29 -> x24, waiting for transfers between devices: 29.4 us -> 27.1 us  [send(): return lax.ppermute(x, axis, [(i, i ^ offset) for i in range(size)])]
    pallas_call x1, Pallas kernels: 2.26 us -> 1.48 us  [local(): pl.pallas_call(functools.partial(prepare_kernel, tiles), out_shape=[shape...]
  transfers between devices with their start and end apart: 29 -> 24, of which waited for: 17 -> 14; matrix products, arithmetic and copies ran while one was open for 0% -> 0% of each run, Pallas kernels for 6% -> 5%
where the time goes in v3:
time: 68.4 us; the launch traced here: 68.2 us
  starting transfers between devices  27.8 us (41%)
  waiting for transfers between devices  27.1 us (40%)
  Pallas kernels  8.43 us (12%)
  local copies, waits for them, and re-layouts  4.07 us (6%)
  between operations  0.77 us (1%)
    ppermute x24, starting transfers between devices, send(): return lax.ppermute(x, axis, [(i, i ^ offset) for i in range(size)])  27.8 us
    ppermute x24, waiting for transfers between devices, send(): return lax.ppermute(x, axis, [(i, i ^ offset) for i in range(size)])  27.1 us
    unnamed x16, local copies, waits for them, and re-layouts  4.06 us
    pallas_call x1, Pallas kernels, local(): pl.pallas_call(functools.partial(prepare_kernel, tiles), out_shape=[shape...  1.48 us
  transfers between devices with their start and end apart: 24, of which 14 were waited for; matrix products, arithmetic and copies ran while one was open for 0% of the time, Pallas kernels for 5%

profile of v3, /device:TPU:0, one launch (start us, length us, event | category | flops | bytes accessed | tf_op | source)
XLA Modules:
  0.0 68.2 jit_solution(15679132076609377942)
XLA Ops:
  0.6 0.5 collective-permute-start
  1.1 2.6 %collective-permute-start.2 = (bf16[256,256]{1,0:T(8,128)(2,1)}, bf16[256,256]{1,0:T(8,128)(2,1)S(1)}, u32[]{:S(2)}, u32[]{:S(2)}) collective-permute-start(bf16[256,256]{1,0:T(8,128)(2,1)} %feat_ref.1), channel_id=1, source_target_pairs={{0,3},{1,2},{2,1},{3,0},{4,7},{5,6},{6,5},{7,4},{8,11},{9,10},{10,... | collective-permute-start | bytes 393224 | tf_op jit(solution)/shard_map/ppermute | solution.py:42
  3.8 0.0 collective-permute-start.1
  3.8 1.1 %copy-done = bf16[1,1,8,3,128,128]{5,4,3,2,1,0:T(8,128)(2,1)S(1)} copy-done((bf16[1,1,8,3,128,128]{5,4,3,2,1,0:T(8,128)(2,1)S(1)}, bf16[1,1,8,3,128,128]{5,4,3,2,1,0:T(8,128)(2,1)}, u32[]{:S(2)}) %copy-start) | copy-done | bytes 786456
  4.9 0.9 %copy-done.1 = bf16[256,256]{1,0:T(8,128)(2,1)S(1)} copy-done((bf16[256,256]{1,0:T(8,128)(2,1)S(1)}, bf16[256,256]{1,0:T(8,128)(2,1)}, u32[]{:S(2)}) %copy-start.1) | copy-done | bytes 131096
  5.8 0.7 copy-done.4
  6.5 0.7 copy-done.5
  7.2 0.7 copy-done.7
  7.9 1.5 %shard_map.111 = (bf16[8,3,128,256]{3,2,1,0:T(8,128)(2,1)S(1)}, bf16[2,256,128]{2,1,0:T(8,128)(2,1)S(1)}, s32[24]{0:T(128)S(1)}) custom-call(s32[1,3,1,8]{3,2,1,0:T(1,128)S(1)} %bitcast.8, s32[1,3,1,8]{3,2,1,0:T(1,128)S(1)} %bitcast.9, s32[1,1,8]{2,1,0:T(1,128)S(1)} %copy-done.7, bf16[256,256]{1,0:T(8,128)(2,1)S(1)} %copy-done.1, ...), custom_call_target="tpu_custom_call" | custom-call | flops 201326592 | bytes 2000000 | tf_op jit(solution)/shard_map/pallas_call | solution.py:203
  9.4 0.1 pad_add_fusion.place_ref
  9.4 0.0 collective-permute-done.refs_1_
  9.4 0.0 collective-permute-done.2.refs_3_
  9.4 1.4 %collective-permute-done.1.refs_2_ = bf16[256,256]{1,0:T(8,128)(2,1)S(1)} collective-permute-done((bf16[256,256]{1,0:T(8,128)(2,1)}, bf16[256,256]{1,0:T(8,128)(2,1)S(1)}, u32[]{:S(2)}, u32[]{:S(2)}) %collective-permute-start.1) | collective-permute-done | bytes 131104 | tf_op jit(solution)/shard_map/ppermute | solution.py:42
  10.8 1.1 %shard_map.112 = (bf16[256,256]{1,0:T(8,128)(2,1)S(1)}, bf16[256,256]{1,0:T(8,128)(2,1)S(1)}, bf16[256,256]{1,0:T(8,128)(2,1)S(1)}, bf16[256,256]{1,0:T(8,128)(2,1)S(1)}, bf16[8,256,128]{2,1,0:T(8,128)(2,1)S(1)}) custom-call(s32[2]{0:T(128)S(1)} %pad_add_fusion.place_ref, s32[24]{0:T(128)S(1)} %get-tuple-element.29.code_ref, ...), custom_call_target="tpu_custom_call" | custom-call | flops 201326592 | bytes 2000000 | tf_op jit(solution)/shard_map/pallas_call | solution.py:218
  11.9 1.8 %collective-permute-start.7 = (bf16[256,256]{1,0:T(8,128)(2,1)S(1)}, bf16[256,256]{1,0:T(8,128)(2,1)S(1)}, u32[]{:S(2)}, u32[]{:S(2)}) collective-permute-start(bf16[256,256]{1,0:T(8,128)(2,1)S(1)} %get-tuple-element.40), channel_id=1, source_target_pairs={{0,4},{4,0},{8,12},{12,8},{16,20},{20,16},{24,28},{28,24},{1,5},{5... | collective-permute-start | bytes 393224 | tf_op jit(solution)/shard_map/ppermute | solution.py:42
  13.7 0.3 collective-permute-start.4
  14.0 1.0 %shard_map.113 = (bf16[256,256]{1,0:T(8,128)(2,1)S(1)}, bf16[256,256]{1,0:T(8,128)(2,1)S(1)}, bf16[256,256]{1,0:T(8,128)(2,1)S(1)}, bf16[256,256]{1,0:T(8,128)(2,1)S(1)}) custom-call(s32[2]{0:T(128)S(1)} %pad_add_fusion.place_ref, s32[24]{0:T(128)S(1)} %get-tuple-element.29.code_ref, bf16[8,256,128]{2,1,0:T(8,128)(2,1)S(1)} %get-tuple-element.32.turned, ...), custom_call_target="tpu_custom_call" | custom-call | flops 201326592 | bytes 2000000 | tf_op jit(solution)/shard_map/pallas_call | solution.py:225
  15.0 1.8 %collective-permute-start.6 = (bf16[256,256]{1,0:T(8,128)(2,1)S(1)}, bf16[256,256]{1,0:T(8,128)(2,1)S(1)}, u32[]{:S(2)}, u32[]{:S(2)}) collective-permute-start(bf16[256,256]{1,0:T(8,128)(2,1)S(1)} %get-tuple-element.38), channel_id=1, source_target_pairs={{0,4},{4,0},{8,12},{12,8},{16,20},{20,16},{24,28},{28,24},{1,5},{5... | collective-permute-start | bytes 393224 | tf_op jit(solution)/shard_map/ppermute | solution.py:42
  16.8 1.6 %collective-permute-done.7.refs_1_ = bf16[256,256]{1,0:T(8,128)(2,1)S(1)} collective-permute-done((bf16[256,256]{1,0:T(8,128)(2,1)S(1)}, bf16[256,256]{1,0:T(8,128)(2,1)S(1)}, u32[]{:S(2)}, u32[]{:S(2)}) %collective-permute-start.7) | collective-permute-done | bytes 131104 | tf_op jit(solution)/shard_map/ppermute | solution.py:42
  18.4 1.9 %collective-permute-start.8 = (bf16[256,256]{1,0:T(8,128)(2,1)S(1)}, bf16[256,256]{1,0:T(8,128)(2,1)S(1)}, u32[]{:S(2)}, u32[]{:S(2)}) collective-permute-start(bf16[256,256]{1,0:T(8,128)(2,1)S(1)} %shard_map.115), channel_id=1, source_target_pairs={{0,8},{4,12},{8,0},{12,4},{16,24},{20,28},{24,16},{28,20},{1,9},{5... | collective-permute-start | bytes 393224 | tf_op jit(solution)/shard_map/ppermute | solution.py:42
  20.3 1.5 %collective-permute-start.3 = (bf16[256,256]{1,0:T(8,128)(2,1)S(1)}, bf16[256,256]{1,0:T(8,128)(2,1)S(1)}, u32[]{:S(2)}, u32[]{:S(2)}) collective-permute-start(bf16[256,256]{1,0:T(8,128)(2,1)S(1)} %get-tuple-element.34), channel_id=1, source_target_pairs={{0,4},{4,0},{8,12},{12,8},{16,20},{20,16},{24,28},{28,24},{1,5},{5... | collective-permute-start | bytes 393224 | tf_op jit(solution)/shard_map/ppermute | solution.py:42
  21.8 0.0 collective-permute-done.4.refs_1_
  21.9 1.2 %collective-permute-start.5 = (bf16[256,256]{1,0:T(8,128)(2,1)S(1)}, bf16[256,256]{1,0:T(8,128)(2,1)S(1)}, u32[]{:S(2)}, u32[]{:S(2)}) collective-permute-start(bf16[256,256]{1,0:T(8,128)(2,1)S(1)} %shard_map.114), channel_id=1, source_target_pairs={{0,8},{4,12},{8,0},{12,4},{16,24},{20,28},{24,16},{28,20},{1,9},{5... | collective-permute-start | bytes 393224 | tf_op jit(solution)/shard_map/ppermute | solution.py:42
  23.1 0.9 %collective-permute-done.6.refs_1_ = bf16[256,256]{1,0:T(8,128)(2,1)S(1)} collective-permute-done((bf16[256,256]{1,0:T(8,128)(2,1)S(1)}, bf16[256,256]{1,0:T(8,128)(2,1)S(1)}, u32[]{:S(2)}, u32[]{:S(2)}) %collective-permute-start.6) | collective-permute-done | bytes 131104 | tf_op jit(solution)/shard_map/ppermute | solution.py:42
  24.0 0.5 collective-permute-done.8.refs_2_
  24.5 0.1 shard_map.116
  24.6 2.3 %collective-permute-start.9 = (bf16[256,256]{1,0:T(8,128)(2,1)S(1)}, bf16[256,256]{1,0:T(8,128)(2,1)S(1)}, u32[]{:S(2)}, u32[]{:S(2)}) collective-permute-start(bf16[256,256]{1,0:T(8,128)(2,1)S(1)} %shard_map.116), channel_id=1, source_target_pairs={{0,16},{4,20},{8,24},{12,28},{16,0},{20,4},{24,8},{28,12},{1,17},{... | collective-permute-start | bytes 393224 | tf_op jit(solution)/shard_map/ppermute | solution.py:42
  26.9 0.0 collective-permute-done.3.refs_1_
  26.9 0.7 %collective-permute-done.5.refs_2_ = bf16[256,256]{1,0:T(8,128)(2,1)S(1)} collective-permute-done((bf16[256,256]{1,0:T(8,128)(2,1)S(1)}, bf16[256,256]{1,0:T(8,128)(2,1)S(1)}, u32[]{:S(2)}, u32[]{:S(2)}) %collective-permute-start.5) | collective-permute-done | bytes 131104 | tf_op jit(solution)/shard_map/ppermute | solution.py:42
  27.6 4.3 %collective-permute-done.9.refs_3_ = bf16[256,256]{1,0:T(8,128)(2,1)S(1)} collective-permute-done((bf16[256,256]{1,0:T(8,128)(2,1)S(1)}, bf16[256,256]{1,0:T(8,128)(2,1)S(1)}, u32[]{:S(2)}, u32[]{:S(2)}) %collective-permute-start.9) | collective-permute-done | bytes 131104 | tf_op jit(solution)/shard_map/ppermute | solution.py:42
  31.9 0.0 copy-done.2
  31.9 0.0 copy-done.6
  31.9 1.3 %shard_map.117 = (bf16[256,256]{1,0:T(8,128)(2,1)S(1)}, f32[256,256]{1,0:T(8,128)S(1)}, bf16[144,256]{1,0:T(8,128)(2,1)S(1)}, bf16[144,256]{1,0:T(8,128)(2,1)S(1)}) custom-call(s32[2]{0:T(128)S(1)} %pad_add_fusion.place_ref, bf16[256,256]{1,0:T(8,128)(2,1)S(1)} %get-tuple-element.33.refs_0_, bf16[256,256]{1,0:T(8,128)(2,1)S(1)} %collective-permute-done.3.refs_1_, ...), custom_call_target="tpu_custom_call" | custom-call | flops 134217728 | bytes 2000000 | tf_op jit(solution)/shard_map/pallas_call | solution.py:245
  33.2 0.1 collective-permute-start.15
  33.3 1.0 %collective-permute-start.13 = (bf16[256,256]{1,0:T(8,128)(2,1)S(1)}, bf16[256,256]{1,0:T(8,128)(2,1)S(1)}, u32[]{:S(2)}, u32[]{:S(2)}) collective-permute-start(bf16[256,256]{1,0:T(8,128)(2,1)S(1)} %get-tuple-element.42.refs_0_), channel_id=1, source_target_pairs={{0,16},{4,20},{8,24},{12,28},{16,0},{20,4},{24,8},{28,12},{1,17},{... | collective-permute-start | bytes 393224 | tf_op jit(solution)/shard_map/ppermute | solution.py:42
  34.3 1.5 %collective-permute-start.10 = (bf16[256,256]{1,0:T(8,128)(2,1)S(1)}, bf16[256,256]{1,0:T(8,128)(2,1)S(1)}, u32[]{:S(2)}, u32[]{:S(2)}) collective-permute-start(bf16[256,256]{1,0:T(8,128)(2,1)S(1)} %get-tuple-element.42.refs_0_), channel_id=1, source_target_pairs={{0,4},{4,0},{8,12},{12,8},{16,20},{20,16},{24,28},{28,24},{1,5},{5... | collective-permute-start | bytes 393224 | tf_op jit(solution)/shard_map/ppermute | solution.py:42
  35.8 0.0 collective-permute-done.15.refs_1_
  35.8 1.6 %collective-permute-start.16 = (bf16[144,256]{1,0:T(8,128)(2,1)S(1)}, bf16[144,256]{1,0:T(8,128)(2,1)S(1)}, u32[]{:S(2)}, u32[]{:S(2)}) collective-permute-start(bf16[144,256]{1,0:T(8,128)(2,1)S(1)} %shard_map.119.refs_0_), channel_id=1, source_target_pairs={{0,2},{1,3},{2,0},{3,1},{4,6},{5,7},{6,4},{7,5},{8,10},{9,11},{10,... | collective-permute-start | bytes 221192 | tf_op jit(solution)/shard_map/ppermute | solution.py:42
  37.4 2.8 %collective-permute-start.11 = (bf16[256,256]{1,0:T(8,128)(2,1)S(1)}, bf16[256,256]{1,0:T(8,128)(2,1)S(1)}, u32[]{:S(2)}, u32[]{:S(2)}) collective-permute-start(bf16[256,256]{1,0:T(8,128)(2,1)S(1)} %get-tuple-element.42.refs_0_), channel_id=1, source_target_pairs={{0,8},{4,12},{8,0},{12,4},{16,24},{20,28},{24,16},{28,20},{1,9},{5... | collective-permute-start | bytes 393224 | tf_op jit(solution)/shard_map/ppermute | solution.py:42
  40.2 0.1 collective-permute-done.16.refs_1_
  40.3 2.7 %collective-permute-done.13.block_ref.refs_4_ = bf16[256,256]{1,0:T(8,128)(2,1)S(1)} collective-permute-done((bf16[256,256]{1,0:T(8,128)(2,1)S(1)}, bf16[256,256]{1,0:T(8,128)(2,1)S(1)}, u32[]{:S(2)}, u32[]{:S(2)}) %collective-permute-start.13) | collective-permute-done | bytes 131104 | tf_op jit(solution)/shard_map/ppermute | solution.py:42
  43.0 0.0 collective-permute-done.10.refs_0_.refs_1_
  43.0 0.1 collective-permute-start.17
  43.2 1.2 %collective-permute-start.14 = (bf16[256,256]{1,0:T(8,128)(2,1)S(1)}, bf16[256,256]{1,0:T(8,128)(2,1)S(1)}, u32[]{:S(2)}, u32[]{:S(2)}) collective-permute-start(bf16[256,256]{1,0:T(8,128)(2,1)S(1)} %collective-permute-done.13.block_ref.refs_4_), channel_id=1, source_target_pairs={{0,4},{4,0},{8,12},{12,8},{16,20},{20,16},{24,28},{28,24},{1,5},{5... | collective-permute-start | bytes 393224 | tf_op jit(solution)/shard_map/ppermute | solution.py:42
  44.3 1.5 %collective-permute-done.11.refs_2_ = bf16[256,256]{1,0:T(8,128)(2,1)S(1)} collective-permute-done((bf16[256,256]{1,0:T(8,128)(2,1)S(1)}, bf16[256,256]{1,0:T(8,128)(2,1)S(1)}, u32[]{:S(2)}, u32[]{:S(2)}) %collective-permute-start.11) | collective-permute-done | bytes 131104 | tf_op jit(solution)/shard_map/ppermute | solution.py:42
  45.8 0.0 collective-permute-start.12
  45.8 2.4 %collective-permute-done.14.refs_2_.refs_5_ = bf16[256,256]{1,0:T(8,128)(2,1)S(1)} collective-permute-done((bf16[256,256]{1,0:T(8,128)(2,1)S(1)}, bf16[256,256]{1,0:T(8,128)(2,1)S(1)}, u32[]{:S(2)}, u32[]{:S(2)}) %collective-permute-start.14) | collective-permute-done | bytes 131104 | tf_op jit(solution)/shard_map/ppermute | solution.py:42
  48.2 2.8 %collective-permute-done.12.refs_1_.refs_3_ = bf16[256,256]{1,0:T(8,128)(2,1)S(1)} collective-permute-done((bf16[256,256]{1,0:T(8,128)(2,1)S(1)}, bf16[256,256]{1,0:T(8,128)(2,1)S(1)}, u32[]{:S(2)}, u32[]{:S(2)}) %collective-permute-start.12) | collective-permute-done | bytes 131104 | tf_op jit(solution)/shard_map/ppermute | solution.py:42
  51.0 0.0 collective-permute-done.17.packed_ref.refs_6_
  51.0 1.2 %collective-permute-start.18 = (bf16[400,256]{1,0:T(8,128)(2,1)S(1)}, bf16[400,256]{1,0:T(8,128)(2,1)S(1)}, u32[]{:S(2)}, u32[]{:S(2)}) collective-permute-start(bf16[400,256]{1,0:T(8,128)(2,1)S(1)} %get-tuple-element.45), channel_id=1, source_target_pairs={{0,4},{4,0},{8,12},{12,8},{16,20},{20,16},{24,28},{28,24},{1,5},{5... | collective-permute-start | bytes 614408 | tf_op jit(solution)/shard_map/ppermute | solution.py:42
  52.3 4.7 %collective-permute-done.18.packed_ref.refs_7_ = bf16[400,256]{1,0:T(8,128)(2,1)S(1)} collective-permute-done((bf16[400,256]{1,0:T(8,128)(2,1)S(1)}, bf16[400,256]{1,0:T(8,128)(2,1)S(1)}, u32[]{:S(2)}, u32[]{:S(2)}) %collective-permute-start.18) | collective-permute-done | bytes 204832 | tf_op jit(solution)/shard_map/ppermute | solution.py:42
  57.0 1.3 %shard_map.124 = (bf16[256,256]{1,0:T(8,128)(2,1)S(1)}, bf16[256,256]{1,0:T(8,128)(2,1)S(1)}, bf16[256,256]{1,0:T(8,128)(2,1)S(1)}, bf16[256,256]{1,0:T(8,128)(2,1)S(1)}) custom-call(s32[2]{0:T(128)S(1)} %pad_add_fusion.place_ref, s32[24]{0:T(128)S(1)} %get-tuple-element.29.code_ref, bf16[256,256]{1,0:T(8,128)(2,1)S(1)} %get-tuple-element.42.refs_0_, ...), custom_call_target="tpu_custom_call" | custom-call | flops 201326592 | bytes 2000000 | tf_op jit(solution)/shard_map/pallas_call | solution.py:288
  58.3 0.1 collective-permute-start.19
  58.4 2.4 %collective-permute-start.22 = (bf16[144,256]{1,0:T(8,128)(2,1)S(1)}, bf16[144,256]{1,0:T(8,128)(2,1)S(1)}, u32[]{:S(2)}, u32[]{:S(2)}) collective-permute-start(bf16[144,256]{1,0:T(8,128)(2,1)S(1)} %shard_map.123.refs_9_.refs_0_), channel_id=1, source_target_pairs={{0,16},{4,20},{8,24},{12,28},{16,0},{20,4},{24,8},{28,12},{1,17},{... | collective-permute-start | bytes 221192 | tf_op jit(solution)/shard_map/ppermute | solution.py:42
  60.8 0.2 collective-permute-start.21
  61.0 0.0 collective-permute-done.19.refs_1_
  61.0 1.6 %collective-permute-start.20 = (bf16[256,256]{1,0:T(8,128)(2,1)S(1)}, bf16[256,256]{1,0:T(8,128)(2,1)S(1)}, u32[]{:S(2)}, u32[]{:S(2)}) collective-permute-start(bf16[256,256]{1,0:T(8,128)(2,1)S(1)} %shard_map.125), channel_id=1, source_target_pairs={{0,2},{1,3},{2,0},{3,1},{4,6},{5,7},{6,4},{7,5},{8,10},{9,11},{10,... | collective-permute-start | bytes 393224 | tf_op jit(solution)/shard_map/ppermute | solution.py:42
  62.6 3.0 %collective-permute-done.22.refs_1_ = bf16[144,256]{1,0:T(8,128)(2,1)S(1)} collective-permute-done((bf16[144,256]{1,0:T(8,128)(2,1)S(1)}, bf16[144,256]{1,0:T(8,128)(2,1)S(1)}, u32[]{:S(2)}, u32[]{:S(2)}) %collective-permute-start.22) | collective-permute-done | bytes 73760 | tf_op jit(solution)/shard_map/ppermute | solution.py:42
  65.6 0.1 collective-permute-start.23
  65.6 0.7 %shard_map.118 = bf16[256,256]{1,0:T(8,128)(2,1)} custom-call(f32[256,256]{1,0:T(8,128)S(1)} %get-tuple-element.41.pre_ref), custom_call_target="tpu_custom_call" | custom-call | bytes 2000000 | tf_op jit(solution)/shard_map/pallas_call | solution.py:253
  66.4 0.0 collective-permute-done.21.refs_2_
  66.4 0.5 collective-permute-done.23.refs_4_
  66.9 0.0 collective-permute-done.20.refs_1_
  66.9 1.3 %shard_map.127 = (bf16[256,256]{1,0:T(8,128)(2,1)}, f32[256,256]{1,0:T(8,128)}, f32[1,256]{1,0:T(1,128)}) custom-call(s32[2]{0:T(128)S(1)} %pad_add_fusion.place_ref, bf16[256,256]{1,0:T(8,128)(2,1)S(1)} %get-tuple-element.47.refs_0_, bf16[256,256]{1,0:T(8,128)(2,1)S(1)} %collective-permute-done.20.refs_1_, ...), custom_call_target="tpu_custom_call" | custom-call | bytes 2000000 | tf_op jit(solution)/shard_map/pallas_call | solution.py:304
  (19 shorter events, 0.2 us)
Async XLA Ops:
  0.6 8.8 %collective-permute-start = (bf16[256,256]{1,0:T(8,128)(2,1)}, bf16[256,256]{1,0:T(8,128)(2,1)S(1)}, u32[]{:S(2)}, u32[]{:S(2)}) collective-permute-start(bf16[256,256]{1,0:T(8,128)(2,1)} %feat_ref.1), channel_id=1, source_target_pairs={{0,1},{1,0},{2,3},{3,2},{4,5},{5,4},{6,7},{7,6},{8,9},{9,8},{10,11... | collective-permute-start | bytes 393224 | tf_op jit(solution)/shard_map/ppermute | solution.py:42
  1.1 8.3 %collective-permute-start.2 = (bf16[256,256]{1,0:T(8,128)(2,1)}, bf16[256,256]{1,0:T(8,128)(2,1)S(1)}, u32[]{:S(2)}, u32[]{:S(2)}) collective-permute-start(bf16[256,256]{1,0:T(8,128)(2,1)} %feat_ref.1), channel_id=1, source_target_pairs={{0,3},{1,2},{2,1},{3,0},{4,7},{5,6},{6,5},{7,4},{8,11},{9,10},{10,... | collective-permute-start | bytes 393224 | tf_op jit(solution)/shard_map/ppermute | solution.py:42
  3.8 7.1 %collective-permute-start.1 = (bf16[256,256]{1,0:T(8,128)(2,1)}, bf16[256,256]{1,0:T(8,128)(2,1)S(1)}, u32[]{:S(2)}, u32[]{:S(2)}) collective-permute-start(bf16[256,256]{1,0:T(8,128)(2,1)} %feat_ref.1), channel_id=1, source_target_pairs={{0,2},{1,3},{2,0},{3,1},{4,6},{5,7},{6,4},{7,5},{8,10},{9,11},{10,... | collective-permute-start | bytes 393224 | tf_op jit(solution)/shard_map/ppermute | solution.py:42
  3.8 1.1 %copy-start = (bf16[1,1,8,3,128,128]{5,4,3,2,1,0:T(8,128)(2,1)S(1)}, bf16[1,1,8,3,128,128]{5,4,3,2,1,0:T(8,128)(2,1)}, u32[]{:S(2)}) copy-start(bf16[1,1,8,3,128,128]{5,4,3,2,1,0:T(8,128)(2,1)} %param.11) | copy-start | bytes 2359300
  4.9 0.9 %copy-start.1 = (bf16[256,256]{1,0:T(8,128)(2,1)S(1)}, bf16[256,256]{1,0:T(8,128)(2,1)}, u32[]{:S(2)}) copy-start(bf16[256,256]{1,0:T(8,128)(2,1)} %feat_ref.1) | copy-start | bytes 393220
  5.8 0.7 copy-start.4
  6.5 0.7 copy-start.5
  7.2 0.7 copy-start.7
  11.9 6.5 %collective-permute-start.7 = (bf16[256,256]{1,0:T(8,128)(2,1)S(1)}, bf16[256,256]{1,0:T(8,128)(2,1)S(1)}, u32[]{:S(2)}, u32[]{:S(2)}) collective-permute-start(bf16[256,256]{1,0:T(8,128)(2,1)S(1)} %get-tuple-element.40), channel_id=1, source_target_pairs={{0,4},{4,0},{8,12},{12,8},{16,20},{20,16},{24,28},{28,24},{1,5},{5... | collective-permute-start | bytes 393224 | tf_op jit(solution)/shard_map/ppermute | solution.py:42
  13.7 8.1 %collective-permute-start.4 = (bf16[256,256]{1,0:T(8,128)(2,1)S(1)}, bf16[256,256]{1,0:T(8,128)(2,1)S(1)}, u32[]{:S(2)}, u32[]{:S(2)}) collective-permute-start(bf16[256,256]{1,0:T(8,128)(2,1)S(1)} %get-tuple-element.36), channel_id=1, source_target_pairs={{0,4},{4,0},{8,12},{12,8},{16,20},{20,16},{24,28},{28,24},{1,5},{5... | collective-permute-start | bytes 393224 | tf_op jit(solution)/shard_map/ppermute | solution.py:42
  14.0 17.9 %copy-start.2 = (bf16[256,256]{1,0:T(8,128)(2,1)S(1)}, bf16[256,256]{1,0:T(8,128)(2,1)}, u32[]{:S(2)}) copy-start(bf16[256,256]{1,0:T(8,128)(2,1)} %refs_4_.1) | copy-start | bytes 393220
  14.0 17.9 %copy-start.3 = (bf16[256,256]{1,0:T(8,128)(2,1)S(1)}, bf16[256,256]{1,0:T(8,128)(2,1)}, u32[]{:S(2)}) copy-start(bf16[256,256]{1,0:T(8,128)(2,1)} %refs_6_.1) | copy-start | bytes 393220
  14.0 17.9 %copy-start.6 = (f32[256]{0:T(256)S(1)}, f32[256]{0:T(256)}, u32[]{:S(2)}) copy-start(f32[256]{0:T(256)} %param.10) | copy-start | bytes 3076
  15.0 9.0 %collective-permute-start.6 = (bf16[256,256]{1,0:T(8,128)(2,1)S(1)}, bf16[256,256]{1,0:T(8,128)(2,1)S(1)}, u32[]{:S(2)}, u32[]{:S(2)}) collective-permute-start(bf16[256,256]{1,0:T(8,128)(2,1)S(1)} %get-tuple-element.38), channel_id=1, source_target_pairs={{0,4},{4,0},{8,12},{12,8},{16,20},{20,16},{24,28},{28,24},{1,5},{5... | collective-permute-start | bytes 393224 | tf_op jit(solution)/shard_map/ppermute | solution.py:42
  18.4 6.1 %collective-permute-start.8 = (bf16[256,256]{1,0:T(8,128)(2,1)S(1)}, bf16[256,256]{1,0:T(8,128)(2,1)S(1)}, u32[]{:S(2)}, u32[]{:S(2)}) collective-permute-start(bf16[256,256]{1,0:T(8,128)(2,1)S(1)} %shard_map.115), channel_id=1, source_target_pairs={{0,8},{4,12},{8,0},{12,4},{16,24},{20,28},{24,16},{28,20},{1,9},{5... | collective-permute-start | bytes 393224 | tf_op jit(solution)/shard_map/ppermute | solution.py:42
  20.3 6.6 %collective-permute-start.3 = (bf16[256,256]{1,0:T(8,128)(2,1)S(1)}, bf16[256,256]{1,0:T(8,128)(2,1)S(1)}, u32[]{:S(2)}, u32[]{:S(2)}) collective-permute-start(bf16[256,256]{1,0:T(8,128)(2,1)S(1)} %get-tuple-element.34), channel_id=1, source_target_pairs={{0,4},{4,0},{8,12},{12,8},{16,20},{20,16},{24,28},{28,24},{1,5},{5... | collective-permute-start | bytes 393224 | tf_op jit(solution)/shard_map/ppermute | solution.py:42
  21.9 5.7 %collective-permute-start.5 = (bf16[256,256]{1,0:T(8,128)(2,1)S(1)}, bf16[256,256]{1,0:T(8,128)(2,1)S(1)}, u32[]{:S(2)}, u32[]{:S(2)}) collective-permute-start(bf16[256,256]{1,0:T(8,128)(2,1)S(1)} %shard_map.114), channel_id=1, source_target_pairs={{0,8},{4,12},{8,0},{12,4},{16,24},{20,28},{24,16},{28,20},{1,9},{5... | collective-permute-start | bytes 393224 | tf_op jit(solution)/shard_map/ppermute | solution.py:42
  24.6 7.3 %collective-permute-start.9 = (bf16[256,256]{1,0:T(8,128)(2,1)S(1)}, bf16[256,256]{1,0:T(8,128)(2,1)S(1)}, u32[]{:S(2)}, u32[]{:S(2)}) collective-permute-start(bf16[256,256]{1,0:T(8,128)(2,1)S(1)} %shard_map.116), channel_id=1, source_target_pairs={{0,16},{4,20},{8,24},{12,28},{16,0},{20,4},{24,8},{28,12},{1,17},{... | collective-permute-start | bytes 393224 | tf_op jit(solution)/shard_map/ppermute | solution.py:42
  33.2 2.6 %collective-permute-start.15 = (bf16[144,256]{1,0:T(8,128)(2,1)S(1)}, bf16[144,256]{1,0:T(8,128)(2,1)S(1)}, u32[]{:S(2)}, u32[]{:S(2)}) collective-permute-start(bf16[144,256]{1,0:T(8,128)(2,1)S(1)} %get-tuple-element.44), channel_id=1, source_target_pairs={{0,1},{1,0},{2,3},{3,2},{4,5},{5,4},{6,7},{7,6},{8,9},{9,8},{10,11... | collective-permute-start | bytes 221192 | tf_op jit(solution)/shard_map/ppermute | solution.py:42
  33.3 9.7 %collective-permute-start.13 = (bf16[256,256]{1,0:T(8,128)(2,1)S(1)}, bf16[256,256]{1,0:T(8,128)(2,1)S(1)}, u32[]{:S(2)}, u32[]{:S(2)}) collective-permute-start(bf16[256,256]{1,0:T(8,128)(2,1)S(1)} %get-tuple-element.42.refs_0_), channel_id=1, source_target_pairs={{0,16},{4,20},{8,24},{12,28},{16,0},{20,4},{24,8},{28,12},{1,17},{... | collective-permute-start | bytes 393224 | tf_op jit(solution)/shard_map/ppermute | solution.py:42
  34.3 8.7 %collective-permute-start.10 = (bf16[256,256]{1,0:T(8,128)(2,1)S(1)}, bf16[256,256]{1,0:T(8,128)(2,1)S(1)}, u32[]{:S(2)}, u32[]{:S(2)}) collective-permute-start(bf16[256,256]{1,0:T(8,128)(2,1)S(1)} %get-tuple-element.42.refs_0_), channel_id=1, source_target_pairs={{0,4},{4,0},{8,12},{12,8},{16,20},{20,16},{24,28},{28,24},{1,5},{5... | collective-permute-start | bytes 393224 | tf_op jit(solution)/shard_map/ppermute | solution.py:42
  35.8 4.4 %collective-permute-start.16 = (bf16[144,256]{1,0:T(8,128)(2,1)S(1)}, bf16[144,256]{1,0:T(8,128)(2,1)S(1)}, u32[]{:S(2)}, u32[]{:S(2)}) collective-permute-start(bf16[144,256]{1,0:T(8,128)(2,1)S(1)} %shard_map.119.refs_0_), channel_id=1, source_target_pairs={{0,2},{1,3},{2,0},{3,1},{4,6},{5,7},{6,4},{7,5},{8,10},{9,11},{10,... | collective-permute-start | bytes 221192 | tf_op jit(solution)/shard_map/ppermute | solution.py:42
  37.4 8.4 %collective-permute-start.11 = (bf16[256,256]{1,0:T(8,128)(2,1)S(1)}, bf16[256,256]{1,0:T(8,128)(2,1)S(1)}, u32[]{:S(2)}, u32[]{:S(2)}) collective-permute-start(bf16[256,256]{1,0:T(8,128)(2,1)S(1)} %get-tuple-element.42.refs_0_), channel_id=1, source_target_pairs={{0,8},{4,12},{8,0},{12,4},{16,24},{20,28},{24,16},{28,20},{1,9},{5... | collective-permute-start | bytes 393224 | tf_op jit(solution)/shard_map/ppermute | solution.py:42
  43.0 8.0 %collective-permute-start.17 = (bf16[400,256]{1,0:T(8,128)(2,1)S(1)}, bf16[400,256]{1,0:T(8,128)(2,1)S(1)}, u32[]{:S(2)}, u32[]{:S(2)}) collective-permute-start(bf16[400,256]{1,0:T(8,128)(2,1)S(1)} %shard_map.121), channel_id=1, source_target_pairs={{0,8},{4,12},{8,0},{12,4},{16,24},{20,28},{24,16},{28,20},{1,9},{5... | collective-permute-start | bytes 614408 | tf_op jit(solution)/shard_map/ppermute | solution.py:42
  43.2 5.0 %collective-permute-start.14 = (bf16[256,256]{1,0:T(8,128)(2,1)S(1)}, bf16[256,256]{1,0:T(8,128)(2,1)S(1)}, u32[]{:S(2)}, u32[]{:S(2)}) collective-permute-start(bf16[256,256]{1,0:T(8,128)(2,1)S(1)} %collective-permute-done.13.block_ref.refs_4_), channel_id=1, source_target_pairs={{0,4},{4,0},{8,12},{12,8},{16,20},{20,16},{24,28},{28,24},{1,5},{5... | collective-permute-start | bytes 393224 | tf_op jit(solution)/shard_map/ppermute | solution.py:42
  45.8 5.2 %collective-permute-start.12 = (bf16[256,256]{1,0:T(8,128)(2,1)S(1)}, bf16[256,256]{1,0:T(8,128)(2,1)S(1)}, u32[]{:S(2)}, u32[]{:S(2)}) collective-permute-start(bf16[256,256]{1,0:T(8,128)(2,1)S(1)} %collective-permute-done.11.refs_2_), channel_id=1, source_target_pairs={{0,4},{4,0},{8,12},{12,8},{16,20},{20,16},{24,28},{28,24},{1,5},{5... | collective-permute-start | bytes 393224 | tf_op jit(solution)/shard_map/ppermute | solution.py:42
  51.0 6.0 %collective-permute-start.18 = (bf16[400,256]{1,0:T(8,128)(2,1)S(1)}, bf16[400,256]{1,0:T(8,128)(2,1)S(1)}, u32[]{:S(2)}, u32[]{:S(2)}) collective-permute-start(bf16[400,256]{1,0:T(8,128)(2,1)S(1)} %get-tuple-element.45), channel_id=1, source_target_pairs={{0,4},{4,0},{8,12},{12,8},{16,20},{20,16},{24,28},{28,24},{1,5},{5... | collective-permute-start | bytes 614408 | tf_op jit(solution)/shard_map/ppermute | solution.py:42
  58.3 2.7 %collective-permute-start.19 = (bf16[256,256]{1,0:T(8,128)(2,1)S(1)}, bf16[256,256]{1,0:T(8,128)(2,1)S(1)}, u32[]{:S(2)}, u32[]{:S(2)}) collective-permute-start(bf16[256,256]{1,0:T(8,128)(2,1)S(1)} %get-tuple-element.49), channel_id=1, source_target_pairs={{0,1},{1,0},{2,3},{3,2},{4,5},{5,4},{6,7},{7,6},{8,9},{9,8},{10,11... | collective-permute-start | bytes 393224 | tf_op jit(solution)/shard_map/ppermute | solution.py:42
  58.4 7.2 %collective-permute-start.22 = (bf16[144,256]{1,0:T(8,128)(2,1)S(1)}, bf16[144,256]{1,0:T(8,128)(2,1)S(1)}, u32[]{:S(2)}, u32[]{:S(2)}) collective-permute-start(bf16[144,256]{1,0:T(8,128)(2,1)S(1)} %shard_map.123.refs_9_.refs_0_), channel_id=1, source_target_pairs={{0,16},{4,20},{8,24},{12,28},{16,0},{20,4},{24,8},{28,12},{1,17},{... | collective-permute-start | bytes 221192 | tf_op jit(solution)/shard_map/ppermute | solution.py:42
  60.8 5.6 %collective-permute-start.21 = (bf16[256,256]{1,0:T(8,128)(2,1)S(1)}, bf16[256,256]{1,0:T(8,128)(2,1)S(1)}, u32[]{:S(2)}, u32[]{:S(2)}) collective-permute-start(bf16[256,256]{1,0:T(8,128)(2,1)S(1)} %get-tuple-element.50), channel_id=1, source_target_pairs={{0,1},{1,0},{2,3},{3,2},{4,5},{5,4},{6,7},{7,6},{8,9},{9,8},{10,11... | collective-permute-start | bytes 393224 | tf_op jit(solution)/shard_map/ppermute | solution.py:42
  61.0 5.9 %collective-permute-start.20 = (bf16[256,256]{1,0:T(8,128)(2,1)S(1)}, bf16[256,256]{1,0:T(8,128)(2,1)S(1)}, u32[]{:S(2)}, u32[]{:S(2)}) collective-permute-start(bf16[256,256]{1,0:T(8,128)(2,1)S(1)} %shard_map.125), channel_id=1, source_target_pairs={{0,2},{1,3},{2,0},{3,1},{4,6},{5,7},{6,4},{7,5},{8,10},{9,11},{10,... | collective-permute-start | bytes 393224 | tf_op jit(solution)/shard_map/ppermute | solution.py:42
  65.6 1.3 %collective-permute-start.23 = (bf16[128,256]{1,0:T(8,128)(2,1)S(1)}, bf16[128,256]{1,0:T(8,128)(2,1)S(1)}, u32[]{:S(2)}, u32[]{:S(2)}) collective-permute-start(bf16[128,256]{1,0:T(8,128)(2,1)S(1)} %slice.4), channel_id=1, source_target_pairs={{0,1},{1,0},{2,3},{3,2},{4,5},{5,4},{6,7},{7,6},{8,9},{9,8},{10,11... | collective-permute-start | bytes 196616 | tf_op jit(solution)/shard_map/ppermute | solution.py:42

commit v4 on v3

--- a/solution.py
+++ b/solution.py
@@ -130,26 +130,8 @@
     out_ref[...] = (pre * (0.5 * (1.0 + t))).astype(BF16)
 
 
-def pack_kernel(block_ref, part_ref, *refs):
-    out_ref = refs[-1]
-    nodes = part_ref.shape[0]
-    out_ref[:-nodes, :] = block_ref[...]
-    out_ref[-nodes:, :] = part_ref[...]
-
-
-def repack_kernel(packed_ref, part_ref, *refs):
-    sum_ref, out_ref = refs[-2:]
-    depth = part_ref.shape[0]
-    nodes = packed_ref.shape[0] - depth
-    total = (part_ref[...].astype(F32) + packed_ref[nodes:, :].astype(F32)).astype(BF16)
-    sum_ref[...] = total
-    out_ref[:nodes, :] = packed_ref[:nodes, :]
-    out_ref[nodes:, :] = total
-
-
-def unpack_kernel(packed_ref, part_ref, sum_ref):
-    nodes = packed_ref.shape[0] - part_ref.shape[0]
-    sum_ref[...] = (part_ref[...].astype(F32) + packed_ref[nodes:, :].astype(F32)).astype(BF16)
+def after_add_kernel(a_ref, b_ref, *refs):
+    refs[-1][...] = (a_ref[...].astype(F32) + b_ref[...].astype(F32)).astype(BF16)
 
 
 def pull_kernel(rows, cols, tiles, place_ref, code_ref, *refs):
@@ -253,35 +235,35 @@
     output = call(output_kernel, shape((nodes, width), BF16), n_vmem=1)(pre)
 
     part = call(add_kernel, part_shape, n_vmem=2)(part, send(away, "cols", 1))
+    got = {0: back, 1: send(back, "rows", 1)}
     bit = 2
     while bit < cols:
-        part = call(add_kernel, part_shape, n_vmem=2)(part, send(part, "cols", bit))
+        order = [got[1]]
+        part = call(after_add_kernel, part_shape, n_vmem=2, n_any=len(order))(
+            part, send(part, "cols", bit), *order
+        )
         bit *= 2
 
-    got = {0: back, 1: send(back, "rows", 1)}
-    packed_shape = shape((nodes + depth + PAD, width), BF16)
     bit = rows // 2
     while bit > 1:
         for k in sorted(k for k in got if k % 2 == 0):
-            if k ^ bit == rows - 2:
-                packed = call(pack_kernel, packed_shape, n_vmem=2, n_any=1)(got[k], part, got[1])
-                got[k ^ bit] = send(packed, "rows", bit)
-            else:
-                got[k ^ bit] = send(got[k], "rows", bit)
+            got[k ^ bit] = send(got[k], "rows", bit)
         bit //= 2
     for k in range(2, rows - 2, 2):
         got[k + 1] = send(got[k], "rows", 1)
-    others = [got[k] for k in range(1, rows - 2, 2)]
-    part, packed = call(
-        repack_kernel, [part_shape, packed_shape], n_vmem=2, n_any=len(others)
-    )(got[rows - 2], part, *others)
-    got[rows - 1] = send(packed, "rows", 1)
-    part = call(unpack_kernel, part_shape, n_vmem=2)(got[rows - 1], part)
+
+    got[rows - 1] = send(got[rows - 2], "rows", 1)
+    first = [got[3]] if rows > 4 else []
+    others = [got[k] for k in range(5, rows - 2, 2)]
+    bit = rows // 2
+    while bit > 1:
+        order = others if bit == 2 else first
+        part = call(after_add_kernel, part_shape, n_vmem=2, n_any=len(order))(
+            part, send(part, "rows", bit), *order
+        )
+        bit //= 2
     after = part
-    bit = 4
-    while bit < rows:
-        part = call(add_kernel, part_shape, n_vmem=2)(part, send(part, "rows", bit))
-        bit *= 2
+    part = call(add_kernel, part_shape, n_vmem=2)(part, send(part, "rows", 1))
     half = part[:depth]
     other = send(half, "cols", 1)
 

time: 68.4 us -> 65.1 us (0.952)
  waiting for transfers between devices: 27.1 us -> 19.9 us
  starting transfers between devices: 27.8 us -> 31.6 us
    ppermute x24 -> x26, waiting for transfers between devices: 27.1 us -> 19.9 us  [send(): return lax.ppermute(x, axis, [(i, i ^ offset) for i in range(size)])]
    ppermute x24 -> x26, starting transfers between devices: 27.8 us -> 31.6 us  [send(): return lax.ppermute(x, axis, [(i, i ^ offset) for i in range(size)])]
  transfers between devices with their start and end apart: 24 -> 26, of which waited for: 14 -> 13; matrix products, arithmetic and copies ran while one was open for 0% -> 0% of each run, Pallas kernels for 5% -> 5%
where the time goes in v4:
time: 65.1 us; the launch traced here: 64.8 us
  starting transfers between devices  31.6 us (49%)
  waiting for transfers between devices  19.9 us (31%)
  Pallas kernels  8.4 us (13%)
  local copies, waits for them, and re-layouts  4.07 us (6%)
  between operations  0.77 us (1%)
    ppermute x26, starting transfers between devices, send(): return lax.ppermute(x, axis, [(i, i ^ offset) for i in range(size)])  31.6 us
    ppermute x26, waiting for transfers between devices, send(): return lax.ppermute(x, axis, [(i, i ^ offset) for i in range(size)])  19.9 us
    unnamed x16, local copies, waits for them, and re-layouts  4.06 us
    pallas_call x1, Pallas kernels, local(): pl.pallas_call(functools.partial(prepare_kernel, tiles), out_shape=[shape...  1.48 us
    pallas_call x1, Pallas kernels, local(): call(functools.partial(last_kernel, len(arrived), scale), [shape((nodes,...  1.32 us
  transfers between devices with their start and end apart: 26, of which 13 were waited for; matrix products, arithmetic and copies ran while one was open for 0% of the time, Pallas kernels for 5%

profile of v4, /device:TPU:0, one launch (start us, length us, event | category | flops | bytes accessed | tf_op | source)
XLA Modules:
  0.0 64.8 jit_solution(16339720905716589555)
XLA Ops:
  0.6 0.5 collective-permute-start
  1.1 2.6 %collective-permute-start.2 = (bf16[256,256]{1,0:T(8,128)(2,1)}, bf16[256,256]{1,0:T(8,128)(2,1)S(1)}, u32[]{:S(2)}, u32[]{:S(2)}) collective-permute-start(bf16[256,256]{1,0:T(8,128)(2,1)} %feat_ref.1), channel_id=1, source_target_pairs={{0,3},{1,2},{2,1},{3,0},{4,7},{5,6},{6,5},{7,4},{8,11},{9,10},{10,... | collective-permute-start | bytes 393224 | tf_op jit(solution)/shard_map/ppermute | solution.py:42
  3.8 0.0 collective-permute-start.1
  3.8 1.1 %copy-done = bf16[1,1,8,3,128,128]{5,4,3,2,1,0:T(8,128)(2,1)S(1)} copy-done((bf16[1,1,8,3,128,128]{5,4,3,2,1,0:T(8,128)(2,1)S(1)}, bf16[1,1,8,3,128,128]{5,4,3,2,1,0:T(8,128)(2,1)}, u32[]{:S(2)}) %copy-start) | copy-done | bytes 786456
  4.9 0.9 %copy-done.1 = bf16[256,256]{1,0:T(8,128)(2,1)S(1)} copy-done((bf16[256,256]{1,0:T(8,128)(2,1)S(1)}, bf16[256,256]{1,0:T(8,128)(2,1)}, u32[]{:S(2)}) %copy-start.1) | copy-done | bytes 131096
  5.8 0.7 %copy-done.4 = s32[1,1,8,3]{2,1,3,0:T(1,128)S(1)} copy-done((s32[1,1,8,3]{2,1,3,0:T(1,128)S(1)}, s32[1,1,8,3]{2,1,3,0:T(1,128)}, u32[]{:S(2)}) %copy-start.4) | copy-done | bytes 120
  6.5 0.7 %copy-done.5 = s32[1,1,8,3]{2,1,3,0:T(1,128)S(1)} copy-done((s32[1,1,8,3]{2,1,3,0:T(1,128)S(1)}, s32[1,1,8,3]{2,1,3,0:T(1,128)}, u32[]{:S(2)}) %copy-start.5) | copy-done | bytes 120
  7.2 0.7 %copy-done.7 = s32[1,1,8]{2,1,0:T(1,128)S(1)} copy-done((s32[1,1,8]{2,1,0:T(1,128)S(1)}, s32[1,1,8]{2,1,0:T(1,128)}, u32[]{:S(2)}) %copy-start.7) | copy-done | bytes 56
  7.9 1.5 %shard_map.111 = (bf16[8,3,128,256]{3,2,1,0:T(8,128)(2,1)S(1)}, bf16[2,256,128]{2,1,0:T(8,128)(2,1)S(1)}, s32[24]{0:T(128)S(1)}) custom-call(s32[1,3,1,8]{3,2,1,0:T(1,128)S(1)} %bitcast.8, s32[1,3,1,8]{3,2,1,0:T(1,128)S(1)} %bitcast.9, s32[1,1,8]{2,1,0:T(1,128)S(1)} %copy-done.7, bf16[256,256]{1,0:T(8,128)(2,1)S(1)} %copy-done.1, ...), custom_call_target="tpu_custom_call" | custom-call | flops 201326592 | bytes 2000000 | tf_op jit(solution)/shard_map/pallas_call | solution.py:185
  9.4 0.1 pad_add_fusion.place_ref
  9.4 0.0 collective-permute-done.refs_1_
  9.4 0.0 collective-permute-done.2.refs_3_
  9.4 1.4 %collective-permute-done.1.refs_2_ = bf16[256,256]{1,0:T(8,128)(2,1)S(1)} collective-permute-done((bf16[256,256]{1,0:T(8,128)(2,1)}, bf16[256,256]{1,0:T(8,128)(2,1)S(1)}, u32[]{:S(2)}, u32[]{:S(2)}) %collective-permute-start.1) | collective-permute-done | bytes 131104 | tf_op jit(solution)/shard_map/ppermute | solution.py:42
  10.8 1.1 %shard_map.112 = (bf16[256,256]{1,0:T(8,128)(2,1)S(1)}, bf16[256,256]{1,0:T(8,128)(2,1)S(1)}, bf16[256,256]{1,0:T(8,128)(2,1)S(1)}, bf16[256,256]{1,0:T(8,128)(2,1)S(1)}, bf16[8,256,128]{2,1,0:T(8,128)(2,1)S(1)}) custom-call(s32[2]{0:T(128)S(1)} %pad_add_fusion.place_ref, s32[24]{0:T(128)S(1)} %get-tuple-element.27.code_ref, ...), custom_call_target="tpu_custom_call" | custom-call | flops 201326592 | bytes 2000000 | tf_op jit(solution)/shard_map/pallas_call | solution.py:200
  11.9 1.8 %collective-permute-start.7 = (bf16[256,256]{1,0:T(8,128)(2,1)S(1)}, bf16[256,256]{1,0:T(8,128)(2,1)S(1)}, u32[]{:S(2)}, u32[]{:S(2)}) collective-permute-start(bf16[256,256]{1,0:T(8,128)(2,1)S(1)} %get-tuple-element.38), channel_id=1, source_target_pairs={{0,4},{4,0},{8,12},{12,8},{16,20},{20,16},{24,28},{28,24},{1,5},{5... | collective-permute-start | bytes 393224 | tf_op jit(solution)/shard_map/ppermute | solution.py:42
  13.7 0.3 collective-permute-start.4
  14.0 1.0 %shard_map.113 = (bf16[256,256]{1,0:T(8,128)(2,1)S(1)}, bf16[256,256]{1,0:T(8,128)(2,1)S(1)}, bf16[256,256]{1,0:T(8,128)(2,1)S(1)}, bf16[256,256]{1,0:T(8,128)(2,1)S(1)}) custom-call(s32[2]{0:T(128)S(1)} %pad_add_fusion.place_ref, s32[24]{0:T(128)S(1)} %get-tuple-element.27.code_ref, bf16[8,256,128]{2,1,0:T(8,128)(2,1)S(1)} %get-tuple-element.30.turned, ...), custom_call_target="tpu_custom_call" | custom-call | flops 201326592 | bytes 2000000 | tf_op jit(solution)/shard_map/pallas_call | solution.py:207
  15.0 1.8 %collective-permute-start.6 = (bf16[256,256]{1,0:T(8,128)(2,1)S(1)}, bf16[256,256]{1,0:T(8,128)(2,1)S(1)}, u32[]{:S(2)}, u32[]{:S(2)}) collective-permute-start(bf16[256,256]{1,0:T(8,128)(2,1)S(1)} %get-tuple-element.36), channel_id=1, source_target_pairs={{0,4},{4,0},{8,12},{12,8},{16,20},{20,16},{24,28},{28,24},{1,5},{5... | collective-permute-start | bytes 393224 | tf_op jit(solution)/shard_map/ppermute | solution.py:42
  16.8 1.6 %collective-permute-done.7.refs_1_ = bf16[256,256]{1,0:T(8,128)(2,1)S(1)} collective-permute-done((bf16[256,256]{1,0:T(8,128)(2,1)S(1)}, bf16[256,256]{1,0:T(8,128)(2,1)S(1)}, u32[]{:S(2)}, u32[]{:S(2)}) %collective-permute-start.7) | collective-permute-done | bytes 131104 | tf_op jit(solution)/shard_map/ppermute | solution.py:42
  18.4 1.9 %collective-permute-start.8 = (bf16[256,256]{1,0:T(8,128)(2,1)S(1)}, bf16[256,256]{1,0:T(8,128)(2,1)S(1)}, u32[]{:S(2)}, u32[]{:S(2)}) collective-permute-start(bf16[256,256]{1,0:T(8,128)(2,1)S(1)} %shard_map.115), channel_id=1, source_target_pairs={{0,8},{4,12},{8,0},{12,4},{16,24},{20,28},{24,16},{28,20},{1,9},{5... | collective-permute-start | bytes 393224 | tf_op jit(solution)/shard_map/ppermute | solution.py:42
  20.3 1.5 %collective-permute-start.3 = (bf16[256,256]{1,0:T(8,128)(2,1)S(1)}, bf16[256,256]{1,0:T(8,128)(2,1)S(1)}, u32[]{:S(2)}, u32[]{:S(2)}) collective-permute-start(bf16[256,256]{1,0:T(8,128)(2,1)S(1)} %get-tuple-element.32), channel_id=1, source_target_pairs={{0,4},{4,0},{8,12},{12,8},{16,20},{20,16},{24,28},{28,24},{1,5},{5... | collective-permute-start | bytes 393224 | tf_op jit(solution)/shard_map/ppermute | solution.py:42
  21.8 0.0 collective-permute-done.4.refs_1_
  21.9 1.2 %collective-permute-start.5 = (bf16[256,256]{1,0:T(8,128)(2,1)S(1)}, bf16[256,256]{1,0:T(8,128)(2,1)S(1)}, u32[]{:S(2)}, u32[]{:S(2)}) collective-permute-start(bf16[256,256]{1,0:T(8,128)(2,1)S(1)} %shard_map.114), channel_id=1, source_target_pairs={{0,8},{4,12},{8,0},{12,4},{16,24},{20,28},{24,16},{28,20},{1,9},{5... | collective-permute-start | bytes 393224 | tf_op jit(solution)/shard_map/ppermute | solution.py:42
  23.1 0.9 %collective-permute-done.6.refs_1_ = bf16[256,256]{1,0:T(8,128)(2,1)S(1)} collective-permute-done((bf16[256,256]{1,0:T(8,128)(2,1)S(1)}, bf16[256,256]{1,0:T(8,128)(2,1)S(1)}, u32[]{:S(2)}, u32[]{:S(2)}) %collective-permute-start.6) | collective-permute-done | bytes 131104 | tf_op jit(solution)/shard_map/ppermute | solution.py:42
  24.0 0.5 collective-permute-done.8.refs_2_
  24.5 0.1 shard_map.116
  24.6 2.3 %collective-permute-start.9 = (bf16[256,256]{1,0:T(8,128)(2,1)S(1)}, bf16[256,256]{1,0:T(8,128)(2,1)S(1)}, u32[]{:S(2)}, u32[]{:S(2)}) collective-permute-start(bf16[256,256]{1,0:T(8,128)(2,1)S(1)} %shard_map.116), channel_id=1, source_target_pairs={{0,16},{4,20},{8,24},{12,28},{16,0},{20,4},{24,8},{28,12},{1,17},{... | collective-permute-start | bytes 393224 | tf_op jit(solution)/shard_map/ppermute | solution.py:42
  26.9 0.0 collective-permute-done.3.refs_1_
  26.9 0.7 %collective-permute-done.5.refs_2_ = bf16[256,256]{1,0:T(8,128)(2,1)S(1)} collective-permute-done((bf16[256,256]{1,0:T(8,128)(2,1)S(1)}, bf16[256,256]{1,0:T(8,128)(2,1)S(1)}, u32[]{:S(2)}, u32[]{:S(2)}) %collective-permute-start.5) | collective-permute-done | bytes 131104 | tf_op jit(solution)/shard_map/ppermute | solution.py:42
  27.6 4.3 %collective-permute-done.9.refs_3_ = bf16[256,256]{1,0:T(8,128)(2,1)S(1)} collective-permute-done((bf16[256,256]{1,0:T(8,128)(2,1)S(1)}, bf16[256,256]{1,0:T(8,128)(2,1)S(1)}, u32[]{:S(2)}, u32[]{:S(2)}) %collective-permute-start.9) | collective-permute-done | bytes 131104 | tf_op jit(solution)/shard_map/ppermute | solution.py:42
  32.0 1.3 %shard_map.117 = (bf16[256,256]{1,0:T(8,128)(2,1)S(1)}, f32[256,256]{1,0:T(8,128)S(1)}, bf16[144,256]{1,0:T(8,128)(2,1)S(1)}, bf16[144,256]{1,0:T(8,128)(2,1)S(1)}) custom-call(s32[2]{0:T(128)S(1)} %pad_add_fusion.place_ref, bf16[256,256]{1,0:T(8,128)(2,1)S(1)} %get-tuple-element.31.refs_0_, bf16[256,256]{1,0:T(8,128)(2,1)S(1)} %collective-permute-done.3.refs_1_, ...), custom_call_target="tpu_custom_call" | custom-call | flops 134217728 | bytes 2000000 | tf_op jit(solution)/shard_map/pallas_call | solution.py:227
  33.2 1.0 %collective-permute-start.13 = (bf16[256,256]{1,0:T(8,128)(2,1)S(1)}, bf16[256,256]{1,0:T(8,128)(2,1)S(1)}, u32[]{:S(2)}, u32[]{:S(2)}) collective-permute-start(bf16[256,256]{1,0:T(8,128)(2,1)S(1)} %get-tuple-element.40.refs_0_), channel_id=1, source_target_pairs={{0,16},{4,20},{8,24},{12,28},{16,0},{20,4},{24,8},{28,12},{1,17},{... | collective-permute-start | bytes 393224 | tf_op jit(solution)/shard_map/ppermute | solution.py:42
  34.2 2.8 %collective-permute-start.11 = (bf16[256,256]{1,0:T(8,128)(2,1)S(1)}, bf16[256,256]{1,0:T(8,128)(2,1)S(1)}, u32[]{:S(2)}, u32[]{:S(2)}) collective-permute-start(bf16[256,256]{1,0:T(8,128)(2,1)S(1)} %get-tuple-element.40.refs_0_), channel_id=1, source_target_pairs={{0,8},{4,12},{8,0},{12,4},{16,24},{20,28},{24,16},{28,20},{1,9},{5... | collective-permute-start | bytes 393224 | tf_op jit(solution)/shard_map/ppermute | solution.py:42
  37.0 0.0 collective-permute-start.17
  37.0 1.5 %collective-permute-start.10 = (bf16[256,256]{1,0:T(8,128)(2,1)S(1)}, bf16[256,256]{1,0:T(8,128)(2,1)S(1)}, u32[]{:S(2)}, u32[]{:S(2)}) collective-permute-start(bf16[256,256]{1,0:T(8,128)(2,1)S(1)} %get-tuple-element.40.refs_0_), channel_id=1, source_target_pairs={{0,4},{4,0},{8,12},{12,8},{16,20},{20,16},{24,28},{28,24},{1,5},{5... | collective-permute-start | bytes 393224 | tf_op jit(solution)/shard_map/ppermute | solution.py:42
  38.5 2.2 %collective-permute-done.13.refs_4_ = bf16[256,256]{1,0:T(8,128)(2,1)S(1)} collective-permute-done((bf16[256,256]{1,0:T(8,128)(2,1)S(1)}, bf16[256,256]{1,0:T(8,128)(2,1)S(1)}, u32[]{:S(2)}, u32[]{:S(2)}) %collective-permute-start.13) | collective-permute-done | bytes 131104 | tf_op jit(solution)/shard_map/ppermute | solution.py:42
  40.7 0.0 collective-permute-start.15
  40.7 0.0 collective-permute-done.17.refs_1_
  40.7 1.2 %collective-permute-start.18 = (bf16[144,256]{1,0:T(8,128)(2,1)S(1)}, bf16[144,256]{1,0:T(8,128)(2,1)S(1)}, u32[]{:S(2)}, u32[]{:S(2)}) collective-permute-start(bf16[144,256]{1,0:T(8,128)(2,1)S(1)} %shard_map.119.a_ref), channel_id=1, source_target_pairs={{0,2},{1,3},{2,0},{3,1},{4,6},{5,7},{6,4},{7,5},{8,10},{9,11},{10,... | collective-permute-start | bytes 221192 | tf_op jit(solution)/shard_map/ppermute | solution.py:42
  41.9 0.0 collective-permute-done.11.refs_2_
  41.9 1.5 %collective-permute-start.12 = (bf16[256,256]{1,0:T(8,128)(2,1)S(1)}, bf16[256,256]{1,0:T(8,128)(2,1)S(1)}, u32[]{:S(2)}, u32[]{:S(2)}) collective-permute-start(bf16[256,256]{1,0:T(8,128)(2,1)S(1)} %collective-permute-done.11.refs_2_), channel_id=1, source_target_pairs={{0,4},{4,0},{8,12},{12,8},{16,20},{20,16},{24,28},{28,24},{1,5},{5... | collective-permute-start | bytes 393224 | tf_op jit(solution)/shard_map/ppermute | solution.py:42
  43.4 0.0 collective-permute-done.10.refs_0_.refs_1_
  43.4 1.7 %collective-permute-done.18.b_ref = bf16[144,256]{1,0:T(8,128)(2,1)S(1)} collective-permute-done((bf16[144,256]{1,0:T(8,128)(2,1)S(1)}, bf16[144,256]{1,0:T(8,128)(2,1)S(1)}, u32[]{:S(2)}, u32[]{:S(2)}) %collective-permute-start.18) | collective-permute-done | bytes 73760 | tf_op jit(solution)/shard_map/ppermute | solution.py:42
  45.1 2.4 %collective-permute-start.19 = (bf16[144,256]{1,0:T(8,128)(2,1)S(1)}, bf16[144,256]{1,0:T(8,128)(2,1)S(1)}, u32[]{:S(2)}, u32[]{:S(2)}) collective-permute-start(bf16[144,256]{1,0:T(8,128)(2,1)S(1)} %shard_map.120.a_ref), channel_id=1, source_target_pairs={{0,16},{4,20},{8,24},{12,28},{16,0},{20,4},{24,8},{28,12},{1,17},{... | collective-permute-start | bytes 221192 | tf_op jit(solution)/shard_map/ppermute | solution.py:42
  47.6 1.5 %collective-permute-start.14 = (bf16[256,256]{1,0:T(8,128)(2,1)S(1)}, bf16[256,256]{1,0:T(8,128)(2,1)S(1)}, u32[]{:S(2)}, u32[]{:S(2)}) collective-permute-start(bf16[256,256]{1,0:T(8,128)(2,1)S(1)} %collective-permute-done.13.refs_4_), channel_id=1, source_target_pairs={{0,4},{4,0},{8,12},{12,8},{16,20},{20,16},{24,28},{28,24},{1,5},{5... | collective-permute-start | bytes 393224 | tf_op jit(solution)/shard_map/ppermute | solution.py:42
  49.1 0.0 collective-permute-done.15.refs_6_
  49.1 0.5 collective-permute-start.16
  49.6 0.9 %collective-permute-done.19.b_ref = bf16[144,256]{1,0:T(8,128)(2,1)S(1)} collective-permute-done((bf16[144,256]{1,0:T(8,128)(2,1)S(1)}, bf16[144,256]{1,0:T(8,128)(2,1)S(1)}, u32[]{:S(2)}, u32[]{:S(2)}) %collective-permute-start.19) | collective-permute-done | bytes 73760 | tf_op jit(solution)/shard_map/ppermute | solution.py:42
  50.5 2.1 %collective-permute-start.20 = (bf16[144,256]{1,0:T(8,128)(2,1)S(1)}, bf16[144,256]{1,0:T(8,128)(2,1)S(1)}, u32[]{:S(2)}, u32[]{:S(2)}) collective-permute-start(bf16[144,256]{1,0:T(8,128)(2,1)S(1)} %shard_map.121.a_ref), channel_id=1, source_target_pairs={{0,8},{4,12},{8,0},{12,4},{16,24},{20,28},{24,16},{28,20},{1,9},{5... | collective-permute-start | bytes 221192 | tf_op jit(solution)/shard_map/ppermute | solution.py:42
  52.6 0.0 collective-permute-done.14.refs_0_.refs_5_
  52.6 2.3 %collective-permute-done.20.b_ref = bf16[144,256]{1,0:T(8,128)(2,1)S(1)} collective-permute-done((bf16[144,256]{1,0:T(8,128)(2,1)S(1)}, bf16[144,256]{1,0:T(8,128)(2,1)S(1)}, u32[]{:S(2)}, u32[]{:S(2)}) %collective-permute-start.20) | collective-permute-done | bytes 73760 | tf_op jit(solution)/shard_map/ppermute | solution.py:42
  54.9 0.0 collective-permute-done.16.refs_7_
  54.9 1.3 %shard_map.123 = (bf16[256,256]{1,0:T(8,128)(2,1)S(1)}, bf16[256,256]{1,0:T(8,128)(2,1)S(1)}, bf16[256,256]{1,0:T(8,128)(2,1)S(1)}, bf16[256,256]{1,0:T(8,128)(2,1)S(1)}) custom-call(s32[2]{0:T(128)S(1)} %pad_add_fusion.place_ref, s32[24]{0:T(128)S(1)} %get-tuple-element.27.code_ref, bf16[256,256]{1,0:T(8,128)(2,1)S(1)} %get-tuple-element.40.refs_0_, ...), custom_call_target="tpu_custom_call" | custom-call | flops 201326592 | bytes 2000000 | tf_op jit(solution)/shard_map/pallas_call | solution.py:270
  56.2 0.1 collective-permute-start.21
  56.3 1.2 %collective-permute-start.24 = (bf16[144,256]{1,0:T(8,128)(2,1)S(1)}, bf16[144,256]{1,0:T(8,128)(2,1)S(1)}, u32[]{:S(2)}, u32[]{:S(2)}) collective-permute-start(bf16[144,256]{1,0:T(8,128)(2,1)S(1)} %shard_map.122.refs_9_.refs_0_), channel_id=1, source_target_pairs={{0,4},{4,0},{8,12},{12,8},{16,20},{20,16},{24,28},{28,24},{1,5},{5... | collective-permute-start | bytes 221192 | tf_op jit(solution)/shard_map/ppermute | solution.py:42
  57.5 0.2 collective-permute-start.23
  57.7 1.6 %collective-permute-start.22 = (bf16[256,256]{1,0:T(8,128)(2,1)S(1)}, bf16[256,256]{1,0:T(8,128)(2,1)S(1)}, u32[]{:S(2)}, u32[]{:S(2)}) collective-permute-start(bf16[256,256]{1,0:T(8,128)(2,1)S(1)} %shard_map.124), channel_id=1, source_target_pairs={{0,2},{1,3},{2,0},{3,1},{4,6},{5,7},{6,4},{7,5},{8,10},{9,11},{10,... | collective-permute-start | bytes 393224 | tf_op jit(solution)/shard_map/ppermute | solution.py:42
  59.3 1.7 %collective-permute-done.24.refs_1_ = bf16[144,256]{1,0:T(8,128)(2,1)S(1)} collective-permute-done((bf16[144,256]{1,0:T(8,128)(2,1)S(1)}, bf16[144,256]{1,0:T(8,128)(2,1)S(1)}, u32[]{:S(2)}, u32[]{:S(2)}) %collective-permute-start.24) | collective-permute-done | bytes 73760 | tf_op jit(solution)/shard_map/ppermute | solution.py:42
  61.0 0.1 collective-permute-start.25
  61.1 0.7 %shard_map.118 = bf16[256,256]{1,0:T(8,128)(2,1)} custom-call(f32[256,256]{1,0:T(8,128)S(1)} %get-tuple-element.39.pre_ref), custom_call_target="tpu_custom_call" | custom-call | bytes 2000000 | tf_op jit(solution)/shard_map/pallas_call | solution.py:235
  61.8 0.5 collective-permute-done.25.refs_4_
  62.3 0.0 collective-permute-done.23.refs_2_
  62.3 1.2 %collective-permute-done.22.refs_1_ = bf16[256,256]{1,0:T(8,128)(2,1)S(1)} collective-permute-done((bf16[256,256]{1,0:T(8,128)(2,1)S(1)}, bf16[256,256]{1,0:T(8,128)(2,1)S(1)}, u32[]{:S(2)}, u32[]{:S(2)}) %collective-permute-start.22) | collective-permute-done | bytes 131104 | tf_op jit(solution)/shard_map/ppermute | solution.py:42
  63.5 1.3 %shard_map.126 = (bf16[256,256]{1,0:T(8,128)(2,1)}, f32[256,256]{1,0:T(8,128)}, f32[1,256]{1,0:T(1,128)}) custom-call(s32[2]{0:T(128)S(1)} %pad_add_fusion.place_ref, bf16[256,256]{1,0:T(8,128)(2,1)S(1)} %get-tuple-element.43.refs_0_, bf16[256,256]{1,0:T(8,128)(2,1)S(1)} %collective-permute-done.22.refs_1_, ...), custom_call_target="tpu_custom_call" | custom-call | bytes 2000000 | tf_op jit(solution)/shard_map/pallas_call | solution.py:286
  (22 shorter events, 0.2 us)
Async XLA Ops:
  0.6 8.8 %collective-permute-start = (bf16[256,256]{1,0:T(8,128)(2,1)}, bf16[256,256]{1,0:T(8,128)(2,1)S(1)}, u32[]{:S(2)}, u32[]{:S(2)}) collective-permute-start(bf16[256,256]{1,0:T(8,128)(2,1)} %feat_ref.1), channel_id=1, source_target_pairs={{0,1},{1,0},{2,3},{3,2},{4,5},{5,4},{6,7},{7,6},{8,9},{9,8},{10,11... | collective-permute-start | bytes 393224 | tf_op jit(solution)/shard_map/ppermute | solution.py:42
  1.1 8.3 %collective-permute-start.2 = (bf16[256,256]{1,0:T(8,128)(2,1)}, bf16[256,256]{1,0:T(8,128)(2,1)S(1)}, u32[]{:S(2)}, u32[]{:S(2)}) collective-permute-start(bf16[256,256]{1,0:T(8,128)(2,1)} %feat_ref.1), channel_id=1, source_target_pairs={{0,3},{1,2},{2,1},{3,0},{4,7},{5,6},{6,5},{7,4},{8,11},{9,10},{10,... | collective-permute-start | bytes 393224 | tf_op jit(solution)/shard_map/ppermute | solution.py:42
  3.8 7.1 %collective-permute-start.1 = (bf16[256,256]{1,0:T(8,128)(2,1)}, bf16[256,256]{1,0:T(8,128)(2,1)S(1)}, u32[]{:S(2)}, u32[]{:S(2)}) collective-permute-start(bf16[256,256]{1,0:T(8,128)(2,1)} %feat_ref.1), channel_id=1, source_target_pairs={{0,2},{1,3},{2,0},{3,1},{4,6},{5,7},{6,4},{7,5},{8,10},{9,11},{10,... | collective-permute-start | bytes 393224 | tf_op jit(solution)/shard_map/ppermute | solution.py:42
  3.8 1.1 %copy-start = (bf16[1,1,8,3,128,128]{5,4,3,2,1,0:T(8,128)(2,1)S(1)}, bf16[1,1,8,3,128,128]{5,4,3,2,1,0:T(8,128)(2,1)}, u32[]{:S(2)}) copy-start(bf16[1,1,8,3,128,128]{5,4,3,2,1,0:T(8,128)(2,1)} %param.11) | copy-start | bytes 2359300
  4.9 0.9 %copy-start.1 = (bf16[256,256]{1,0:T(8,128)(2,1)S(1)}, bf16[256,256]{1,0:T(8,128)(2,1)}, u32[]{:S(2)}) copy-start(bf16[256,256]{1,0:T(8,128)(2,1)} %feat_ref.1) | copy-start | bytes 393220
  5.8 0.7 %copy-start.4 = (s32[1,1,8,3]{2,1,3,0:T(1,128)S(1)}, s32[1,1,8,3]{2,1,3,0:T(1,128)}, u32[]{:S(2)}) copy-start(s32[1,1,8,3]{2,1,3,0:T(1,128)} %param.12) | copy-start | bytes 292
  6.5 0.7 %copy-start.5 = (s32[1,1,8,3]{2,1,3,0:T(1,128)S(1)}, s32[1,1,8,3]{2,1,3,0:T(1,128)}, u32[]{:S(2)}) copy-start(s32[1,1,8,3]{2,1,3,0:T(1,128)} %param.13) | copy-start | bytes 292
  7.2 0.7 %copy-start.7 = (s32[1,1,8]{2,1,0:T(1,128)S(1)}, s32[1,1,8]{2,1,0:T(1,128)}, u32[]{:S(2)}) copy-start(s32[1,1,8]{2,1,0:T(1,128)} %count_ref.1) | copy-start | bytes 100
  11.9 6.5 %collective-permute-start.7 = (bf16[256,256]{1,0:T(8,128)(2,1)S(1)}, bf16[256,256]{1,0:T(8,128)(2,1)S(1)}, u32[]{:S(2)}, u32[]{:S(2)}) collective-permute-start(bf16[256,256]{1,0:T(8,128)(2,1)S(1)} %get-tuple-element.38), channel_id=1, source_target_pairs={{0,4},{4,0},{8,12},{12,8},{16,20},{20,16},{24,28},{28,24},{1,5},{5... | collective-permute-start | bytes 393224 | tf_op jit(solution)/shard_map/ppermute | solution.py:42
  13.7 8.1 %collective-permute-start.4 = (bf16[256,256]{1,0:T(8,128)(2,1)S(1)}, bf16[256,256]{1,0:T(8,128)(2,1)S(1)}, u32[]{:S(2)}, u32[]{:S(2)}) collective-permute-start(bf16[256,256]{1,0:T(8,128)(2,1)S(1)} %get-tuple-element.34), channel_id=1, source_target_pairs={{0,4},{4,0},{8,12},{12,8},{16,20},{20,16},{24,28},{28,24},{1,5},{5... | collective-permute-start | bytes 393224 | tf_op jit(solution)/shard_map/ppermute | solution.py:42
  14.0 17.9 %copy-start.2 = (bf16[256,256]{1,0:T(8,128)(2,1)S(1)}, bf16[256,256]{1,0:T(8,128)(2,1)}, u32[]{:S(2)}) copy-start(bf16[256,256]{1,0:T(8,128)(2,1)} %refs_4_.1) | copy-start | bytes 393220
  14.0 17.9 %copy-start.3 = (bf16[256,256]{1,0:T(8,128)(2,1)S(1)}, bf16[256,256]{1,0:T(8,128)(2,1)}, u32[]{:S(2)}) copy-start(bf16[256,256]{1,0:T(8,128)(2,1)} %refs_6_.1) | copy-start | bytes 393220
  14.0 17.9 %copy-start.6 = (f32[256]{0:T(256)S(1)}, f32[256]{0:T(256)}, u32[]{:S(2)}) copy-start(f32[256]{0:T(256)} %param.10) | copy-start | bytes 3076
  15.0 9.0 %collective-permute-start.6 = (bf16[256,256]{1,0:T(8,128)(2,1)S(1)}, bf16[256,256]{1,0:T(8,128)(2,1)S(1)}, u32[]{:S(2)}, u32[]{:S(2)}) collective-permute-start(bf16[256,256]{1,0:T(8,128)(2,1)S(1)} %get-tuple-element.36), channel_id=1, source_target_pairs={{0,4},{4,0},{8,12},{12,8},{16,20},{20,16},{24,28},{28,24},{1,5},{5... | collective-permute-start | bytes 393224 | tf_op jit(solution)/shard_map/ppermute | solution.py:42
  18.4 6.1 %collective-permute-start.8 = (bf16[256,256]{1,0:T(8,128)(2,1)S(1)}, bf16[256,256]{1,0:T(8,128)(2,1)S(1)}, u32[]{:S(2)}, u32[]{:S(2)}) collective-permute-start(bf16[256,256]{1,0:T(8,128)(2,1)S(1)} %shard_map.115), channel_id=1, source_target_pairs={{0,8},{4,12},{8,0},{12,4},{16,24},{20,28},{24,16},{28,20},{1,9},{5... | collective-permute-start | bytes 393224 | tf_op jit(solution)/shard_map/ppermute | solution.py:42
  20.3 6.6 %collective-permute-start.3 = (bf16[256,256]{1,0:T(8,128)(2,1)S(1)}, bf16[256,256]{1,0:T(8,128)(2,1)S(1)}, u32[]{:S(2)}, u32[]{:S(2)}) collective-permute-start(bf16[256,256]{1,0:T(8,128)(2,1)S(1)} %get-tuple-element.32), channel_id=1, source_target_pairs={{0,4},{4,0},{8,12},{12,8},{16,20},{20,16},{24,28},{28,24},{1,5},{5... | collective-permute-start | bytes 393224 | tf_op jit(solution)/shard_map/ppermute | solution.py:42
  21.9 5.7 %collective-permute-start.5 = (bf16[256,256]{1,0:T(8,128)(2,1)S(1)}, bf16[256,256]{1,0:T(8,128)(2,1)S(1)}, u32[]{:S(2)}, u32[]{:S(2)}) collective-permute-start(bf16[256,256]{1,0:T(8,128)(2,1)S(1)} %shard_map.114), channel_id=1, source_target_pairs={{0,8},{4,12},{8,0},{12,4},{16,24},{20,28},{24,16},{28,20},{1,9},{5... | collective-permute-start | bytes 393224 | tf_op jit(solution)/shard_map/ppermute | solution.py:42
  24.6 7.3 %collective-permute-start.9 = (bf16[256,256]{1,0:T(8,128)(2,1)S(1)}, bf16[256,256]{1,0:T(8,128)(2,1)S(1)}, u32[]{:S(2)}, u32[]{:S(2)}) collective-permute-start(bf16[256,256]{1,0:T(8,128)(2,1)S(1)} %shard_map.116), channel_id=1, source_target_pairs={{0,16},{4,20},{8,24},{12,28},{16,0},{20,4},{24,8},{28,12},{1,17},{... | collective-permute-start | bytes 393224 | tf_op jit(solution)/shard_map/ppermute | solution.py:42
  33.2 7.4 %collective-permute-start.13 = (bf16[256,256]{1,0:T(8,128)(2,1)S(1)}, bf16[256,256]{1,0:T(8,128)(2,1)S(1)}, u32[]{:S(2)}, u32[]{:S(2)}) collective-permute-start(bf16[256,256]{1,0:T(8,128)(2,1)S(1)} %get-tuple-element.40.refs_0_), channel_id=1, source_target_pairs={{0,16},{4,20},{8,24},{12,28},{16,0},{20,4},{24,8},{28,12},{1,17},{... | collective-permute-start | bytes 393224 | tf_op jit(solution)/shard_map/ppermute | solution.py:42
  34.2 7.7 %collective-permute-start.11 = (bf16[256,256]{1,0:T(8,128)(2,1)S(1)}, bf16[256,256]{1,0:T(8,128)(2,1)S(1)}, u32[]{:S(2)}, u32[]{:S(2)}) collective-permute-start(bf16[256,256]{1,0:T(8,128)(2,1)S(1)} %get-tuple-element.40.refs_0_), channel_id=1, source_target_pairs={{0,8},{4,12},{8,0},{12,4},{16,24},{20,28},{24,16},{28,20},{1,9},{5... | collective-permute-start | bytes 393224 | tf_op jit(solution)/shard_map/ppermute | solution.py:42
  37.0 3.7 %collective-permute-start.17 = (bf16[144,256]{1,0:T(8,128)(2,1)S(1)}, bf16[144,256]{1,0:T(8,128)(2,1)S(1)}, u32[]{:S(2)}, u32[]{:S(2)}) collective-permute-start(bf16[144,256]{1,0:T(8,128)(2,1)S(1)} %get-tuple-element.42), channel_id=1, source_target_pairs={{0,1},{1,0},{2,3},{3,2},{4,5},{5,4},{6,7},{7,6},{8,9},{9,8},{10,11... | collective-permute-start | bytes 221192 | tf_op jit(solution)/shard_map/ppermute | solution.py:42
  37.0 6.4 %collective-permute-start.10 = (bf16[256,256]{1,0:T(8,128)(2,1)S(1)}, bf16[256,256]{1,0:T(8,128)(2,1)S(1)}, u32[]{:S(2)}, u32[]{:S(2)}) collective-permute-start(bf16[256,256]{1,0:T(8,128)(2,1)S(1)} %get-tuple-element.40.refs_0_), channel_id=1, source_target_pairs={{0,4},{4,0},{8,12},{12,8},{16,20},{20,16},{24,28},{28,24},{1,5},{5... | collective-permute-start | bytes 393224 | tf_op jit(solution)/shard_map/ppermute | solution.py:42
  40.7 8.4 %collective-permute-start.15 = (bf16[256,256]{1,0:T(8,128)(2,1)S(1)}, bf16[256,256]{1,0:T(8,128)(2,1)S(1)}, u32[]{:S(2)}, u32[]{:S(2)}) collective-permute-start(bf16[256,256]{1,0:T(8,128)(2,1)S(1)} %collective-permute-done.13.refs_4_), channel_id=1, source_target_pairs={{0,8},{4,12},{8,0},{12,4},{16,24},{20,28},{24,16},{28,20},{1,9},{5... | collective-permute-start | bytes 393224 | tf_op jit(solution)/shard_map/ppermute | solution.py:42
  40.7 4.4 %collective-permute-start.18 = (bf16[144,256]{1,0:T(8,128)(2,1)S(1)}, bf16[144,256]{1,0:T(8,128)(2,1)S(1)}, u32[]{:S(2)}, u32[]{:S(2)}) collective-permute-start(bf16[144,256]{1,0:T(8,128)(2,1)S(1)} %shard_map.119.a_ref), channel_id=1, source_target_pairs={{0,2},{1,3},{2,0},{3,1},{4,6},{5,7},{6,4},{7,5},{8,10},{9,11},{10,... | collective-permute-start | bytes 221192 | tf_op jit(solution)/shard_map/ppermute | solution.py:42
  41.9 8.6 %collective-permute-start.12 = (bf16[256,256]{1,0:T(8,128)(2,1)S(1)}, bf16[256,256]{1,0:T(8,128)(2,1)S(1)}, u32[]{:S(2)}, u32[]{:S(2)}) collective-permute-start(bf16[256,256]{1,0:T(8,128)(2,1)S(1)} %collective-permute-done.11.refs_2_), channel_id=1, source_target_pairs={{0,4},{4,0},{8,12},{12,8},{16,20},{20,16},{24,28},{28,24},{1,5},{5... | collective-permute-start | bytes 393224 | tf_op jit(solution)/shard_map/ppermute | solution.py:42
  45.1 5.3 %collective-permute-start.19 = (bf16[144,256]{1,0:T(8,128)(2,1)S(1)}, bf16[144,256]{1,0:T(8,128)(2,1)S(1)}, u32[]{:S(2)}, u32[]{:S(2)}) collective-permute-start(bf16[144,256]{1,0:T(8,128)(2,1)S(1)} %shard_map.120.a_ref), channel_id=1, source_target_pairs={{0,16},{4,20},{8,24},{12,28},{16,0},{20,4},{24,8},{28,12},{1,17},{... | collective-permute-start | bytes 221192 | tf_op jit(solution)/shard_map/ppermute | solution.py:42
  47.6 5.0 %collective-permute-start.14 = (bf16[256,256]{1,0:T(8,128)(2,1)S(1)}, bf16[256,256]{1,0:T(8,128)(2,1)S(1)}, u32[]{:S(2)}, u32[]{:S(2)}) collective-permute-start(bf16[256,256]{1,0:T(8,128)(2,1)S(1)} %collective-permute-done.13.refs_4_), channel_id=1, source_target_pairs={{0,4},{4,0},{8,12},{12,8},{16,20},{20,16},{24,28},{28,24},{1,5},{5... | collective-permute-start | bytes 393224 | tf_op jit(solution)/shard_map/ppermute | solution.py:42
  49.1 5.8 %collective-permute-start.16 = (bf16[256,256]{1,0:T(8,128)(2,1)S(1)}, bf16[256,256]{1,0:T(8,128)(2,1)S(1)}, u32[]{:S(2)}, u32[]{:S(2)}) collective-permute-start(bf16[256,256]{1,0:T(8,128)(2,1)S(1)} %collective-permute-done.15.refs_6_), channel_id=1, source_target_pairs={{0,4},{4,0},{8,12},{12,8},{16,20},{20,16},{24,28},{28,24},{1,5},{5... | collective-permute-start | bytes 393224 | tf_op jit(solution)/shard_map/ppermute | solution.py:42
  50.5 4.4 %collective-permute-start.20 = (bf16[144,256]{1,0:T(8,128)(2,1)S(1)}, bf16[144,256]{1,0:T(8,128)(2,1)S(1)}, u32[]{:S(2)}, u32[]{:S(2)}) collective-permute-start(bf16[144,256]{1,0:T(8,128)(2,1)S(1)} %shard_map.121.a_ref), channel_id=1, source_target_pairs={{0,8},{4,12},{8,0},{12,4},{16,24},{20,28},{24,16},{28,20},{1,9},{5... | collective-permute-start | bytes 221192 | tf_op jit(solution)/shard_map/ppermute | solution.py:42
  56.2 1.5 %collective-permute-start.21 = (bf16[256,256]{1,0:T(8,128)(2,1)S(1)}, bf16[256,256]{1,0:T(8,128)(2,1)S(1)}, u32[]{:S(2)}, u32[]{:S(2)}) collective-permute-start(bf16[256,256]{1,0:T(8,128)(2,1)S(1)} %get-tuple-element.45), channel_id=1, source_target_pairs={{0,1},{1,0},{2,3},{3,2},{4,5},{5,4},{6,7},{7,6},{8,9},{9,8},{10,11... | collective-permute-start | bytes 393224 | tf_op jit(solution)/shard_map/ppermute | solution.py:42
  56.3 4.7 %collective-permute-start.24 = (bf16[144,256]{1,0:T(8,128)(2,1)S(1)}, bf16[144,256]{1,0:T(8,128)(2,1)S(1)}, u32[]{:S(2)}, u32[]{:S(2)}) collective-permute-start(bf16[144,256]{1,0:T(8,128)(2,1)S(1)} %shard_map.122.refs_9_.refs_0_), channel_id=1, source_target_pairs={{0,4},{4,0},{8,12},{12,8},{16,20},{20,16},{24,28},{28,24},{1,5},{5... | collective-permute-start | bytes 221192 | tf_op jit(solution)/shard_map/ppermute | solution.py:42
  57.5 4.8 %collective-permute-start.23 = (bf16[256,256]{1,0:T(8,128)(2,1)S(1)}, bf16[256,256]{1,0:T(8,128)(2,1)S(1)}, u32[]{:S(2)}, u32[]{:S(2)}) collective-permute-start(bf16[256,256]{1,0:T(8,128)(2,1)S(1)} %get-tuple-element.46), channel_id=1, source_target_pairs={{0,1},{1,0},{2,3},{3,2},{4,5},{5,4},{6,7},{7,6},{8,9},{9,8},{10,11... | collective-permute-start | bytes 393224 | tf_op jit(solution)/shard_map/ppermute | solution.py:42
  57.7 5.8 %collective-permute-start.22 = (bf16[256,256]{1,0:T(8,128)(2,1)S(1)}, bf16[256,256]{1,0:T(8,128)(2,1)S(1)}, u32[]{:S(2)}, u32[]{:S(2)}) collective-permute-start(bf16[256,256]{1,0:T(8,128)(2,1)S(1)} %shard_map.124), channel_id=1, source_target_pairs={{0,2},{1,3},{2,0},{3,1},{4,6},{5,7},{6,4},{7,5},{8,10},{9,11},{10,... | collective-permute-start | bytes 393224 | tf_op jit(solution)/shard_map/ppermute | solution.py:42
  61.0 1.3 %collective-permute-start.25 = (bf16[128,256]{1,0:T(8,128)(2,1)S(1)}, bf16[128,256]{1,0:T(8,128)(2,1)S(1)}, u32[]{:S(2)}, u32[]{:S(2)}) collective-permute-start(bf16[128,256]{1,0:T(8,128)(2,1)S(1)} %slice.4), channel_id=1, source_target_pairs={{0,1},{1,0},{2,3},{3,2},{4,5},{5,4},{6,7},{7,6},{8,9},{9,8},{10,11... | collective-permute-start | bytes 196616 | tf_op jit(solution)/shard_map/ppermute | solution.py:42

commit v5 on v4

--- a/solution.py
+++ b/solution.py
@@ -152,10 +152,7 @@
             outs[k][t * size : (t + 1) * size, :] = total[(col ^ k) * tiles + t].astype(BF16)
 
 
-def last_kernel(n_blocks, scale, place_ref, *refs):
-    blocks = refs[:n_blocks]
-    part_ref, other_ref, in_ref, wg_ref, bg_ref = refs[n_blocks:]
-    in_ref[...] = tree_sum([b[...] for b in blocks]).astype(BF16)
+def weight_kernel(scale, place_ref, part_ref, other_ref, wg_ref, bg_ref):
     depth = other_ref.shape[0]
     mine = place_ref[1] % 2
     for which, ref in ((mine, part_ref), (1 - mine, other_ref)):
@@ -283,16 +280,13 @@
         arrived.append(send(both, "cols", k))
     arrived.append(send(blocks[1], "cols", 1))
     scale = 1.0 / math.sqrt(nodes * rows * cols)
-    input_grad, weight_grad, bias_grad = call(
-        functools.partial(last_kernel, len(arrived), scale),
-        [
-            shape((nodes, width_in), BF16),
-            shape((width_in, width), F32),
-            shape((1, width), F32),
-        ],
+    weight_grad, bias_grad = call(
+        functools.partial(weight_kernel, scale),
+        [shape((width_in, width), F32), shape((1, width), F32)],
         n_smem=1,
-        n_vmem=len(arrived) + 2,
-    )(place, *arrived, part, other)
+        n_vmem=2,
+    )(place, part, other)
+    input_grad = call(add_kernel, shape((nodes, width_in), BF16), n_vmem=len(arrived))(*arrived)
     return output, input_grad, weight_grad, bias_grad[0]
 
 

time: 65.1 us -> 64.6 us (level)
  waiting for transfers between devices: 19.9 us -> 18.7 us
  Pallas kernels: 8.4 us -> 9.07 us
    ppermute x26, waiting for transfers between devices: 19.9 us -> 18.7 us  [send(): return lax.ppermute(x, axis, [(i, i ^ offset) for i in range(size)])]
    pallas_call x1 -> x2, Pallas kernels: 1.32 us -> 1.98 us  [the longest x1 1.27 us: local(): call(functools.partial(weight_kernel, scale), [shape((width_in, width), F...]
  transfers between devices with their start and end apart: 26 -> 26, of which waited for: 13 -> 12; matrix products, arithmetic and copies ran while one was open for 0% -> 0% of each run, Pallas kernels for 5% -> 7%
where the time goes in v5:
time: 64.6 us; the launch traced here: 64.3 us
  starting transfers between devices  31.6 us (49%)
  waiting for transfers between devices  18.7 us (29%)
  Pallas kernels  9.07 us (14%)
  local copies, waits for them, and re-layouts  4.07 us (6%)
  between operations  0.78 us (1%)
    ppermute x26, starting transfers between devices, send(): return lax.ppermute(x, axis, [(i, i ^ offset) for i in range(size)])  31.6 us
    ppermute x26, waiting for transfers between devices, send(): return lax.ppermute(x, axis, [(i, i ^ offset) for i in range(size)])  18.7 us
    unnamed x16, local copies, waits for them, and re-layouts  4.06 us
    pallas_call x1, Pallas kernels, local(): pl.pallas_call(functools.partial(prepare_kernel, tiles), out_shape=[shape...  1.48 us
  transfers between devices with their start and end apart: 26, of which 12 were waited for; matrix products, arithmetic and copies ran while one was open for 0% of the time, Pallas kernels for 7%

profile of v5, /device:TPU:0, one launch (start us, length us, event | category | flops | bytes accessed | tf_op | source)
XLA Modules:
  0.0 64.3 jit_solution(4701452633890989199)
XLA Ops:
  0.6 0.5 collective-permute-start
  1.1 2.6 %collective-permute-start.2 = (bf16[256,256]{1,0:T(8,128)(2,1)}, bf16[256,256]{1,0:T(8,128)(2,1)S(1)}, u32[]{:S(2)}, u32[]{:S(2)}) collective-permute-start(bf16[256,256]{1,0:T(8,128)(2,1)} %feat_ref.1), channel_id=1, source_target_pairs={{0,3},{1,2},{2,1},{3,0},{4,7},{5,6},{6,5},{7,4},{8,11},{9,10},{10,... | collective-permute-start | bytes 393224 | tf_op jit(solution)/shard_map/ppermute | solution.py:42
  3.8 0.0 collective-permute-start.1
  3.8 1.1 %copy-done = bf16[1,1,8,3,128,128]{5,4,3,2,1,0:T(8,128)(2,1)S(1)} copy-done((bf16[1,1,8,3,128,128]{5,4,3,2,1,0:T(8,128)(2,1)S(1)}, bf16[1,1,8,3,128,128]{5,4,3,2,1,0:T(8,128)(2,1)}, u32[]{:S(2)}) %copy-start) | copy-done | bytes 786456
  4.9 0.9 %copy-done.1 = bf16[256,256]{1,0:T(8,128)(2,1)S(1)} copy-done((bf16[256,256]{1,0:T(8,128)(2,1)S(1)}, bf16[256,256]{1,0:T(8,128)(2,1)}, u32[]{:S(2)}) %copy-start.1) | copy-done | bytes 131096
  5.8 0.7 %copy-done.4 = s32[1,1,8,3]{2,1,3,0:T(1,128)S(1)} copy-done((s32[1,1,8,3]{2,1,3,0:T(1,128)S(1)}, s32[1,1,8,3]{2,1,3,0:T(1,128)}, u32[]{:S(2)}) %copy-start.4) | copy-done | bytes 120
  6.5 0.7 %copy-done.5 = s32[1,1,8,3]{2,1,3,0:T(1,128)S(1)} copy-done((s32[1,1,8,3]{2,1,3,0:T(1,128)S(1)}, s32[1,1,8,3]{2,1,3,0:T(1,128)}, u32[]{:S(2)}) %copy-start.5) | copy-done | bytes 120
  7.2 0.7 %copy-done.7 = s32[1,1,8]{2,1,0:T(1,128)S(1)} copy-done((s32[1,1,8]{2,1,0:T(1,128)S(1)}, s32[1,1,8]{2,1,0:T(1,128)}, u32[]{:S(2)}) %copy-start.7) | copy-done | bytes 56
  7.9 1.5 %shard_map.111 = (bf16[8,3,128,256]{3,2,1,0:T(8,128)(2,1)S(1)}, bf16[2,256,128]{2,1,0:T(8,128)(2,1)S(1)}, s32[24]{0:T(128)S(1)}) custom-call(s32[1,3,1,8]{3,2,1,0:T(1,128)S(1)} %bitcast.8, s32[1,3,1,8]{3,2,1,0:T(1,128)S(1)} %bitcast.9, s32[1,1,8]{2,1,0:T(1,128)S(1)} %copy-done.7, bf16[256,256]{1,0:T(8,128)(2,1)S(1)} %copy-done.1, ...), custom_call_target="tpu_custom_call" | custom-call | flops 201326592 | bytes 2000000 | tf_op jit(solution)/shard_map/pallas_call | solution.py:182
  9.4 0.1 pad_add_fusion.place_ref
  9.4 0.0 collective-permute-done.refs_1_
  9.4 0.0 collective-permute-done.2.refs_3_
  9.4 1.4 %collective-permute-done.1.refs_2_ = bf16[256,256]{1,0:T(8,128)(2,1)S(1)} collective-permute-done((bf16[256,256]{1,0:T(8,128)(2,1)}, bf16[256,256]{1,0:T(8,128)(2,1)S(1)}, u32[]{:S(2)}, u32[]{:S(2)}) %collective-permute-start.1) | collective-permute-done | bytes 131104 | tf_op jit(solution)/shard_map/ppermute | solution.py:42
  10.8 1.1 %shard_map.112 = (bf16[256,256]{1,0:T(8,128)(2,1)S(1)}, bf16[256,256]{1,0:T(8,128)(2,1)S(1)}, bf16[256,256]{1,0:T(8,128)(2,1)S(1)}, bf16[256,256]{1,0:T(8,128)(2,1)S(1)}, bf16[8,256,128]{2,1,0:T(8,128)(2,1)S(1)}) custom-call(s32[2]{0:T(128)S(1)} %pad_add_fusion.place_ref, s32[24]{0:T(128)S(1)} %get-tuple-element.26.code_ref, ...), custom_call_target="tpu_custom_call" | custom-call | flops 201326592 | bytes 2000000 | tf_op jit(solution)/shard_map/pallas_call | solution.py:197
  11.9 1.8 %collective-permute-start.7 = (bf16[256,256]{1,0:T(8,128)(2,1)S(1)}, bf16[256,256]{1,0:T(8,128)(2,1)S(1)}, u32[]{:S(2)}, u32[]{:S(2)}) collective-permute-start(bf16[256,256]{1,0:T(8,128)(2,1)S(1)} %get-tuple-element.37), channel_id=1, source_target_pairs={{0,4},{4,0},{8,12},{12,8},{16,20},{20,16},{24,28},{28,24},{1,5},{5... | collective-permute-start | bytes 393224 | tf_op jit(solution)/shard_map/ppermute | solution.py:42
  13.7 0.3 collective-permute-start.4
  14.0 1.0 %shard_map.113 = (bf16[256,256]{1,0:T(8,128)(2,1)S(1)}, bf16[256,256]{1,0:T(8,128)(2,1)S(1)}, bf16[256,256]{1,0:T(8,128)(2,1)S(1)}, bf16[256,256]{1,0:T(8,128)(2,1)S(1)}) custom-call(s32[2]{0:T(128)S(1)} %pad_add_fusion.place_ref, s32[24]{0:T(128)S(1)} %get-tuple-element.26.code_ref, bf16[8,256,128]{2,1,0:T(8,128)(2,1)S(1)} %get-tuple-element.29.turned, ...), custom_call_target="tpu_custom_call" | custom-call | flops 201326592 | bytes 2000000 | tf_op jit(solution)/shard_map/pallas_call | solution.py:204
  15.0 1.8 %collective-permute-start.6 = (bf16[256,256]{1,0:T(8,128)(2,1)S(1)}, bf16[256,256]{1,0:T(8,128)(2,1)S(1)}, u32[]{:S(2)}, u32[]{:S(2)}) collective-permute-start(bf16[256,256]{1,0:T(8,128)(2,1)S(1)} %get-tuple-element.35), channel_id=1, source_target_pairs={{0,4},{4,0},{8,12},{12,8},{16,20},{20,16},{24,28},{28,24},{1,5},{5... | collective-permute-start | bytes 393224 | tf_op jit(solution)/shard_map/ppermute | solution.py:42
  16.8 1.6 %collective-permute-done.7.refs_1_ = bf16[256,256]{1,0:T(8,128)(2,1)S(1)} collective-permute-done((bf16[256,256]{1,0:T(8,128)(2,1)S(1)}, bf16[256,256]{1,0:T(8,128)(2,1)S(1)}, u32[]{:S(2)}, u32[]{:S(2)}) %collective-permute-start.7) | collective-permute-done | bytes 131104 | tf_op jit(solution)/shard_map/ppermute | solution.py:42
  18.4 1.9 %collective-permute-start.8 = (bf16[256,256]{1,0:T(8,128)(2,1)S(1)}, bf16[256,256]{1,0:T(8,128)(2,1)S(1)}, u32[]{:S(2)}, u32[]{:S(2)}) collective-permute-start(bf16[256,256]{1,0:T(8,128)(2,1)S(1)} %shard_map.115), channel_id=1, source_target_pairs={{0,8},{4,12},{8,0},{12,4},{16,24},{20,28},{24,16},{28,20},{1,9},{5... | collective-permute-start | bytes 393224 | tf_op jit(solution)/shard_map/ppermute | solution.py:42
  20.3 1.5 %collective-permute-start.3 = (bf16[256,256]{1,0:T(8,128)(2,1)S(1)}, bf16[256,256]{1,0:T(8,128)(2,1)S(1)}, u32[]{:S(2)}, u32[]{:S(2)}) collective-permute-start(bf16[256,256]{1,0:T(8,128)(2,1)S(1)} %get-tuple-element.31), channel_id=1, source_target_pairs={{0,4},{4,0},{8,12},{12,8},{16,20},{20,16},{24,28},{28,24},{1,5},{5... | collective-permute-start | bytes 393224 | tf_op jit(solution)/shard_map/ppermute | solution.py:42
  21.8 0.0 collective-permute-done.4.refs_1_
  21.9 1.2 %collective-permute-start.5 = (bf16[256,256]{1,0:T(8,128)(2,1)S(1)}, bf16[256,256]{1,0:T(8,128)(2,1)S(1)}, u32[]{:S(2)}, u32[]{:S(2)}) collective-permute-start(bf16[256,256]{1,0:T(8,128)(2,1)S(1)} %shard_map.114), channel_id=1, source_target_pairs={{0,8},{4,12},{8,0},{12,4},{16,24},{20,28},{24,16},{28,20},{1,9},{5... | collective-permute-start | bytes 393224 | tf_op jit(solution)/shard_map/ppermute | solution.py:42
  23.1 0.9 %collective-permute-done.6.refs_1_ = bf16[256,256]{1,0:T(8,128)(2,1)S(1)} collective-permute-done((bf16[256,256]{1,0:T(8,128)(2,1)S(1)}, bf16[256,256]{1,0:T(8,128)(2,1)S(1)}, u32[]{:S(2)}, u32[]{:S(2)}) %collective-permute-start.6) | collective-permute-done | bytes 131104 | tf_op jit(solution)/shard_map/ppermute | solution.py:42
  24.0 0.5 collective-permute-done.8.refs_2_
  24.5 0.1 shard_map.116
  24.6 2.3 %collective-permute-start.9 = (bf16[256,256]{1,0:T(8,128)(2,1)S(1)}, bf16[256,256]{1,0:T(8,128)(2,1)S(1)}, u32[]{:S(2)}, u32[]{:S(2)}) collective-permute-start(bf16[256,256]{1,0:T(8,128)(2,1)S(1)} %shard_map.116), channel_id=1, source_target_pairs={{0,16},{4,20},{8,24},{12,28},{16,0},{20,4},{24,8},{28,12},{1,17},{... | collective-permute-start | bytes 393224 | tf_op jit(solution)/shard_map/ppermute | solution.py:42
  26.9 0.0 collective-permute-done.3.refs_1_
  26.9 0.7 %collective-permute-done.5.refs_2_ = bf16[256,256]{1,0:T(8,128)(2,1)S(1)} collective-permute-done((bf16[256,256]{1,0:T(8,128)(2,1)S(1)}, bf16[256,256]{1,0:T(8,128)(2,1)S(1)}, u32[]{:S(2)}, u32[]{:S(2)}) %collective-permute-start.5) | collective-permute-done | bytes 131104 | tf_op jit(solution)/shard_map/ppermute | solution.py:42
  27.6 4.3 %collective-permute-done.9.refs_3_ = bf16[256,256]{1,0:T(8,128)(2,1)S(1)} collective-permute-done((bf16[256,256]{1,0:T(8,128)(2,1)S(1)}, bf16[256,256]{1,0:T(8,128)(2,1)S(1)}, u32[]{:S(2)}, u32[]{:S(2)}) %collective-permute-start.9) | collective-permute-done | bytes 131104 | tf_op jit(solution)/shard_map/ppermute | solution.py:42
  32.0 1.3 %shard_map.117 = (bf16[256,256]{1,0:T(8,128)(2,1)S(1)}, f32[256,256]{1,0:T(8,128)S(1)}, bf16[144,256]{1,0:T(8,128)(2,1)S(1)}, bf16[144,256]{1,0:T(8,128)(2,1)S(1)}) custom-call(s32[2]{0:T(128)S(1)} %pad_add_fusion.place_ref, bf16[256,256]{1,0:T(8,128)(2,1)S(1)} %get-tuple-element.30.refs_0_, bf16[256,256]{1,0:T(8,128)(2,1)S(1)} %collective-permute-done.3.refs_1_, ...), custom_call_target="tpu_custom_call" | custom-call | flops 134217728 | bytes 2000000 | tf_op jit(solution)/shard_map/pallas_call | solution.py:224
  33.2 1.0 %collective-permute-start.13 = (bf16[256,256]{1,0:T(8,128)(2,1)S(1)}, bf16[256,256]{1,0:T(8,128)(2,1)S(1)}, u32[]{:S(2)}, u32[]{:S(2)}) collective-permute-start(bf16[256,256]{1,0:T(8,128)(2,1)S(1)} %get-tuple-element.39.refs_0_), channel_id=1, source_target_pairs={{0,16},{4,20},{8,24},{12,28},{16,0},{20,4},{24,8},{28,12},{1,17},{... | collective-permute-start | bytes 393224 | tf_op jit(solution)/shard_map/ppermute | solution.py:42
  34.2 2.8 %collective-permute-start.11 = (bf16[256,256]{1,0:T(8,128)(2,1)S(1)}, bf16[256,256]{1,0:T(8,128)(2,1)S(1)}, u32[]{:S(2)}, u32[]{:S(2)}) collective-permute-start(bf16[256,256]{1,0:T(8,128)(2,1)S(1)} %get-tuple-element.39.refs_0_), channel_id=1, source_target_pairs={{0,8},{4,12},{8,0},{12,4},{16,24},{20,28},{24,16},{28,20},{1,9},{5... | collective-permute-start | bytes 393224 | tf_op jit(solution)/shard_map/ppermute | solution.py:42
  37.0 0.0 collective-permute-start.17
  37.0 1.5 %collective-permute-start.10 = (bf16[256,256]{1,0:T(8,128)(2,1)S(1)}, bf16[256,256]{1,0:T(8,128)(2,1)S(1)}, u32[]{:S(2)}, u32[]{:S(2)}) collective-permute-start(bf16[256,256]{1,0:T(8,128)(2,1)S(1)} %get-tuple-element.39.refs_0_), channel_id=1, source_target_pairs={{0,4},{4,0},{8,12},{12,8},{16,20},{20,16},{24,28},{28,24},{1,5},{5... | collective-permute-start | bytes 393224 | tf_op jit(solution)/shard_map/ppermute | solution.py:42
  38.5 2.2 %collective-permute-done.13.refs_4_ = bf16[256,256]{1,0:T(8,128)(2,1)S(1)} collective-permute-done((bf16[256,256]{1,0:T(8,128)(2,1)S(1)}, bf16[256,256]{1,0:T(8,128)(2,1)S(1)}, u32[]{:S(2)}, u32[]{:S(2)}) %collective-permute-start.13) | collective-permute-done | bytes 131104 | tf_op jit(solution)/shard_map/ppermute | solution.py:42
  40.7 0.0 collective-permute-start.15
  40.7 0.0 collective-permute-done.17.refs_1_
  40.7 1.2 %collective-permute-start.18 = (bf16[144,256]{1,0:T(8,128)(2,1)S(1)}, bf16[144,256]{1,0:T(8,128)(2,1)S(1)}, u32[]{:S(2)}, u32[]{:S(2)}) collective-permute-start(bf16[144,256]{1,0:T(8,128)(2,1)S(1)} %shard_map.119.a_ref), channel_id=1, source_target_pairs={{0,2},{1,3},{2,0},{3,1},{4,6},{5,7},{6,4},{7,5},{8,10},{9,11},{10,... | collective-permute-start | bytes 221192 | tf_op jit(solution)/shard_map/ppermute | solution.py:42
  41.9 0.0 collective-permute-done.11.refs_2_
  41.9 1.5 %collective-permute-start.12 = (bf16[256,256]{1,0:T(8,128)(2,1)S(1)}, bf16[256,256]{1,0:T(8,128)(2,1)S(1)}, u32[]{:S(2)}, u32[]{:S(2)}) collective-permute-start(bf16[256,256]{1,0:T(8,128)(2,1)S(1)} %collective-permute-done.11.refs_2_), channel_id=1, source_target_pairs={{0,4},{4,0},{8,12},{12,8},{16,20},{20,16},{24,28},{28,24},{1,5},{5... | collective-permute-start | bytes 393224 | tf_op jit(solution)/shard_map/ppermute | solution.py:42
  43.4 0.0 collective-permute-done.10.refs_0_.refs_1_
  43.4 1.7 %collective-permute-done.18.b_ref = bf16[144,256]{1,0:T(8,128)(2,1)S(1)} collective-permute-done((bf16[144,256]{1,0:T(8,128)(2,1)S(1)}, bf16[144,256]{1,0:T(8,128)(2,1)S(1)}, u32[]{:S(2)}, u32[]{:S(2)}) %collective-permute-start.18) | collective-permute-done | bytes 73760 | tf_op jit(solution)/shard_map/ppermute | solution.py:42
  45.1 2.4 %collective-permute-start.19 = (bf16[144,256]{1,0:T(8,128)(2,1)S(1)}, bf16[144,256]{1,0:T(8,128)(2,1)S(1)}, u32[]{:S(2)}, u32[]{:S(2)}) collective-permute-start(bf16[144,256]{1,0:T(8,128)(2,1)S(1)} %shard_map.120.a_ref), channel_id=1, source_target_pairs={{0,16},{4,20},{8,24},{12,28},{16,0},{20,4},{24,8},{28,12},{1,17},{... | collective-permute-start | bytes 221192 | tf_op jit(solution)/shard_map/ppermute | solution.py:42
  47.6 1.5 %collective-permute-start.14 = (bf16[256,256]{1,0:T(8,128)(2,1)S(1)}, bf16[256,256]{1,0:T(8,128)(2,1)S(1)}, u32[]{:S(2)}, u32[]{:S(2)}) collective-permute-start(bf16[256,256]{1,0:T(8,128)(2,1)S(1)} %collective-permute-done.13.refs_4_), channel_id=1, source_target_pairs={{0,4},{4,0},{8,12},{12,8},{16,20},{20,16},{24,28},{28,24},{1,5},{5... | collective-permute-start | bytes 393224 | tf_op jit(solution)/shard_map/ppermute | solution.py:42
  49.1 0.0 collective-permute-done.15.refs_6_
  49.1 0.5 collective-permute-start.16
  49.6 0.9 %collective-permute-done.19.b_ref = bf16[144,256]{1,0:T(8,128)(2,1)S(1)} collective-permute-done((bf16[144,256]{1,0:T(8,128)(2,1)S(1)}, bf16[144,256]{1,0:T(8,128)(2,1)S(1)}, u32[]{:S(2)}, u32[]{:S(2)}) %collective-permute-start.19) | collective-permute-done | bytes 73760 | tf_op jit(solution)/shard_map/ppermute | solution.py:42
  50.5 2.1 %collective-permute-start.20 = (bf16[144,256]{1,0:T(8,128)(2,1)S(1)}, bf16[144,256]{1,0:T(8,128)(2,1)S(1)}, u32[]{:S(2)}, u32[]{:S(2)}) collective-permute-start(bf16[144,256]{1,0:T(8,128)(2,1)S(1)} %shard_map.121.a_ref), channel_id=1, source_target_pairs={{0,8},{4,12},{8,0},{12,4},{16,24},{20,28},{24,16},{28,20},{1,9},{5... | collective-permute-start | bytes 221192 | tf_op jit(solution)/shard_map/ppermute | solution.py:42
  52.6 0.0 collective-permute-done.14.refs_0_.refs_5_
  52.6 2.3 %collective-permute-done.20.b_ref = bf16[144,256]{1,0:T(8,128)(2,1)S(1)} collective-permute-done((bf16[144,256]{1,0:T(8,128)(2,1)S(1)}, bf16[144,256]{1,0:T(8,128)(2,1)S(1)}, u32[]{:S(2)}, u32[]{:S(2)}) %collective-permute-start.20) | collective-permute-done | bytes 73760 | tf_op jit(solution)/shard_map/ppermute | solution.py:42
  54.9 0.0 collective-permute-done.16.refs_7_
  54.9 1.3 %shard_map.123 = (bf16[256,256]{1,0:T(8,128)(2,1)S(1)}, bf16[256,256]{1,0:T(8,128)(2,1)S(1)}, bf16[256,256]{1,0:T(8,128)(2,1)S(1)}, bf16[256,256]{1,0:T(8,128)(2,1)S(1)}) custom-call(s32[2]{0:T(128)S(1)} %pad_add_fusion.place_ref, s32[24]{0:T(128)S(1)} %get-tuple-element.26.code_ref, bf16[256,256]{1,0:T(8,128)(2,1)S(1)} %get-tuple-element.39.refs_0_, ...), custom_call_target="tpu_custom_call" | custom-call | flops 201326592 | bytes 2000000 | tf_op jit(solution)/shard_map/pallas_call | solution.py:267
  56.2 0.1 collective-permute-start.21
  56.3 1.2 %collective-permute-start.24 = (bf16[144,256]{1,0:T(8,128)(2,1)S(1)}, bf16[144,256]{1,0:T(8,128)(2,1)S(1)}, u32[]{:S(2)}, u32[]{:S(2)}) collective-permute-start(bf16[144,256]{1,0:T(8,128)(2,1)S(1)} %shard_map.122.refs_9_.refs_0_), channel_id=1, source_target_pairs={{0,4},{4,0},{8,12},{12,8},{16,20},{20,16},{24,28},{28,24},{1,5},{5... | collective-permute-start | bytes 221192 | tf_op jit(solution)/shard_map/ppermute | solution.py:42
  57.5 0.2 collective-permute-start.23
  57.7 0.0 collective-permute-done.21.refs_1_
  57.7 1.6 %collective-permute-start.22 = (bf16[256,256]{1,0:T(8,128)(2,1)S(1)}, bf16[256,256]{1,0:T(8,128)(2,1)S(1)}, u32[]{:S(2)}, u32[]{:S(2)}) collective-permute-start(bf16[256,256]{1,0:T(8,128)(2,1)S(1)} %shard_map.124), channel_id=1, source_target_pairs={{0,2},{1,3},{2,0},{3,1},{4,6},{5,7},{6,4},{7,5},{8,10},{9,11},{10,... | collective-permute-start | bytes 393224 | tf_op jit(solution)/shard_map/ppermute | solution.py:42
  59.3 1.7 %collective-permute-done.24.refs_1_ = bf16[144,256]{1,0:T(8,128)(2,1)S(1)} collective-permute-done((bf16[144,256]{1,0:T(8,128)(2,1)S(1)}, bf16[144,256]{1,0:T(8,128)(2,1)S(1)}, u32[]{:S(2)}, u32[]{:S(2)}) %collective-permute-start.24) | collective-permute-done | bytes 73760 | tf_op jit(solution)/shard_map/ppermute | solution.py:42
  61.0 0.1 collective-permute-start.25
  61.1 0.7 %shard_map.118 = bf16[256,256]{1,0:T(8,128)(2,1)} custom-call(f32[256,256]{1,0:T(8,128)S(1)} %get-tuple-element.38.pre_ref), custom_call_target="tpu_custom_call" | custom-call | bytes 2000000 | tf_op jit(solution)/shard_map/pallas_call | solution.py:232
  61.8 0.5 collective-permute-done.25.other_ref
  62.3 1.3 %shard_map.127 = (f32[256,256]{1,0:T(8,128)}, f32[1,256]{1,0:T(1,128)}) custom-call(s32[2]{0:T(128)S(1)} %pad_add_fusion.place_ref, bf16[144,256]{1,0:T(8,128)(2,1)S(1)} %shard_map.126.part_ref, bf16[128,256]{1,0:T(8,128)(2,1)S(1)} %collective-permute-done.25.other_ref), custom_call_target="tpu_custom_call" | custom-call | bytes 2000000 | tf_op jit(solution)/shard_map/pallas_call | solution.py:283
  63.6 0.7 %shard_map.125 = bf16[256,256]{1,0:T(8,128)(2,1)} custom-call(bf16[256,256]{1,0:T(8,128)(2,1)S(1)} %get-tuple-element.42.refs_0_, bf16[256,256]{1,0:T(8,128)(2,1)S(1)} %collective-permute-done.22.refs_1_, bf16[256,256]{1,0:T(8,128)(2,1)S(1)} %collective-permute-done.23.refs_2_), custom_call_target="tpu_custom_call" | custom-call | bytes 2000000 | tf_op jit(solution)/shard_map/pallas_call | solution.py:289
  (23 shorter events, 0.2 us)
Async XLA Ops:
  0.6 8.8 %collective-permute-start = (bf16[256,256]{1,0:T(8,128)(2,1)}, bf16[256,256]{1,0:T(8,128)(2,1)S(1)}, u32[]{:S(2)}, u32[]{:S(2)}) collective-permute-start(bf16[256,256]{1,0:T(8,128)(2,1)} %feat_ref.1), channel_id=1, source_target_pairs={{0,1},{1,0},{2,3},{3,2},{4,5},{5,4},{6,7},{7,6},{8,9},{9,8},{10,11... | collective-permute-start | bytes 393224 | tf_op jit(solution)/shard_map/ppermute | solution.py:42
  1.1 8.3 %collective-permute-start.2 = (bf16[256,256]{1,0:T(8,128)(2,1)}, bf16[256,256]{1,0:T(8,128)(2,1)S(1)}, u32[]{:S(2)}, u32[]{:S(2)}) collective-permute-start(bf16[256,256]{1,0:T(8,128)(2,1)} %feat_ref.1), channel_id=1, source_target_pairs={{0,3},{1,2},{2,1},{3,0},{4,7},{5,6},{6,5},{7,4},{8,11},{9,10},{10,... | collective-permute-start | bytes 393224 | tf_op jit(solution)/shard_map/ppermute | solution.py:42
  3.8 7.1 %collective-permute-start.1 = (bf16[256,256]{1,0:T(8,128)(2,1)}, bf16[256,256]{1,0:T(8,128)(2,1)S(1)}, u32[]{:S(2)}, u32[]{:S(2)}) collective-permute-start(bf16[256,256]{1,0:T(8,128)(2,1)} %feat_ref.1), channel_id=1, source_target_pairs={{0,2},{1,3},{2,0},{3,1},{4,6},{5,7},{6,4},{7,5},{8,10},{9,11},{10,... | collective-permute-start | bytes 393224 | tf_op jit(solution)/shard_map/ppermute | solution.py:42
  3.8 1.1 %copy-start = (bf16[1,1,8,3,128,128]{5,4,3,2,1,0:T(8,128)(2,1)S(1)}, bf16[1,1,8,3,128,128]{5,4,3,2,1,0:T(8,128)(2,1)}, u32[]{:S(2)}) copy-start(bf16[1,1,8,3,128,128]{5,4,3,2,1,0:T(8,128)(2,1)} %param.11) | copy-start | bytes 2359300
  4.9 0.9 %copy-start.1 = (bf16[256,256]{1,0:T(8,128)(2,1)S(1)}, bf16[256,256]{1,0:T(8,128)(2,1)}, u32[]{:S(2)}) copy-start(bf16[256,256]{1,0:T(8,128)(2,1)} %feat_ref.1) | copy-start | bytes 393220
  5.8 0.7 %copy-start.4 = (s32[1,1,8,3]{2,1,3,0:T(1,128)S(1)}, s32[1,1,8,3]{2,1,3,0:T(1,128)}, u32[]{:S(2)}) copy-start(s32[1,1,8,3]{2,1,3,0:T(1,128)} %param.12) | copy-start | bytes 292
  6.5 0.7 %copy-start.5 = (s32[1,1,8,3]{2,1,3,0:T(1,128)S(1)}, s32[1,1,8,3]{2,1,3,0:T(1,128)}, u32[]{:S(2)}) copy-start(s32[1,1,8,3]{2,1,3,0:T(1,128)} %param.13) | copy-start | bytes 292
  7.2 0.7 %copy-start.7 = (s32[1,1,8]{2,1,0:T(1,128)S(1)}, s32[1,1,8]{2,1,0:T(1,128)}, u32[]{:S(2)}) copy-start(s32[1,1,8]{2,1,0:T(1,128)} %count_ref.1) | copy-start | bytes 100
  11.9 6.5 %collective-permute-start.7 = (bf16[256,256]{1,0:T(8,128)(2,1)S(1)}, bf16[256,256]{1,0:T(8,128)(2,1)S(1)}, u32[]{:S(2)}, u32[]{:S(2)}) collective-permute-start(bf16[256,256]{1,0:T(8,128)(2,1)S(1)} %get-tuple-element.37), channel_id=1, source_target_pairs={{0,4},{4,0},{8,12},{12,8},{16,20},{20,16},{24,28},{28,24},{1,5},{5... | collective-permute-start | bytes 393224 | tf_op jit(solution)/shard_map/ppermute | solution.py:42
  13.7 8.1 %collective-permute-start.4 = (bf16[256,256]{1,0:T(8,128)(2,1)S(1)}, bf16[256,256]{1,0:T(8,128)(2,1)S(1)}, u32[]{:S(2)}, u32[]{:S(2)}) collective-permute-start(bf16[256,256]{1,0:T(8,128)(2,1)S(1)} %get-tuple-element.33), channel_id=1, source_target_pairs={{0,4},{4,0},{8,12},{12,8},{16,20},{20,16},{24,28},{28,24},{1,5},{5... | collective-permute-start | bytes 393224 | tf_op jit(solution)/shard_map/ppermute | solution.py:42
  14.0 17.9 %copy-start.2 = (bf16[256,256]{1,0:T(8,128)(2,1)S(1)}, bf16[256,256]{1,0:T(8,128)(2,1)}, u32[]{:S(2)}) copy-start(bf16[256,256]{1,0:T(8,128)(2,1)} %refs_4_.1) | copy-start | bytes 393220
  14.0 17.9 %copy-start.3 = (bf16[256,256]{1,0:T(8,128)(2,1)S(1)}, bf16[256,256]{1,0:T(8,128)(2,1)}, u32[]{:S(2)}) copy-start(bf16[256,256]{1,0:T(8,128)(2,1)} %refs_6_.1) | copy-start | bytes 393220
  14.0 17.9 %copy-start.6 = (f32[256]{0:T(256)S(1)}, f32[256]{0:T(256)}, u32[]{:S(2)}) copy-start(f32[256]{0:T(256)} %param.10) | copy-start | bytes 3076
  15.0 9.0 %collective-permute-start.6 = (bf16[256,256]{1,0:T(8,128)(2,1)S(1)}, bf16[256,256]{1,0:T(8,128)(2,1)S(1)}, u32[]{:S(2)}, u32[]{:S(2)}) collective-permute-start(bf16[256,256]{1,0:T(8,128)(2,1)S(1)} %get-tuple-element.35), channel_id=1, source_target_pairs={{0,4},{4,0},{8,12},{12,8},{16,20},{20,16},{24,28},{28,24},{1,5},{5... | collective-permute-start | bytes 393224 | tf_op jit(solution)/shard_map/ppermute | solution.py:42
  18.4 6.1 %collective-permute-start.8 = (bf16[256,256]{1,0:T(8,128)(2,1)S(1)}, bf16[256,256]{1,0:T(8,128)(2,1)S(1)}, u32[]{:S(2)}, u32[]{:S(2)}) collective-permute-start(bf16[256,256]{1,0:T(8,128)(2,1)S(1)} %shard_map.115), channel_id=1, source_target_pairs={{0,8},{4,12},{8,0},{12,4},{16,24},{20,28},{24,16},{28,20},{1,9},{5... | collective-permute-start | bytes 393224 | tf_op jit(solution)/shard_map/ppermute | solution.py:42
  20.3 6.6 %collective-permute-start.3 = (bf16[256,256]{1,0:T(8,128)(2,1)S(1)}, bf16[256,256]{1,0:T(8,128)(2,1)S(1)}, u32[]{:S(2)}, u32[]{:S(2)}) collective-permute-start(bf16[256,256]{1,0:T(8,128)(2,1)S(1)} %get-tuple-element.31), channel_id=1, source_target_pairs={{0,4},{4,0},{8,12},{12,8},{16,20},{20,16},{24,28},{28,24},{1,5},{5... | collective-permute-start | bytes 393224 | tf_op jit(solution)/shard_map/ppermute | solution.py:42
  21.9 5.7 %collective-permute-start.5 = (bf16[256,256]{1,0:T(8,128)(2,1)S(1)}, bf16[256,256]{1,0:T(8,128)(2,1)S(1)}, u32[]{:S(2)}, u32[]{:S(2)}) collective-permute-start(bf16[256,256]{1,0:T(8,128)(2,1)S(1)} %shard_map.114), channel_id=1, source_target_pairs={{0,8},{4,12},{8,0},{12,4},{16,24},{20,28},{24,16},{28,20},{1,9},{5... | collective-permute-start | bytes 393224 | tf_op jit(solution)/shard_map/ppermute | solution.py:42
  24.6 7.3 %collective-permute-start.9 = (bf16[256,256]{1,0:T(8,128)(2,1)S(1)}, bf16[256,256]{1,0:T(8,128)(2,1)S(1)}, u32[]{:S(2)}, u32[]{:S(2)}) collective-permute-start(bf16[256,256]{1,0:T(8,128)(2,1)S(1)} %shard_map.116), channel_id=1, source_target_pairs={{0,16},{4,20},{8,24},{12,28},{16,0},{20,4},{24,8},{28,12},{1,17},{... | collective-permute-start | bytes 393224 | tf_op jit(solution)/shard_map/ppermute | solution.py:42
  33.2 7.4 %collective-permute-start.13 = (bf16[256,256]{1,0:T(8,128)(2,1)S(1)}, bf16[256,256]{1,0:T(8,128)(2,1)S(1)}, u32[]{:S(2)}, u32[]{:S(2)}) collective-permute-start(bf16[256,256]{1,0:T(8,128)(2,1)S(1)} %get-tuple-element.39.refs_0_), channel_id=1, source_target_pairs={{0,16},{4,20},{8,24},{12,28},{16,0},{20,4},{24,8},{28,12},{1,17},{... | collective-permute-start | bytes 393224 | tf_op jit(solution)/shard_map/ppermute | solution.py:42
  34.2 7.7 %collective-permute-start.11 = (bf16[256,256]{1,0:T(8,128)(2,1)S(1)}, bf16[256,256]{1,0:T(8,128)(2,1)S(1)}, u32[]{:S(2)}, u32[]{:S(2)}) collective-permute-start(bf16[256,256]{1,0:T(8,128)(2,1)S(1)} %get-tuple-element.39.refs_0_), channel_id=1, source_target_pairs={{0,8},{4,12},{8,0},{12,4},{16,24},{20,28},{24,16},{28,20},{1,9},{5... | collective-permute-start | bytes 393224 | tf_op jit(solution)/shard_map/ppermute | solution.py:42
  37.0 3.7 %collective-permute-start.17 = (bf16[144,256]{1,0:T(8,128)(2,1)S(1)}, bf16[144,256]{1,0:T(8,128)(2,1)S(1)}, u32[]{:S(2)}, u32[]{:S(2)}) collective-permute-start(bf16[144,256]{1,0:T(8,128)(2,1)S(1)} %get-tuple-element.41), channel_id=1, source_target_pairs={{0,1},{1,0},{2,3},{3,2},{4,5},{5,4},{6,7},{7,6},{8,9},{9,8},{10,11... | collective-permute-start | bytes 221192 | tf_op jit(solution)/shard_map/ppermute | solution.py:42
  37.0 6.4 %collective-permute-start.10 = (bf16[256,256]{1,0:T(8,128)(2,1)S(1)}, bf16[256,256]{1,0:T(8,128)(2,1)S(1)}, u32[]{:S(2)}, u32[]{:S(2)}) collective-permute-start(bf16[256,256]{1,0:T(8,128)(2,1)S(1)} %get-tuple-element.39.refs_0_), channel_id=1, source_target_pairs={{0,4},{4,0},{8,12},{12,8},{16,20},{20,16},{24,28},{28,24},{1,5},{5... | collective-permute-start | bytes 393224 | tf_op jit(solution)/shard_map/ppermute | solution.py:42
  40.7 8.4 %collective-permute-start.15 = (bf16[256,256]{1,0:T(8,128)(2,1)S(1)}, bf16[256,256]{1,0:T(8,128)(2,1)S(1)}, u32[]{:S(2)}, u32[]{:S(2)}) collective-permute-start(bf16[256,256]{1,0:T(8,128)(2,1)S(1)} %collective-permute-done.13.refs_4_), channel_id=1, source_target_pairs={{0,8},{4,12},{8,0},{12,4},{16,24},{20,28},{24,16},{28,20},{1,9},{5... | collective-permute-start | bytes 393224 | tf_op jit(solution)/shard_map/ppermute | solution.py:42
  40.7 4.4 %collective-permute-start.18 = (bf16[144,256]{1,0:T(8,128)(2,1)S(1)}, bf16[144,256]{1,0:T(8,128)(2,1)S(1)}, u32[]{:S(2)}, u32[]{:S(2)}) collective-permute-start(bf16[144,256]{1,0:T(8,128)(2,1)S(1)} %shard_map.119.a_ref), channel_id=1, source_target_pairs={{0,2},{1,3},{2,0},{3,1},{4,6},{5,7},{6,4},{7,5},{8,10},{9,11},{10,... | collective-permute-start | bytes 221192 | tf_op jit(solution)/shard_map/ppermute | solution.py:42
  41.9 8.6 %collective-permute-start.12 = (bf16[256,256]{1,0:T(8,128)(2,1)S(1)}, bf16[256,256]{1,0:T(8,128)(2,1)S(1)}, u32[]{:S(2)}, u32[]{:S(2)}) collective-permute-start(bf16[256,256]{1,0:T(8,128)(2,1)S(1)} %collective-permute-done.11.refs_2_), channel_id=1, source_target_pairs={{0,4},{4,0},{8,12},{12,8},{16,20},{20,16},{24,28},{28,24},{1,5},{5... | collective-permute-start | bytes 393224 | tf_op jit(solution)/shard_map/ppermute | solution.py:42
  45.1 5.3 %collective-permute-start.19 = (bf16[144,256]{1,0:T(8,128)(2,1)S(1)}, bf16[144,256]{1,0:T(8,128)(2,1)S(1)}, u32[]{:S(2)}, u32[]{:S(2)}) collective-permute-start(bf16[144,256]{1,0:T(8,128)(2,1)S(1)} %shard_map.120.a_ref), channel_id=1, source_target_pairs={{0,16},{4,20},{8,24},{12,28},{16,0},{20,4},{24,8},{28,12},{1,17},{... | collective-permute-start | bytes 221192 | tf_op jit(solution)/shard_map/ppermute | solution.py:42
  47.6 5.0 %collective-permute-start.14 = (bf16[256,256]{1,0:T(8,128)(2,1)S(1)}, bf16[256,256]{1,0:T(8,128)(2,1)S(1)}, u32[]{:S(2)}, u32[]{:S(2)}) collective-permute-start(bf16[256,256]{1,0:T(8,128)(2,1)S(1)} %collective-permute-done.13.refs_4_), channel_id=1, source_target_pairs={{0,4},{4,0},{8,12},{12,8},{16,20},{20,16},{24,28},{28,24},{1,5},{5... | collective-permute-start | bytes 393224 | tf_op jit(solution)/shard_map/ppermute | solution.py:42
  49.1 5.8 %collective-permute-start.16 = (bf16[256,256]{1,0:T(8,128)(2,1)S(1)}, bf16[256,256]{1,0:T(8,128)(2,1)S(1)}, u32[]{:S(2)}, u32[]{:S(2)}) collective-permute-start(bf16[256,256]{1,0:T(8,128)(2,1)S(1)} %collective-permute-done.15.refs_6_), channel_id=1, source_target_pairs={{0,4},{4,0},{8,12},{12,8},{16,20},{20,16},{24,28},{28,24},{1,5},{5... | collective-permute-start | bytes 393224 | tf_op jit(solution)/shard_map/ppermute | solution.py:42
  50.5 4.4 %collective-permute-start.20 = (bf16[144,256]{1,0:T(8,128)(2,1)S(1)}, bf16[144,256]{1,0:T(8,128)(2,1)S(1)}, u32[]{:S(2)}, u32[]{:S(2)}) collective-permute-start(bf16[144,256]{1,0:T(8,128)(2,1)S(1)} %shard_map.121.a_ref), channel_id=1, source_target_pairs={{0,8},{4,12},{8,0},{12,4},{16,24},{20,28},{24,16},{28,20},{1,9},{5... | collective-permute-start | bytes 221192 | tf_op jit(solution)/shard_map/ppermute | solution.py:42
  56.2 1.5 %collective-permute-start.21 = (bf16[256,256]{1,0:T(8,128)(2,1)S(1)}, bf16[256,256]{1,0:T(8,128)(2,1)S(1)}, u32[]{:S(2)}, u32[]{:S(2)}) collective-permute-start(bf16[256,256]{1,0:T(8,128)(2,1)S(1)} %get-tuple-element.44), channel_id=1, source_target_pairs={{0,1},{1,0},{2,3},{3,2},{4,5},{5,4},{6,7},{7,6},{8,9},{9,8},{10,11... | collective-permute-start | bytes 393224 | tf_op jit(solution)/shard_map/ppermute | solution.py:42
  56.3 4.7 %collective-permute-start.24 = (bf16[144,256]{1,0:T(8,128)(2,1)S(1)}, bf16[144,256]{1,0:T(8,128)(2,1)S(1)}, u32[]{:S(2)}, u32[]{:S(2)}) collective-permute-start(bf16[144,256]{1,0:T(8,128)(2,1)S(1)} %shard_map.122.refs_9_.refs_0_), channel_id=1, source_target_pairs={{0,4},{4,0},{8,12},{12,8},{16,20},{20,16},{24,28},{28,24},{1,5},{5... | collective-permute-start | bytes 221192 | tf_op jit(solution)/shard_map/ppermute | solution.py:42
  57.5 6.1 %collective-permute-start.23 = (bf16[256,256]{1,0:T(8,128)(2,1)S(1)}, bf16[256,256]{1,0:T(8,128)(2,1)S(1)}, u32[]{:S(2)}, u32[]{:S(2)}) collective-permute-start(bf16[256,256]{1,0:T(8,128)(2,1)S(1)} %get-tuple-element.45), channel_id=1, source_target_pairs={{0,1},{1,0},{2,3},{3,2},{4,5},{5,4},{6,7},{7,6},{8,9},{9,8},{10,11... | collective-permute-start | bytes 393224 | tf_op jit(solution)/shard_map/ppermute | solution.py:42
  57.7 5.9 %collective-permute-start.22 = (bf16[256,256]{1,0:T(8,128)(2,1)S(1)}, bf16[256,256]{1,0:T(8,128)(2,1)S(1)}, u32[]{:S(2)}, u32[]{:S(2)}) collective-permute-start(bf16[256,256]{1,0:T(8,128)(2,1)S(1)} %shard_map.124), channel_id=1, source_target_pairs={{0,2},{1,3},{2,0},{3,1},{4,6},{5,7},{6,4},{7,5},{8,10},{9,11},{10,... | collective-permute-start | bytes 393224 | tf_op jit(solution)/shard_map/ppermute | solution.py:42
  61.0 1.3 %collective-permute-start.25 = (bf16[128,256]{1,0:T(8,128)(2,1)S(1)}, bf16[128,256]{1,0:T(8,128)(2,1)S(1)}, u32[]{:S(2)}, u32[]{:S(2)}) collective-permute-start(bf16[128,256]{1,0:T(8,128)(2,1)S(1)} %slice.4), channel_id=1, source_target_pairs={{0,1},{1,0},{2,3},{3,2},{4,5},{5,4},{6,7},{7,6},{8,9},{9,8},{10,11... | collective-permute-start | bytes 196616 | tf_op jit(solution)/shard_map/ppermute | solution.py:42

commit v6 on v5

--- a/solution.py
+++ b/solution.py
@@ -194,22 +194,26 @@
 
     odd = list(range(rows - 1, 0, -2))
     even = list(range(rows - 2, -1, -2))
-    *sent, turned = call(
-        functools.partial(push_first_kernel, odd, tiles),
-        [block] * len(odd) + [shape((span, width_in, size), BF16)],
+    rest = [k for k in range(rows - 2, -1, -1)]
+    first, turned = call(
+        functools.partial(push_first_kernel, odd[:1], tiles),
+        [block, shape((span, width_in, size), BF16)],
         n_smem=2,
         n_vmem=cols + 1,
         flops=flops,
     )(place, code, own, *[far[k] for k in range(1, cols)], picked)
-    kept = call(
-        functools.partial(push_second_kernel, even),
-        [block] * len(even),
+    contrib = call(
+        functools.partial(push_second_kernel, rest),
+        [block] * len(rest),
         n_smem=2,
         n_vmem=2,
         flops=flops,
     )(place, code, turned, picked)
 
-    summed = {k: [kept_k, send(sent_k, "rows", 1)] for k, kept_k, sent_k in zip(even, kept, sent)}
+    contrib = dict(zip(rest, contrib))
+    contrib[odd[0]] = first
+
+    summed = {k: [contrib[k], send(contrib[k + 1], "rows", 1)] for k in even}
     bit = 2
     while bit < rows:
         for k in range(rows - bit, 0, -2 * bit):

time: 64.6 us -> 64.4 us (level)
  starting transfers between devices: 31.6 us -> 34.1 us
  waiting for transfers between devices: 18.7 us -> 16.2 us
    ppermute x26, waiting for transfers between devices: 18.7 us -> 16.2 us  [send(): return lax.ppermute(x, axis, [(i, i ^ offset) for i in range(size)])]
    ppermute x26, starting transfers between devices: 31.6 us -> 34.1 us  [send(): return lax.ppermute(x, axis, [(i, i ^ offset) for i in range(size)])]
  transfers between devices with their start and end apart: 26 -> 26, of which waited for: 12 -> 13; matrix products, arithmetic and copies ran while one was open for 0% -> 0% of each run, Pallas kernels for 7% -> 8%
where the time goes in v6:
time: 64.4 us; the launch traced here: 64.2 us
  starting transfers between devices  34.1 us (53%)
  waiting for transfers between devices  16.2 us (25%)
  Pallas kernels  9.05 us (14%)
  local copies, waits for them, and re-layouts  4.07 us (6%)
  between operations  0.77 us (1%)
    ppermute x26, starting transfers between devices, send(): return lax.ppermute(x, axis, [(i, i ^ offset) for i in range(size)])  34.1 us
    ppermute x26, waiting for transfers between devices, send(): return lax.ppermute(x, axis, [(i, i ^ offset) for i in range(size)])  16.2 us
    unnamed x16, local copies, waits for them, and re-layouts  4.06 us
    pallas_call x1, Pallas kernels, local(): pl.pallas_call(functools.partial(prepare_kernel, tiles), out_shape=[shape...  1.48 us
  transfers between devices with their start and end apart: 26, of which 13 were waited for; matrix products, arithmetic and copies ran while one was open for 0% of the time, Pallas kernels for 8%

profile of v6, /device:TPU:0, one launch (start us, length us, event | category | flops | bytes accessed | tf_op | source)
XLA Modules:
  0.0 64.2 jit_solution(16262010043246317574)
XLA Ops:
  0.6 0.5 collective-permute-start
  1.1 2.6 %collective-permute-start.2 = (bf16[256,256]{1,0:T(8,128)(2,1)}, bf16[256,256]{1,0:T(8,128)(2,1)S(1)}, u32[]{:S(2)}, u32[]{:S(2)}) collective-permute-start(bf16[256,256]{1,0:T(8,128)(2,1)} %feat_ref.1), channel_id=1, source_target_pairs={{0,3},{1,2},{2,1},{3,0},{4,7},{5,6},{6,5},{7,4},{8,11},{9,10},{10,... | collective-permute-start | bytes 393224 | tf_op jit(solution)/shard_map/ppermute | solution.py:42
  3.8 0.0 collective-permute-start.1
  3.8 1.1 %copy-done = bf16[1,1,8,3,128,128]{5,4,3,2,1,0:T(8,128)(2,1)S(1)} copy-done((bf16[1,1,8,3,128,128]{5,4,3,2,1,0:T(8,128)(2,1)S(1)}, bf16[1,1,8,3,128,128]{5,4,3,2,1,0:T(8,128)(2,1)}, u32[]{:S(2)}) %copy-start) | copy-done | bytes 786456
  4.9 0.9 %copy-done.1 = bf16[256,256]{1,0:T(8,128)(2,1)S(1)} copy-done((bf16[256,256]{1,0:T(8,128)(2,1)S(1)}, bf16[256,256]{1,0:T(8,128)(2,1)}, u32[]{:S(2)}) %copy-start.1) | copy-done | bytes 131096
  5.8 0.7 %copy-done.4 = s32[1,1,8,3]{2,1,3,0:T(1,128)S(1)} copy-done((s32[1,1,8,3]{2,1,3,0:T(1,128)S(1)}, s32[1,1,8,3]{2,1,3,0:T(1,128)}, u32[]{:S(2)}) %copy-start.4) | copy-done | bytes 120
  6.5 0.7 %copy-done.5 = s32[1,1,8,3]{2,1,3,0:T(1,128)S(1)} copy-done((s32[1,1,8,3]{2,1,3,0:T(1,128)S(1)}, s32[1,1,8,3]{2,1,3,0:T(1,128)}, u32[]{:S(2)}) %copy-start.5) | copy-done | bytes 120
  7.2 0.7 %copy-done.7 = s32[1,1,8]{2,1,0:T(1,128)S(1)} copy-done((s32[1,1,8]{2,1,0:T(1,128)S(1)}, s32[1,1,8]{2,1,0:T(1,128)}, u32[]{:S(2)}) %copy-start.7) | copy-done | bytes 56
  7.9 1.5 %shard_map.111 = (bf16[8,3,128,256]{3,2,1,0:T(8,128)(2,1)S(1)}, bf16[2,256,128]{2,1,0:T(8,128)(2,1)S(1)}, s32[24]{0:T(128)S(1)}) custom-call(s32[1,3,1,8]{3,2,1,0:T(1,128)S(1)} %bitcast.8, s32[1,3,1,8]{3,2,1,0:T(1,128)S(1)} %bitcast.9, s32[1,1,8]{2,1,0:T(1,128)S(1)} %copy-done.7, bf16[256,256]{1,0:T(8,128)(2,1)S(1)} %copy-done.1, ...), custom_call_target="tpu_custom_call" | custom-call | flops 201326592 | bytes 2000000 | tf_op jit(solution)/shard_map/pallas_call | solution.py:182
  9.4 0.1 pad_add_fusion.place_ref
  9.4 0.0 collective-permute-done.refs_1_
  9.4 0.0 collective-permute-done.2.refs_3_
  9.4 1.4 %collective-permute-done.1.refs_2_ = bf16[256,256]{1,0:T(8,128)(2,1)S(1)} collective-permute-done((bf16[256,256]{1,0:T(8,128)(2,1)}, bf16[256,256]{1,0:T(8,128)(2,1)S(1)}, u32[]{:S(2)}, u32[]{:S(2)}) %collective-permute-start.1) | collective-permute-done | bytes 131104 | tf_op jit(solution)/shard_map/ppermute | solution.py:42
  10.8 0.9 %shard_map.112 = (bf16[256,256]{1,0:T(8,128)(2,1)S(1)}, bf16[8,256,128]{2,1,0:T(8,128)(2,1)S(1)}) custom-call(s32[2]{0:T(128)S(1)} %pad_add_fusion.place_ref, s32[24]{0:T(128)S(1)} %get-tuple-element.26.code_ref, bf16[2,256,128]{2,1,0:T(8,128)(2,1)S(1)} %get-tuple-element.27.refs_0_, bf16[256,256]{1,0:T(8,128)(2,1)S(1)} %collective-permute-done.refs_1_, ...), custom_call_target="tpu_custom_call" | custom-call | flops 201326592 | bytes 2000000 | tf_op jit(solution)/shard_map/pallas_call | solution.py:198
  11.7 1.8 %collective-permute-start.7 = (bf16[256,256]{1,0:T(8,128)(2,1)S(1)}, bf16[256,256]{1,0:T(8,128)(2,1)S(1)}, u32[]{:S(2)}, u32[]{:S(2)}) collective-permute-start(bf16[256,256]{1,0:T(8,128)(2,1)S(1)} %get-tuple-element.37), channel_id=1, source_target_pairs={{0,4},{4,0},{8,12},{12,8},{16,20},{20,16},{24,28},{28,24},{1,5},{5... | collective-permute-start | bytes 393224 | tf_op jit(solution)/shard_map/ppermute | solution.py:42
  13.5 1.2 %shard_map.113 = (bf16[256,256]{1,0:T(8,128)(2,1)S(1)}, bf16[256,256]{1,0:T(8,128)(2,1)S(1)}, bf16[256,256]{1,0:T(8,128)(2,1)S(1)}, bf16[256,256]{1,0:T(8,128)(2...) custom-call(s32[2]{0:T(128)S(1)} %pad_add_fusion.place_ref, ...), custom_call_target="tpu_custom_call" | custom-call | flops 201326592 | bytes 2000000 | tf_op jit(solution)/shard_map/pallas_call | solution.py:205
  14.7 0.4 collective-permute-start.4
  15.1 1.7 %collective-permute-start.6 = (bf16[256,256]{1,0:T(8,128)(2,1)S(1)}, bf16[256,256]{1,0:T(8,128)(2,1)S(1)}, u32[]{:S(2)}, u32[]{:S(2)}) collective-permute-start(bf16[256,256]{1,0:T(8,128)(2,1)S(1)} %get-tuple-element.35), channel_id=1, source_target_pairs={{0,4},{4,0},{8,12},{12,8},{16,20},{20,16},{24,28},{28,24},{1,5},{5... | collective-permute-start | bytes 393224 | tf_op jit(solution)/shard_map/ppermute | solution.py:42
  16.8 0.6 collective-permute-done.7.refs_1_
  17.4 1.6 %collective-permute-start.8 = (bf16[256,256]{1,0:T(8,128)(2,1)S(1)}, bf16[256,256]{1,0:T(8,128)(2,1)S(1)}, u32[]{:S(2)}, u32[]{:S(2)}) collective-permute-start(bf16[256,256]{1,0:T(8,128)(2,1)S(1)} %shard_map.115), channel_id=1, source_target_pairs={{0,8},{4,12},{8,0},{12,4},{16,24},{20,28},{24,16},{28,20},{1,9},{5... | collective-permute-start | bytes 393224 | tf_op jit(solution)/shard_map/ppermute | solution.py:42
  19.0 2.5 %collective-permute-start.3 = (bf16[256,256]{1,0:T(8,128)(2,1)S(1)}, bf16[256,256]{1,0:T(8,128)(2,1)S(1)}, u32[]{:S(2)}, u32[]{:S(2)}) collective-permute-start(bf16[256,256]{1,0:T(8,128)(2,1)S(1)} %get-tuple-element.31), channel_id=1, source_target_pairs={{0,4},{4,0},{8,12},{12,8},{16,20},{20,16},{24,28},{28,24},{1,5},{5... | collective-permute-start | bytes 393224 | tf_op jit(solution)/shard_map/ppermute | solution.py:42
  21.5 0.0 collective-permute-done.4.refs_1_
  21.6 1.3 %collective-permute-start.5 = (bf16[256,256]{1,0:T(8,128)(2,1)S(1)}, bf16[256,256]{1,0:T(8,128)(2,1)S(1)}, u32[]{:S(2)}, u32[]{:S(2)}) collective-permute-start(bf16[256,256]{1,0:T(8,128)(2,1)S(1)} %shard_map.114), channel_id=1, source_target_pairs={{0,8},{4,12},{8,0},{12,4},{16,24},{20,28},{24,16},{28,20},{1,9},{5... | collective-permute-start | bytes 393224 | tf_op jit(solution)/shard_map/ppermute | solution.py:42
  22.9 1.1 %collective-permute-done.6.refs_1_ = bf16[256,256]{1,0:T(8,128)(2,1)S(1)} collective-permute-done((bf16[256,256]{1,0:T(8,128)(2,1)S(1)}, bf16[256,256]{1,0:T(8,128)(2,1)S(1)}, u32[]{:S(2)}, u32[]{:S(2)}) %collective-permute-start.6) | collective-permute-done | bytes 131104 | tf_op jit(solution)/shard_map/ppermute | solution.py:42
  24.0 0.0 collective-permute-done.8.refs_2_
  24.0 0.1 shard_map.116
  24.1 2.6 %collective-permute-start.9 = (bf16[256,256]{1,0:T(8,128)(2,1)S(1)}, bf16[256,256]{1,0:T(8,128)(2,1)S(1)}, u32[]{:S(2)}, u32[]{:S(2)}) collective-permute-start(bf16[256,256]{1,0:T(8,128)(2,1)S(1)} %shard_map.116), channel_id=1, source_target_pairs={{0,16},{4,20},{8,24},{12,28},{16,0},{20,4},{24,8},{28,12},{1,17},{... | collective-permute-start | bytes 393224 | tf_op jit(solution)/shard_map/ppermute | solution.py:42
  26.7 0.0 collective-permute-done.3.refs_1_
  26.7 0.7 %collective-permute-done.5.refs_2_ = bf16[256,256]{1,0:T(8,128)(2,1)S(1)} collective-permute-done((bf16[256,256]{1,0:T(8,128)(2,1)S(1)}, bf16[256,256]{1,0:T(8,128)(2,1)S(1)}, u32[]{:S(2)}, u32[]{:S(2)}) %collective-permute-start.5) | collective-permute-done | bytes 131104 | tf_op jit(solution)/shard_map/ppermute | solution.py:42
  27.4 4.0 %collective-permute-done.9.refs_3_ = bf16[256,256]{1,0:T(8,128)(2,1)S(1)} collective-permute-done((bf16[256,256]{1,0:T(8,128)(2,1)S(1)}, bf16[256,256]{1,0:T(8,128)(2,1)S(1)}, u32[]{:S(2)}, u32[]{:S(2)}) %collective-permute-start.9) | collective-permute-done | bytes 131104 | tf_op jit(solution)/shard_map/ppermute | solution.py:42
  31.4 1.3 %shard_map.117 = (bf16[256,256]{1,0:T(8,128)(2,1)S(1)}, f32[256,256]{1,0:T(8,128)S(1)}, bf16[144,256]{1,0:T(8,128)(2,1)S(1)}, bf16[144,256]{1,0:T(8,128)(2,1)S(1)}) custom-call(s32[2]{0:T(128)S(1)} %pad_add_fusion.place_ref, bf16[256,256]{1,0:T(8,128)(2,1)S(1)} %get-tuple-element.30.refs_0_, bf16[256,256]{1,0:T(8,128)(2,1)S(1)} %collective-permute-done.3.refs_1_, ...), custom_call_target="tpu_custom_call" | custom-call | flops 134217728 | bytes 2000000 | tf_op jit(solution)/shard_map/pallas_call | solution.py:228
  32.7 1.3 %collective-permute-start.13 = (bf16[256,256]{1,0:T(8,128)(2,1)S(1)}, bf16[256,256]{1,0:T(8,128)(2,1)S(1)}, u32[]{:S(2)}, u32[]{:S(2)}) collective-permute-start(bf16[256,256]{1,0:T(8,128)(2,1)S(1)} %get-tuple-element.39.refs_0_), channel_id=1, source_target_pairs={{0,16},{4,20},{8,24},{12,28},{16,0},{20,4},{24,8},{28,12},{1,17},{... | collective-permute-start | bytes 393224 | tf_op jit(solution)/shard_map/ppermute | solution.py:42
  34.0 2.8 %collective-permute-start.11 = (bf16[256,256]{1,0:T(8,128)(2,1)S(1)}, bf16[256,256]{1,0:T(8,128)(2,1)S(1)}, u32[]{:S(2)}, u32[]{:S(2)}) collective-permute-start(bf16[256,256]{1,0:T(8,128)(2,1)S(1)} %get-tuple-element.39.refs_0_), channel_id=1, source_target_pairs={{0,8},{4,12},{8,0},{12,4},{16,24},{20,28},{24,16},{28,20},{1,9},{5... | collective-permute-start | bytes 393224 | tf_op jit(solution)/shard_map/ppermute | solution.py:42
  36.8 0.0 collective-permute-start.17
  36.8 1.6 %collective-permute-start.10 = (bf16[256,256]{1,0:T(8,128)(2,1)S(1)}, bf16[256,256]{1,0:T(8,128)(2,1)S(1)}, u32[]{:S(2)}, u32[]{:S(2)}) collective-permute-start(bf16[256,256]{1,0:T(8,128)(2,1)S(1)} %get-tuple-element.39.refs_0_), channel_id=1, source_target_pairs={{0,4},{4,0},{8,12},{12,8},{16,20},{20,16},{24,28},{28,24},{1,5},{5... | collective-permute-start | bytes 393224 | tf_op jit(solution)/shard_map/ppermute | solution.py:42
  38.4 1.8 %collective-permute-done.13.refs_4_ = bf16[256,256]{1,0:T(8,128)(2,1)S(1)} collective-permute-done((bf16[256,256]{1,0:T(8,128)(2,1)S(1)}, bf16[256,256]{1,0:T(8,128)(2,1)S(1)}, u32[]{:S(2)}, u32[]{:S(2)}) %collective-permute-start.13) | collective-permute-done | bytes 131104 | tf_op jit(solution)/shard_map/ppermute | solution.py:42
  40.1 0.0 collective-permute-start.15
  40.1 0.0 collective-permute-done.17.refs_1_
  40.2 1.5 %collective-permute-start.18 = (bf16[144,256]{1,0:T(8,128)(2,1)S(1)}, bf16[144,256]{1,0:T(8,128)(2,1)S(1)}, u32[]{:S(2)}, u32[]{:S(2)}) collective-permute-start(bf16[144,256]{1,0:T(8,128)(2,1)S(1)} %shard_map.119.a_ref), channel_id=1, source_target_pairs={{0,2},{1,3},{2,0},{3,1},{4,6},{5,7},{6,4},{7,5},{8,10},{9,11},{10,... | collective-permute-start | bytes 221192 | tf_op jit(solution)/shard_map/ppermute | solution.py:42
  41.7 1.6 %collective-permute-start.12 = (bf16[256,256]{1,0:T(8,128)(2,1)S(1)}, bf16[256,256]{1,0:T(8,128)(2,1)S(1)}, u32[]{:S(2)}, u32[]{:S(2)}) collective-permute-start(bf16[256,256]{1,0:T(8,128)(2,1)S(1)} %collective-permute-done.11.refs_2_), channel_id=1, source_target_pairs={{0,4},{4,0},{8,12},{12,8},{16,20},{20,16},{24,28},{28,24},{1,5},{5... | collective-permute-start | bytes 393224 | tf_op jit(solution)/shard_map/ppermute | solution.py:42
  43.3 0.0 collective-permute-done.10.refs_0_.refs_1_
  43.3 1.3 %collective-permute-done.18.b_ref = bf16[144,256]{1,0:T(8,128)(2,1)S(1)} collective-permute-done((bf16[144,256]{1,0:T(8,128)(2,1)S(1)}, bf16[144,256]{1,0:T(8,128)(2,1)S(1)}, u32[]{:S(2)}, u32[]{:S(2)}) %collective-permute-start.18) | collective-permute-done | bytes 73760 | tf_op jit(solution)/shard_map/ppermute | solution.py:42
  44.6 2.8 %collective-permute-start.19 = (bf16[144,256]{1,0:T(8,128)(2,1)S(1)}, bf16[144,256]{1,0:T(8,128)(2,1)S(1)}, u32[]{:S(2)}, u32[]{:S(2)}) collective-permute-start(bf16[144,256]{1,0:T(8,128)(2,1)S(1)} %shard_map.120.a_ref), channel_id=1, source_target_pairs={{0,16},{4,20},{8,24},{12,28},{16,0},{20,4},{24,8},{28,12},{1,17},{... | collective-permute-start | bytes 221192 | tf_op jit(solution)/shard_map/ppermute | solution.py:42
  47.4 1.6 %collective-permute-start.14 = (bf16[256,256]{1,0:T(8,128)(2,1)S(1)}, bf16[256,256]{1,0:T(8,128)(2,1)S(1)}, u32[]{:S(2)}, u32[]{:S(2)}) collective-permute-start(bf16[256,256]{1,0:T(8,128)(2,1)S(1)} %collective-permute-done.13.refs_4_), channel_id=1, source_target_pairs={{0,4},{4,0},{8,12},{12,8},{16,20},{20,16},{24,28},{28,24},{1,5},{5... | collective-permute-start | bytes 393224 | tf_op jit(solution)/shard_map/ppermute | solution.py:42
  49.0 0.0 collective-permute-done.15.refs_6_
  49.0 0.4 collective-permute-start.16
  49.4 0.6 collective-permute-done.19.b_ref
  50.0 2.0 %collective-permute-start.20 = (bf16[144,256]{1,0:T(8,128)(2,1)S(1)}, bf16[144,256]{1,0:T(8,128)(2,1)S(1)}, u32[]{:S(2)}, u32[]{:S(2)}) collective-permute-start(bf16[144,256]{1,0:T(8,128)(2,1)S(1)} %shard_map.121.a_ref), channel_id=1, source_target_pairs={{0,8},{4,12},{8,0},{12,4},{16,24},{20,28},{24,16},{28,20},{1,9},{5... | collective-permute-start | bytes 221192 | tf_op jit(solution)/shard_map/ppermute | solution.py:42
  52.1 0.3 collective-permute-done.14.refs_0_.refs_5_
  52.4 2.1 %collective-permute-done.20.b_ref = bf16[144,256]{1,0:T(8,128)(2,1)S(1)} collective-permute-done((bf16[144,256]{1,0:T(8,128)(2,1)S(1)}, bf16[144,256]{1,0:T(8,128)(2,1)S(1)}, u32[]{:S(2)}, u32[]{:S(2)}) %collective-permute-start.20) | collective-permute-done | bytes 73760 | tf_op jit(solution)/shard_map/ppermute | solution.py:42
  54.5 0.0 collective-permute-done.16.refs_7_
  54.5 1.3 %shard_map.123 = (bf16[256,256]{1,0:T(8,128)(2,1)S(1)}, bf16[256,256]{1,0:T(8,128)(2,1)S(1)}, bf16[256,256]{1,0:T(8,128)(2,1)S(1)}, bf16[256,256]{1,0:T(8,128)(2,1)S(1)}) custom-call(s32[2]{0:T(128)S(1)} %pad_add_fusion.place_ref, s32[24]{0:T(128)S(1)} %get-tuple-element.26.code_ref, bf16[256,256]{1,0:T(8,128)(2,1)S(1)} %get-tuple-element.39.refs_0_, ...), custom_call_target="tpu_custom_call" | custom-call | flops 201326592 | bytes 2000000 | tf_op jit(solution)/shard_map/pallas_call | solution.py:271
  55.8 0.1 collective-permute-start.21
  55.8 1.6 %collective-permute-start.24 = (bf16[144,256]{1,0:T(8,128)(2,1)S(1)}, bf16[144,256]{1,0:T(8,128)(2,1)S(1)}, u32[]{:S(2)}, u32[]{:S(2)}) collective-permute-start(bf16[144,256]{1,0:T(8,128)(2,1)S(1)} %shard_map.122.refs_9_.refs_0_), channel_id=1, source_target_pairs={{0,4},{4,0},{8,12},{12,8},{16,20},{20,16},{24,28},{28,24},{1,5},{5... | collective-permute-start | bytes 221192 | tf_op jit(solution)/shard_map/ppermute | solution.py:42
  57.5 0.2 collective-permute-start.23
  57.7 1.4 %collective-permute-start.22 = (bf16[256,256]{1,0:T(8,128)(2,1)S(1)}, bf16[256,256]{1,0:T(8,128)(2,1)S(1)}, u32[]{:S(2)}, u32[]{:S(2)}) collective-permute-start(bf16[256,256]{1,0:T(8,128)(2,1)S(1)} %shard_map.124), channel_id=1, source_target_pairs={{0,2},{1,3},{2,0},{3,1},{4,6},{5,7},{6,4},{7,5},{8,10},{9,11},{10,... | collective-permute-start | bytes 393224 | tf_op jit(solution)/shard_map/ppermute | solution.py:42
  59.1 1.4 %collective-permute-done.24.refs_1_ = bf16[144,256]{1,0:T(8,128)(2,1)S(1)} collective-permute-done((bf16[144,256]{1,0:T(8,128)(2,1)S(1)}, bf16[144,256]{1,0:T(8,128)(2,1)S(1)}, u32[]{:S(2)}, u32[]{:S(2)}) %collective-permute-start.24) | collective-permute-done | bytes 73760 | tf_op jit(solution)/shard_map/ppermute | solution.py:42
  60.6 0.1 collective-permute-start.25
  60.6 0.7 %shard_map.118 = bf16[256,256]{1,0:T(8,128)(2,1)} custom-call(f32[256,256]{1,0:T(8,128)S(1)} %get-tuple-element.38.pre_ref), custom_call_target="tpu_custom_call" | custom-call | bytes 2000000 | tf_op jit(solution)/shard_map/pallas_call | solution.py:236
  61.4 0.5 collective-permute-done.25.other_ref
  61.9 1.3 %shard_map.127 = (f32[256,256]{1,0:T(8,128)}, f32[1,256]{1,0:T(1,128)}) custom-call(s32[2]{0:T(128)S(1)} %pad_add_fusion.place_ref, bf16[144,256]{1,0:T(8,128)(2,1)S(1)} %shard_map.126.part_ref, bf16[128,256]{1,0:T(8,128)(2,1)S(1)} %collective-permute-done.25.other_ref), custom_call_target="tpu_custom_call" | custom-call | bytes 2000000 | tf_op jit(solution)/shard_map/pallas_call | solution.py:287
  63.2 0.0 collective-permute-done.23.refs_2_
  63.2 0.3 collective-permute-done.22.refs_1_
  63.5 0.7 %shard_map.125 = bf16[256,256]{1,0:T(8,128)(2,1)} custom-call(bf16[256,256]{1,0:T(8,128)(2,1)S(1)} %get-tuple-element.42.refs_0_, bf16[256,256]{1,0:T(8,128)(2,1)S(1)} %collective-permute-done.22.refs_1_, bf16[256,256]{1,0:T(8,128)(2,1)S(1)} %collective-permute-done.23.refs_2_), custom_call_target="tpu_custom_call" | custom-call | bytes 2000000 | tf_op jit(solution)/shard_map/pallas_call | solution.py:293
  (23 shorter events, 0.2 us)
Async XLA Ops:
  0.6 8.8 %collective-permute-start = (bf16[256,256]{1,0:T(8,128)(2,1)}, bf16[256,256]{1,0:T(8,128)(2,1)S(1)}, u32[]{:S(2)}, u32[]{:S(2)}) collective-permute-start(bf16[256,256]{1,0:T(8,128)(2,1)} %feat_ref.1), channel_id=1, source_target_pairs={{0,1},{1,0},{2,3},{3,2},{4,5},{5,4},{6,7},{7,6},{8,9},{9,8},{10,11... | collective-permute-start | bytes 393224 | tf_op jit(solution)/shard_map/ppermute | solution.py:42
  1.1 8.3 %collective-permute-start.2 = (bf16[256,256]{1,0:T(8,128)(2,1)}, bf16[256,256]{1,0:T(8,128)(2,1)S(1)}, u32[]{:S(2)}, u32[]{:S(2)}) collective-permute-start(bf16[256,256]{1,0:T(8,128)(2,1)} %feat_ref.1), channel_id=1, source_target_pairs={{0,3},{1,2},{2,1},{3,0},{4,7},{5,6},{6,5},{7,4},{8,11},{9,10},{10,... | collective-permute-start | bytes 393224 | tf_op jit(solution)/shard_map/ppermute | solution.py:42
  3.8 7.1 %collective-permute-start.1 = (bf16[256,256]{1,0:T(8,128)(2,1)}, bf16[256,256]{1,0:T(8,128)(2,1)S(1)}, u32[]{:S(2)}, u32[]{:S(2)}) collective-permute-start(bf16[256,256]{1,0:T(8,128)(2,1)} %feat_ref.1), channel_id=1, source_target_pairs={{0,2},{1,3},{2,0},{3,1},{4,6},{5,7},{6,4},{7,5},{8,10},{9,11},{10,... | collective-permute-start | bytes 393224 | tf_op jit(solution)/shard_map/ppermute | solution.py:42
  3.8 1.1 %copy-start = (bf16[1,1,8,3,128,128]{5,4,3,2,1,0:T(8,128)(2,1)S(1)}, bf16[1,1,8,3,128,128]{5,4,3,2,1,0:T(8,128)(2,1)}, u32[]{:S(2)}) copy-start(bf16[1,1,8,3,128,128]{5,4,3,2,1,0:T(8,128)(2,1)} %param.11) | copy-start | bytes 2359300
  4.9 0.9 %copy-start.1 = (bf16[256,256]{1,0:T(8,128)(2,1)S(1)}, bf16[256,256]{1,0:T(8,128)(2,1)}, u32[]{:S(2)}) copy-start(bf16[256,256]{1,0:T(8,128)(2,1)} %feat_ref.1) | copy-start | bytes 393220
  5.8 0.7 %copy-start.4 = (s32[1,1,8,3]{2,1,3,0:T(1,128)S(1)}, s32[1,1,8,3]{2,1,3,0:T(1,128)}, u32[]{:S(2)}) copy-start(s32[1,1,8,3]{2,1,3,0:T(1,128)} %param.12) | copy-start | bytes 292
  6.5 0.7 %copy-start.5 = (s32[1,1,8,3]{2,1,3,0:T(1,128)S(1)}, s32[1,1,8,3]{2,1,3,0:T(1,128)}, u32[]{:S(2)}) copy-start(s32[1,1,8,3]{2,1,3,0:T(1,128)} %param.13) | copy-start | bytes 292
  7.2 0.7 %copy-start.7 = (s32[1,1,8]{2,1,0:T(1,128)S(1)}, s32[1,1,8]{2,1,0:T(1,128)}, u32[]{:S(2)}) copy-start(s32[1,1,8]{2,1,0:T(1,128)} %count_ref.1) | copy-start | bytes 100
  11.7 5.7 %collective-permute-start.7 = (bf16[256,256]{1,0:T(8,128)(2,1)S(1)}, bf16[256,256]{1,0:T(8,128)(2,1)S(1)}, u32[]{:S(2)}, u32[]{:S(2)}) collective-permute-start(bf16[256,256]{1,0:T(8,128)(2,1)S(1)} %get-tuple-element.37), channel_id=1, source_target_pairs={{0,4},{4,0},{8,12},{12,8},{16,20},{20,16},{24,28},{28,24},{1,5},{5... | collective-permute-start | bytes 393224 | tf_op jit(solution)/shard_map/ppermute | solution.py:42
  13.5 17.9 %copy-start.2 = (bf16[256,256]{1,0:T(8,128)(2,1)S(1)}, bf16[256,256]{1,0:T(8,128)(2,1)}, u32[]{:S(2)}) copy-start(bf16[256,256]{1,0:T(8,128)(2,1)} %refs_4_.1) | copy-start | bytes 393220
  13.5 17.9 %copy-start.3 = (bf16[256,256]{1,0:T(8,128)(2,1)S(1)}, bf16[256,256]{1,0:T(8,128)(2,1)}, u32[]{:S(2)}) copy-start(bf16[256,256]{1,0:T(8,128)(2,1)} %refs_6_.1) | copy-start | bytes 393220
  13.5 17.9 %copy-start.6 = (f32[256]{0:T(256)S(1)}, f32[256]{0:T(256)}, u32[]{:S(2)}) copy-start(f32[256]{0:T(256)} %param.10) | copy-start | bytes 3076
  14.7 6.8 %collective-permute-start.4 = (bf16[256,256]{1,0:T(8,128)(2,1)S(1)}, bf16[256,256]{1,0:T(8,128)(2,1)S(1)}, u32[]{:S(2)}, u32[]{:S(2)}) collective-permute-start(bf16[256,256]{1,0:T(8,128)(2,1)S(1)} %get-tuple-element.33), channel_id=1, source_target_pairs={{0,4},{4,0},{8,12},{12,8},{16,20},{20,16},{24,28},{28,24},{1,5},{5... | collective-permute-start | bytes 393224 | tf_op jit(solution)/shard_map/ppermute | solution.py:42
  15.1 9.0 %collective-permute-start.6 = (bf16[256,256]{1,0:T(8,128)(2,1)S(1)}, bf16[256,256]{1,0:T(8,128)(2,1)S(1)}, u32[]{:S(2)}, u32[]{:S(2)}) collective-permute-start(bf16[256,256]{1,0:T(8,128)(2,1)S(1)} %get-tuple-element.35), channel_id=1, source_target_pairs={{0,4},{4,0},{8,12},{12,8},{16,20},{20,16},{24,28},{28,24},{1,5},{5... | collective-permute-start | bytes 393224 | tf_op jit(solution)/shard_map/ppermute | solution.py:42
  17.4 6.6 %collective-permute-start.8 = (bf16[256,256]{1,0:T(8,128)(2,1)S(1)}, bf16[256,256]{1,0:T(8,128)(2,1)S(1)}, u32[]{:S(2)}, u32[]{:S(2)}) collective-permute-start(bf16[256,256]{1,0:T(8,128)(2,1)S(1)} %shard_map.115), channel_id=1, source_target_pairs={{0,8},{4,12},{8,0},{12,4},{16,24},{20,28},{24,16},{28,20},{1,9},{5... | collective-permute-start | bytes 393224 | tf_op jit(solution)/shard_map/ppermute | solution.py:42
  19.0 7.7 %collective-permute-start.3 = (bf16[256,256]{1,0:T(8,128)(2,1)S(1)}, bf16[256,256]{1,0:T(8,128)(2,1)S(1)}, u32[]{:S(2)}, u32[]{:S(2)}) collective-permute-start(bf16[256,256]{1,0:T(8,128)(2,1)S(1)} %get-tuple-element.31), channel_id=1, source_target_pairs={{0,4},{4,0},{8,12},{12,8},{16,20},{20,16},{24,28},{28,24},{1,5},{5... | collective-permute-start | bytes 393224 | tf_op jit(solution)/shard_map/ppermute | solution.py:42
  21.6 5.9 %collective-permute-start.5 = (bf16[256,256]{1,0:T(8,128)(2,1)S(1)}, bf16[256,256]{1,0:T(8,128)(2,1)S(1)}, u32[]{:S(2)}, u32[]{:S(2)}) collective-permute-start(bf16[256,256]{1,0:T(8,128)(2,1)S(1)} %shard_map.114), channel_id=1, source_target_pairs={{0,8},{4,12},{8,0},{12,4},{16,24},{20,28},{24,16},{28,20},{1,9},{5... | collective-permute-start | bytes 393224 | tf_op jit(solution)/shard_map/ppermute | solution.py:42
  24.1 7.3 %collective-permute-start.9 = (bf16[256,256]{1,0:T(8,128)(2,1)S(1)}, bf16[256,256]{1,0:T(8,128)(2,1)S(1)}, u32[]{:S(2)}, u32[]{:S(2)}) collective-permute-start(bf16[256,256]{1,0:T(8,128)(2,1)S(1)} %shard_map.116), channel_id=1, source_target_pairs={{0,16},{4,20},{8,24},{12,28},{16,0},{20,4},{24,8},{28,12},{1,17},{... | collective-permute-start | bytes 393224 | tf_op jit(solution)/shard_map/ppermute | solution.py:42
  32.7 7.4 %collective-permute-start.13 = (bf16[256,256]{1,0:T(8,128)(2,1)S(1)}, bf16[256,256]{1,0:T(8,128)(2,1)S(1)}, u32[]{:S(2)}, u32[]{:S(2)}) collective-permute-start(bf16[256,256]{1,0:T(8,128)(2,1)S(1)} %get-tuple-element.39.refs_0_), channel_id=1, source_target_pairs={{0,16},{4,20},{8,24},{12,28},{16,0},{20,4},{24,8},{28,12},{1,17},{... | collective-permute-start | bytes 393224 | tf_op jit(solution)/shard_map/ppermute | solution.py:42
  34.0 7.7 %collective-permute-start.11 = (bf16[256,256]{1,0:T(8,128)(2,1)S(1)}, bf16[256,256]{1,0:T(8,128)(2,1)S(1)}, u32[]{:S(2)}, u32[]{:S(2)}) collective-permute-start(bf16[256,256]{1,0:T(8,128)(2,1)S(1)} %get-tuple-element.39.refs_0_), channel_id=1, source_target_pairs={{0,8},{4,12},{8,0},{12,4},{16,24},{20,28},{24,16},{28,20},{1,9},{5... | collective-permute-start | bytes 393224 | tf_op jit(solution)/shard_map/ppermute | solution.py:42
  36.8 3.4 %collective-permute-start.17 = (bf16[144,256]{1,0:T(8,128)(2,1)S(1)}, bf16[144,256]{1,0:T(8,128)(2,1)S(1)}, u32[]{:S(2)}, u32[]{:S(2)}) collective-permute-start(bf16[144,256]{1,0:T(8,128)(2,1)S(1)} %get-tuple-element.41), channel_id=1, source_target_pairs={{0,1},{1,0},{2,3},{3,2},{4,5},{5,4},{6,7},{7,6},{8,9},{9,8},{10,11... | collective-permute-start | bytes 221192 | tf_op jit(solution)/shard_map/ppermute | solution.py:42
  36.8 6.5 %collective-permute-start.10 = (bf16[256,256]{1,0:T(8,128)(2,1)S(1)}, bf16[256,256]{1,0:T(8,128)(2,1)S(1)}, u32[]{:S(2)}, u32[]{:S(2)}) collective-permute-start(bf16[256,256]{1,0:T(8,128)(2,1)S(1)} %get-tuple-element.39.refs_0_), channel_id=1, source_target_pairs={{0,4},{4,0},{8,12},{12,8},{16,20},{20,16},{24,28},{28,24},{1,5},{5... | collective-permute-start | bytes 393224 | tf_op jit(solution)/shard_map/ppermute | solution.py:42
  40.1 8.8 %collective-permute-start.15 = (bf16[256,256]{1,0:T(8,128)(2,1)S(1)}, bf16[256,256]{1,0:T(8,128)(2,1)S(1)}, u32[]{:S(2)}, u32[]{:S(2)}) collective-permute-start(bf16[256,256]{1,0:T(8,128)(2,1)S(1)} %collective-permute-done.13.refs_4_), channel_id=1, source_target_pairs={{0,8},{4,12},{8,0},{12,4},{16,24},{20,28},{24,16},{28,20},{1,9},{5... | collective-permute-start | bytes 393224 | tf_op jit(solution)/shard_map/ppermute | solution.py:42
  40.2 4.4 %collective-permute-start.18 = (bf16[144,256]{1,0:T(8,128)(2,1)S(1)}, bf16[144,256]{1,0:T(8,128)(2,1)S(1)}, u32[]{:S(2)}, u32[]{:S(2)}) collective-permute-start(bf16[144,256]{1,0:T(8,128)(2,1)S(1)} %shard_map.119.a_ref), channel_id=1, source_target_pairs={{0,2},{1,3},{2,0},{3,1},{4,6},{5,7},{6,4},{7,5},{8,10},{9,11},{10,... | collective-permute-start | bytes 221192 | tf_op jit(solution)/shard_map/ppermute | solution.py:42
  41.7 8.3 %collective-permute-start.12 = (bf16[256,256]{1,0:T(8,128)(2,1)S(1)}, bf16[256,256]{1,0:T(8,128)(2,1)S(1)}, u32[]{:S(2)}, u32[]{:S(2)}) collective-permute-start(bf16[256,256]{1,0:T(8,128)(2,1)S(1)} %collective-permute-done.11.refs_2_), channel_id=1, source_target_pairs={{0,4},{4,0},{8,12},{12,8},{16,20},{20,16},{24,28},{28,24},{1,5},{5... | collective-permute-start | bytes 393224 | tf_op jit(solution)/shard_map/ppermute | solution.py:42
  44.6 5.4 %collective-permute-start.19 = (bf16[144,256]{1,0:T(8,128)(2,1)S(1)}, bf16[144,256]{1,0:T(8,128)(2,1)S(1)}, u32[]{:S(2)}, u32[]{:S(2)}) collective-permute-start(bf16[144,256]{1,0:T(8,128)(2,1)S(1)} %shard_map.120.a_ref), channel_id=1, source_target_pairs={{0,16},{4,20},{8,24},{12,28},{16,0},{20,4},{24,8},{28,12},{1,17},{... | collective-permute-start | bytes 221192 | tf_op jit(solution)/shard_map/ppermute | solution.py:42
  47.4 5.0 %collective-permute-start.14 = (bf16[256,256]{1,0:T(8,128)(2,1)S(1)}, bf16[256,256]{1,0:T(8,128)(2,1)S(1)}, u32[]{:S(2)}, u32[]{:S(2)}) collective-permute-start(bf16[256,256]{1,0:T(8,128)(2,1)S(1)} %collective-permute-done.13.refs_4_), channel_id=1, source_target_pairs={{0,4},{4,0},{8,12},{12,8},{16,20},{20,16},{24,28},{28,24},{1,5},{5... | collective-permute-start | bytes 393224 | tf_op jit(solution)/shard_map/ppermute | solution.py:42
  49.0 5.5 %collective-permute-start.16 = (bf16[256,256]{1,0:T(8,128)(2,1)S(1)}, bf16[256,256]{1,0:T(8,128)(2,1)S(1)}, u32[]{:S(2)}, u32[]{:S(2)}) collective-permute-start(bf16[256,256]{1,0:T(8,128)(2,1)S(1)} %collective-permute-done.15.refs_6_), channel_id=1, source_target_pairs={{0,4},{4,0},{8,12},{12,8},{16,20},{20,16},{24,28},{28,24},{1,5},{5... | collective-permute-start | bytes 393224 | tf_op jit(solution)/shard_map/ppermute | solution.py:42
  50.0 4.4 %collective-permute-start.20 = (bf16[144,256]{1,0:T(8,128)(2,1)S(1)}, bf16[144,256]{1,0:T(8,128)(2,1)S(1)}, u32[]{:S(2)}, u32[]{:S(2)}) collective-permute-start(bf16[144,256]{1,0:T(8,128)(2,1)S(1)} %shard_map.121.a_ref), channel_id=1, source_target_pairs={{0,8},{4,12},{8,0},{12,4},{16,24},{20,28},{24,16},{28,20},{1,9},{5... | collective-permute-start | bytes 221192 | tf_op jit(solution)/shard_map/ppermute | solution.py:42
  55.8 1.9 %collective-permute-start.21 = (bf16[256,256]{1,0:T(8,128)(2,1)S(1)}, bf16[256,256]{1,0:T(8,128)(2,1)S(1)}, u32[]{:S(2)}, u32[]{:S(2)}) collective-permute-start(bf16[256,256]{1,0:T(8,128)(2,1)S(1)} %get-tuple-element.44), channel_id=1, source_target_pairs={{0,1},{1,0},{2,3},{3,2},{4,5},{5,4},{6,7},{7,6},{8,9},{9,8},{10,11... | collective-permute-start | bytes 393224 | tf_op jit(solution)/shard_map/ppermute | solution.py:42
  55.8 4.7 %collective-permute-start.24 = (bf16[144,256]{1,0:T(8,128)(2,1)S(1)}, bf16[144,256]{1,0:T(8,128)(2,1)S(1)}, u32[]{:S(2)}, u32[]{:S(2)}) collective-permute-start(bf16[144,256]{1,0:T(8,128)(2,1)S(1)} %shard_map.122.refs_9_.refs_0_), channel_id=1, source_target_pairs={{0,4},{4,0},{8,12},{12,8},{16,20},{20,16},{24,28},{28,24},{1,5},{5... | collective-permute-start | bytes 221192 | tf_op jit(solution)/shard_map/ppermute | solution.py:42
  57.5 5.7 %collective-permute-start.23 = (bf16[256,256]{1,0:T(8,128)(2,1)S(1)}, bf16[256,256]{1,0:T(8,128)(2,1)S(1)}, u32[]{:S(2)}, u32[]{:S(2)}) collective-permute-start(bf16[256,256]{1,0:T(8,128)(2,1)S(1)} %get-tuple-element.45), channel_id=1, source_target_pairs={{0,1},{1,0},{2,3},{3,2},{4,5},{5,4},{6,7},{7,6},{8,9},{9,8},{10,11... | collective-permute-start | bytes 393224 | tf_op jit(solution)/shard_map/ppermute | solution.py:42
  57.7 5.8 %collective-permute-start.22 = (bf16[256,256]{1,0:T(8,128)(2,1)S(1)}, bf16[256,256]{1,0:T(8,128)(2,1)S(1)}, u32[]{:S(2)}, u32[]{:S(2)}) collective-permute-start(bf16[256,256]{1,0:T(8,128)(2,1)S(1)} %shard_map.124), channel_id=1, source_target_pairs={{0,2},{1,3},{2,0},{3,1},{4,6},{5,7},{6,4},{7,5},{8,10},{9,11},{10,... | collective-permute-start | bytes 393224 | tf_op jit(solution)/shard_map/ppermute | solution.py:42
  60.6 1.3 %collective-permute-start.25 = (bf16[128,256]{1,0:T(8,128)(2,1)S(1)}, bf16[128,256]{1,0:T(8,128)(2,1)S(1)}, u32[]{:S(2)}, u32[]{:S(2)}) collective-permute-start(bf16[128,256]{1,0:T(8,128)(2,1)S(1)} %slice.4), channel_id=1, source_target_pairs={{0,1},{1,0},{2,3},{3,2},{4,5},{5,4},{6,7},{7,6},{8,9},{9,8},{10,11... | collective-permute-start | bytes 196616 | tf_op jit(solution)/shard_map/ppermute | solution.py:42
